TPU v7x, 32 devices: a whole 2x2x4 slice. The times are simulated.
32 devices in a mesh: loop: 2 (over x), rep: 4 (over z), feat: 4 (over y, core).
Axes of the slice: x: 2, y: 2, z: 4, core: 2. Of those that a mesh axis runs over, the one named last changes fastest.
Arguments:
- features: bfloat16 [128, 2048], P('feat', 'loop'), may hold values from -6 to 6
- tile_values: bfloat16 [2, 4, 112, 128, 128], P('loop', 'rep'), may hold values from -0.1875 to 0.1875
- tile_coords: int32 [2, 4, 2, 112], P('loop', 'rep'), may hold values from 0 to 7, as said below
- section_counts: int32 [2, 4, 1], P('loop', 'rep'), may hold values from 0 to 64, as said below
- weight_one: bfloat16 [128, 128], replicated, may hold values from -0.5 to 0.5
- weight_two: bfloat16 [128, 128], replicated, may hold values from -0.5 to 0.5
- cotangent: bfloat16 [128, 2048], P(None, ('loop', 'feat')), may hold values from -24 to 24
Outputs:
- grad_one: float32 [128, 128], replicated
- grad_two: float32 [128, 128], replicated
- input_grad: bfloat16 [128, 2048], P('feat', 'loop')
Inputs may be any that keep to these rules, and one draw needn't show every extreme that they name: `tile_coords`: slots of a list are grouped by section in order of sections; the live slots of one section name distinct (row, column) pairs; slots past the list's total count hold 0. `section_counts`: section k of rep index r covers the column block r + 4 * k places below the list's own loop index; sections with r + 4 * k of 2 or more hold 0.
All inputs are finite; a program needn't handle non-finite values.
Results may differ from a plain program's by a relative error of at most 0.029.
Values may be sent and summed in bfloat16 or wider, within the bound.
No kernel may reach another device: no remote copies, remote signals or barrier semaphores. Data moves between devices by JAX's collectives and lax.ppermute only.
A program may use at most 64 MiB of HBM per device.

v0:
```python
import math

import jax
import jax.numpy as jnp
from jax import lax
from jax.sharding import PartitionSpec as P

tile_batch = 8


def shortened(shard):

    def short(part):
        return part.astype(jnp.bfloat16) if part.dtype == jnp.float32 else part

    return jax.tree.map(short, shard)


def passed_along(value, axis, steps):
    count = lax.axis_size(axis)
    pairs = [(source, (source + steps) % count) for source in range(count)]
    return lax.ppermute(value, axis, pairs)


def silu_slope(argument):
    sigmoid_value = jax.nn.sigmoid(argument)
    return sigmoid_value * (1.0 + argument * (1.0 - sigmoid_value))


def section_term(source, section_id, layout, transposed, enabled=True):
    tile_set, row_ids, col_ids, starts, filled, panels = layout
    feat_width = source.shape[0]
    tile_side = tile_set.shape[-1]
    slot_total = tile_set.shape[0]
    shaped = source.reshape(feat_width, panels, tile_side)
    first = starts[section_id]
    number = jnp.where(enabled, filled[section_id], 0)
    rounds = (number + tile_batch - 1) // tile_batch
    offsets = jnp.arange(tile_batch, dtype=jnp.int32)
    panel_ids = jnp.arange(panels, dtype=jnp.int32)

    def one_round(round_id, running):
        within = round_id * tile_batch + offsets
        alive_mask = within < number
        slot_ids = jnp.minimum(first + within, slot_total - 1)
        chosen = tile_set[slot_ids]
        if transposed:
            picked = shaped[:, row_ids[slot_ids], :]
            products = jnp.einsum(
                "dba,bac->dbc", picked, chosen, preferred_element_type=jnp.float32
            )
            target = col_ids[slot_ids]
        else:
            picked = shaped[:, col_ids[slot_ids], :]
            products = jnp.einsum(
                "dbc,bac->dba", picked, chosen, preferred_element_type=jnp.float32
            )
            target = row_ids[slot_ids]
        placing = ((target[:, None] == panel_ids[None, :]) & alive_mask[:, None]).astype(
            jnp.float32
        )
        return running + jnp.einsum(
            "dbe,bp->dpe", products, placing, precision=lax.Precision.HIGHEST
        )

    zero_block = jnp.zeros((feat_width, panels, tile_side), jnp.float32)
    return lax.fori_loop(0, rounds, one_round, zero_block).reshape(feat_width, panels * tile_side)


def advance(block, stride):
    return jax.tree.map(
        lambda part, own: part.astype(own.dtype),
        passed_along(shortened(block), "loop", stride),
        block,
    )


def forward_product(source, layout):
    loop_size = lax.axis_size("loop")
    rep_size = lax.axis_size("rep")
    rep_index = lax.axis_index("rep")
    sections = -(-loop_size // rep_size)
    stride = rep_size % loop_size
    current = source
    for bit in range(rep_size.bit_length() - 1):
        jump = (1 << bit) % loop_size
        if jump:
            moved = passed_along(current, "loop", jump)
            current = jnp.where((rep_index >> bit) % 2 == 1, moved, current)
    running = section_term(current, 0, layout, False)
    if sections > 1:

        def onward(step_id, carry):
            ahead, acc = carry
            ahead = advance(ahead, stride)
            return (ahead, acc + section_term(ahead, step_id, layout, False))

        ahead, running = lax.fori_loop(1, sections, onward, (current, running))
    return running


def transposed_product(source, layout):
    loop_size = lax.axis_size("loop")
    rep_size = lax.axis_size("rep")
    rep_index = lax.axis_index("rep")
    sections = -(-loop_size // rep_size)
    stride = rep_size % loop_size
    running = section_term(source, sections - 1, layout, True)
    if sections > 1:

        def backward(step_id, acc):
            acc = jax.tree.map(
                lambda part, own: part.astype(own.dtype),
                passed_along(shortened(acc), "loop", -stride),
                acc,
            )
            return acc + section_term(source, sections - 1 - step_id, layout, True)

        running = lax.fori_loop(1, sections, backward, running)
    for bit in range(rep_size.bit_length() - 1):
        jump = (1 << bit) % loop_size
        if jump:
            moved = passed_along(running.astype(jnp.bfloat16), "loop", -jump).astype(running.dtype)
            running = jnp.where((rep_index >> bit) % 2 == 1, moved, running)
    return running


def to_nodes(partial_value):
    summed = lax.psum(partial_value.astype(jnp.bfloat16), "rep")
    return lax.all_to_all(summed, "feat", split_axis=1, concat_axis=0, tiled=True)


def to_features(node_block):
    return lax.all_to_all(node_block, "feat", split_axis=0, concat_axis=1, tiled=True)


def weight_grad(mixed, slope):
    part_sum = jnp.einsum("dq,eq->de", mixed, slope, preferred_element_type=jnp.float32)
    return lax.psum(part_sum, ("loop", "feat"))


def shards(features, tile_values, tile_coords, section_counts, weight_one, weight_two, cotangent):
    tile_set = tile_values[0, 0]
    row_ids = tile_coords[0, 0, 0]
    col_ids = tile_coords[0, 0, 1]
    filled = section_counts[0, 0]
    starts = jnp.cumsum(filled) - filled
    panels = features.shape[1] // tile_set.shape[-1]
    layout = (tile_set, row_ids, col_ids, starts, filled, panels)
    scale = 1.0 / math.sqrt(features.shape[1] * lax.axis_size("loop"))
    mix_one = to_nodes(forward_product(features, layout))
    z_one = jnp.einsum("de,dq->eq", weight_one, mix_one, preferred_element_type=jnp.float32)
    h_one = jax.nn.silu(z_one).astype(jnp.bfloat16)
    mix_two = to_nodes(forward_product(to_features(h_one), layout))
    z_two = jnp.einsum("de,dq->eq", weight_two, mix_two, preferred_element_type=jnp.float32)
    dz_two = (cotangent * silu_slope(z_two)).astype(jnp.bfloat16)
    grad_two = weight_grad(mix_two, dz_two) * scale
    dm_two = jnp.einsum("de,eq->dq", weight_two, dz_two, preferred_element_type=jnp.float32).astype(
        jnp.bfloat16
    )
    dh_one = to_nodes(transposed_product(to_features(dm_two), layout))
    dz_one = (dh_one * silu_slope(z_one)).astype(jnp.bfloat16)
    grad_one = weight_grad(mix_one, dz_one) * scale
    dm_one = jnp.einsum("de,eq->dq", weight_one, dz_one, preferred_element_type=jnp.float32).astype(
        jnp.bfloat16
    )
    partial_value = transposed_product(to_features(dm_one), layout)
    input_grad = lax.psum(partial_value.astype(jnp.bfloat16), "rep")
    return (grad_one, grad_two, input_grad)


def solution(mesh):
    return jax.shard_map(
        shards,
        mesh=mesh,
        in_specs=(
            P("feat", "loop"),
            P("loop", "rep", None, None, None),
            P("loop", "rep", None, None),
            P("loop", "rep", None),
            P(),
            P(),
            P(None, ("loop", "feat")),
        ),
        out_specs=(P(), P(), P("feat", "loop")),
        check_vma=False,
    )
```

profile of v0, /device:TPU:24, one launch (start us, length us, event | category | flops | bytes accessed | tf_op | source)
XLA Modules:
  0.0 441.9 jit_solution(5446487745784056705)
XLA Ops:
  7.2 0.0 all-reduce.7.cloned.1.call-start
  7.2 1.6 collective-permute-start
  8.8 0.8 slice_bitcast_fusion
  10.2 1.5 collective-permute-done
  11.9 0.7 all_to_all.76
  12.5 0.0 all-reduce.7.cloned.1.call-update
  12.6 0.0 all-reduce.9.cloned.1.call-start
  12.6 77.7 %all-reduce.7.cloned.1.call-done = bf16[32,4,256]{2,1,0:T(4,128)(2,1)} async-done(((bf16[32,4,256]{2,1,0:T(4,128)(2,1)}), bf16[32,4,256]{2,1,0:T(4,128)(2,1)}) %all-reduce.7.cloned.1.call-update) | async-done | bytes 65552 | tf_op jit(solution)/shard_map/psum | solution.py:129
  90.3 0.8 copy.40
  91.2 6.7 %all_to_all.102 = bf16[32,4,256]{2,0,1:T(8,128)(2,1)S(1)} all-to-all(bf16[32,4,256]{2,0,1:T(8,128)(2,1)S(1)} %copy.40), channel_id=1, replica_groups=mesh['loop'=2,'rep'=4,'feat'=4] {'feat'}, dimensions={1} | all-to-all | bytes 131072 | tf_op jit(solution)/shard_map/all_to_all | solution.py:130
  97.8 0.2 multiply_convert_fusion.1
  98.1 6.5 %all_to_all.103 = bf16[4,32,256]{2,1,0:T(8,128)(2,1)S(1)} all-to-all(bf16[4,32,256]{2,1,0:T(8,128)(2,1)S(1)} %bitcast.251), channel_id=1, replica_groups=mesh['loop'=2,'rep'=4,'feat'=4] {'feat'}, dimensions={0} | all-to-all | bytes 131072 | tf_op jit(solution)/shard_map/all_to_all | solution.py:134
  104.6 1.5 collective-permute-start.1
  106.0 2.8 collective-permute-done.1
  108.9 0.7 all_to_all.84
  109.6 0.0 all-reduce.9.cloned.1.call-update
  109.7 77.5 %all-reduce.9.cloned.1.call-done = bf16[32,4,256]{2,1,0:T(4,128)(2,1)} async-done(((bf16[32,4,256]{2,1,0:T(4,128)(2,1)}), bf16[32,4,256]{2,1,0:T(4,128)(2,1)}) %all-reduce.9.cloned.1.call-update) | async-done | bytes 65552 | tf_op jit(solution)/shard_map/psum | solution.py:129
  187.1 0.8 copy.43
  188.0 6.7 %all_to_all.104 = bf16[32,4,256]{2,0,1:T(8,128)(2,1)S(1)} all-to-all(bf16[32,4,256]{2,0,1:T(8,128)(2,1)S(1)} %copy.43), channel_id=1, replica_groups=mesh['loop'=2,'rep'=4,'feat'=4] {'feat'}, dimensions={1} | all-to-all | bytes 131072 | tf_op jit(solution)/shard_map/all_to_all | solution.py:130
  194.6 0.2 multiply_convert_fusion
  194.9 0.8 convolution_convert_fusion.1
  195.7 3.3 all-to-all-start.3
  198.9 0.0 all-reduce.11.cloned.1.call-start
  199.0 4.0 all-to-all-done.3
  203.0 0.1 copy.45
  203.2 1.5 collective-permute-start.2
  204.8 2.8 collective-permute-done.2
  207.6 0.6 copy.74
  208.2 0.0 all-reduce.11.cloned.1.call-update
  208.2 76.9 %all-reduce.11.cloned.1.call-done = bf16[32,4,256]{2,0,1:T(8,128)(2,1)} async-done(((bf16[32,4,256]{2,0,1:T(8,128)(2,1)}), bf16[32,4,256]{2,0,1:T(8,128)(2,1)}) %all-reduce.11.cloned.1.call-update) | async-done | bytes 65552 | tf_op jit(solution)/shard_map/psum | solution.py:129
  285.1 7.4 %all_to_all.105 = bf16[32,4,256]{2,0,1:T(8,128)(2,1)S(1)} all-to-all(bf16[32,4,256]{2,0,1:T(8,128)(2,1)} %all-reduce.11.cloned.1.call-done), channel_id=1, replica_groups=mesh['loop'=2,'rep'=4,'feat'=4] {'feat'}, dimensions={1} | all-to-all | bytes 131072 | tf_op jit(solution)/shard_map/all_to_all | solution.py:130
  292.5 0.1 fusion.58
  292.6 0.8 convolution_convert_fusion
  293.4 3.3 all-to-all-start.5
  296.7 0.0 all-reduce.15.cloned.1.call-start
  296.7 0.8 fusion.60
  297.5 3.2 all-to-all-done.5
  300.7 0.1 copy.48
  300.9 1.5 collective-permute-start.3
  302.5 0.8 fusion.59
  303.3 0.0 all-reduce.15.cloned.1.call-update
  303.3 0.0 all-reduce.13.cloned.1.call-start
  303.3 1.9 collective-permute-done.3
  305.3 0.7 fusion.56
  305.9 93.6 %all-reduce.15.cloned.1.call-done = (f32[128,128]{1,0:T(8,128)}, f32[128,128]{1,0:T(8,128)}) async-done(((f32[128,128]{1,0:T(8,128)}, f32[128,128]{1,0:T(8,128)}), (f32[128,128]{1,0:T(8,128)}, f32[128,128]{1,0:T(8,128)})) %all-reduce.15.cloned.1.call-update) | async-done | bytes 131088 | tf_op jit(solution)/shard_map/psum | solution.py:139
  399.5 1.5 broadcast_multiply_fusion
  401.1 32.8 %all-reduce.13.cloned.1.call-done = bf16[32,1024]{1,0:T(8,128)(2,1)} async-done(((bf16[32,1024]{1,0:T(8,128)(2,1)}), bf16[32,1024]{1,0:T(8,128)(2,1)}) %all-reduce.13.cloned.1.call-update) | async-done | bytes 65552 | tf_op jit(solution)/shard_map/psum | solution.py:168
  433.9 1.5 copy.116
  (27 shorter events, 0.4 us)
Async XLA Ops:
  7.2 90.7 %copy-start = (bf16[128,128]{1,0:T(8,128)(2,1)S(1)}, bf16[128,128]{1,0:T(8,128)(2,1)}, u32[]{:S(2)}) copy-start(bf16[128,128]{1,0:T(8,128)(2,1)} %param.19) | copy-start | bytes 98308
  7.2 83.1 %all-reduce.7.cloned.1.call-start = ((), (), s32[]{:S(2)}) async-start(), calls=%async_computation.6 | async-start | bytes 131072 | tf_op jit(solution)/shard_map/psum | solution.py:129
  7.2 4.5 %collective-permute-start = (bf16[32,1024]{1,0:T(8,128)(2,1)}, bf16[32,1024]{1,0:T(8,128)(2,1)S(1)}, u32[]{:S(2)}, u32[]{:S(2)}) collective-permute-start(bf16[32,1024]{1,0:T(8,128)(2,1)} %param.15), channel_id=1, source_target_pairs={{0,16},{16,0},{1,17},{17,1},{2,18},{18,2},{3,19},{19,3},{4,20},{20... | collective-permute-start | bytes 196616 | tf_op jit(solution)/shard_map/ppermute | solution.py:22
  12.6 174.6 %all-reduce.9.cloned.1.call-start = ((), (), s32[]{:S(2)}) async-start(), calls=%async_computation.7 | async-start | bytes 131072 | tf_op jit(solution)/shard_map/psum | solution.py:129
  104.6 4.3 collective-permute-start.1
  108.9 85.7 %copy-start.1 = (bf16[128,128]{1,0:T(8,128)(2,1)S(1)}, bf16[128,128]{1,0:T(8,128)(2,1)}, u32[]{:S(2)}) copy-start(bf16[128,128]{1,0:T(8,128)(2,1)} %param.20) | copy-start | bytes 98308
  108.9 85.7 %copy-start.2 = (bf16[128,256]{1,0:T(8,128)(2,1)S(1)}, bf16[128,256]{1,0:T(8,128)(2,1)}, u32[]{:S(2)}) copy-start(bf16[128,256]{1,0:T(8,128)(2,1)} %param.21) | copy-start | bytes 196612
  195.7 7.4 %all-to-all-start.3 = ((bf16[4,32,256]{2,1,0:T(8,128)(2,1)}), bf16[4,32,256]{2,1,0:T(8,128)(2,1)S(1)}, u32[]{:S(2)}, u32[]{:S(2)}) async-start(bf16[4,32,256]{2,1,0:T(8,128)(2,1)} %bitcast.14), calls=%async_computation.3 | async-start | bytes 131072 | tf_op jit(solution)/shard_map/all_to_all | solution.py:134
  198.9 86.2 %all-reduce.11.cloned.1.call-start = ((), (), s32[]{:S(2)}) async-start(), calls=%async_computation.8 | async-start | bytes 131072 | tf_op jit(solution)/shard_map/psum | solution.py:129
  203.2 4.3 collective-permute-start.2
  293.4 7.4 %all-to-all-start.5 = ((bf16[4,32,256]{2,1,0:T(8,128)(2,1)}), bf16[4,32,256]{2,1,0:T(8,128)(2,1)S(1)}, u32[]{:S(2)}, u32[]{:S(2)}) async-start(bf16[4,32,256]{2,1,0:T(8,128)(2,1)} %bitcast.20), calls=%async_computation.5 | async-start | bytes 131072 | tf_op jit(solution)/shard_map/all_to_all | solution.py:134
  296.7 102.9 %all-reduce.15.cloned.1.call-start = ((), (), s32[]{:S(2)}) async-start(), calls=%async_computation.10 | async-start | bytes 262144 | tf_op jit(solution)/shard_map/psum | solution.py:139
  300.9 4.3 collective-permute-start.3
  303.3 130.6 %all-reduce.13.cloned.1.call-start = ((), (), s32[]{:S(2)}) async-start(), calls=%async_computation.9 | async-start | bytes 131072 | tf_op jit(solution)/shard_map/psum | solution.py:168
Sparse Core Ops, SparseCore 0:
  12.7 77.6 all-reduce.6
  109.8 77.2 all-reduce.8
  208.4 76.7 all-reduce.10
  303.4 96.0 all-reduce.14
  401.7 32.1 all-reduce.12
where the time goes:
time: 447 us; the launch traced here: 442 us
  waiting for transfers between devices  375 us (84%)
  blocking collectives  27.2 us (6%)
  between operations  14.7 us (3%)
  starting transfers between devices  12.9 us (3%)
  local copies, waits for them, and re-layouts  6.24 us (1%)
    psum x3, waiting for transfers between devices, to_nodes(): summed = lax.psum(partial_value.astype(jnp.bfloat16), 'rep')  232 us
    psum x1, waiting for transfers between devices, weight_grad(): return lax.psum(part_sum, ('loop', 'feat'))  93.6 us
    psum x1, waiting for transfers between devices, shards(): input_grad = lax.psum(partial_value.astype(jnp.bfloat16), 'rep')  32.8 us
    all_to_all x3, blocking collectives, to_nodes(): lax.all_to_all(summed, 'feat', split_axis=1, concat_axis=0, tiled=True)  20.7 us
    ppermute x4, waiting for transfers between devices, passed_along(): return lax.ppermute(value, axis, pairs)  9.07 us
  transfers between devices with their start and end apart: 11, of which 11 were waited for; matrix products, arithmetic and copies ran while one was open for 1% of the time, Pallas kernels for 0%

commit v1 on v0

--- a/solution.py
+++ b/solution.py
@@ -1,8 +1,11 @@
+import functools
 import math
 
 import jax
 import jax.numpy as jnp
 from jax import lax
+from jax.experimental import pallas as pl
+from jax.experimental.pallas import tpu as pltpu
 from jax.sharding import PartitionSpec as P
 
 tile_batch = 8
@@ -139,7 +142,7 @@
     return lax.psum(part_sum, ("loop", "feat"))
 
 
-def shards(features, tile_values, tile_coords, section_counts, weight_one, weight_two, cotangent):
+def ring_shards(features, tile_values, tile_coords, section_counts, weight_one, weight_two, cotangent):
     tile_set = tile_values[0, 0]
     row_ids = tile_coords[0, 0, 0]
     col_ids = tile_coords[0, 0, 1]
@@ -169,9 +172,362 @@
     return (grad_one, grad_two, input_grad)
 
 
+mesh_axes = ("loop", "rep", "feat")
+vmem_bytes = 24 * 1024 * 1024
+
+
+def routed(value, target):
+    loops, reps, feats = (lax.axis_size(axis) for axis in mesh_axes)
+    pairs = []
+    for i in range(loops):
+        for r in range(reps):
+            for f in range(feats):
+                to_loop, to_rep, to_feat = target(i, r, f)
+                pairs.append(
+                    ((i * reps + r) * feats + f, (to_loop * reps + to_rep) * feats + to_feat)
+                )
+    return lax.ppermute(value, mesh_axes, pairs)
+
+
+def to_other_core(i, r, f):
+    return i, r, f ^ 1
+
+
+def to_other_pair(i, r, f):
+    return i, r, f ^ 2
+
+
+def to_other_loop(i, r, f):
+    return 1 - i, r, f
+
+
+def to_other_rep(i, r, f):
+    return i, r ^ 1, f
+
+
+def to_far_rep(i, r, f):
+    return i, r ^ 2, f
+
+
+def to_row_owner(i, r, f):
+    return (i, r - 1, f) if r % 2 else (1 - i, r + 1, f)
+
+
+def to_column_owner(i, r, f):
+    return (1 - i, r - 1, f) if r % 2 else (i, r + 1, f)
+
+
+def to_feature_pair(i, r, f):
+    return (1 - i if r % 2 else i), r, f ^ 2
+
+
+def local_call(kernel, outs, operands, spaces=None, scratch=(), flops=0):
+    spaces = spaces or [pltpu.VMEM] * len(operands)
+    moved = sum(o.size * o.dtype.itemsize for o in operands) + sum(
+        math.prod(o.shape) * 4 for o in outs
+    )
+    return pl.pallas_call(
+        kernel,
+        out_shape=list(outs),
+        in_specs=[pl.BlockSpec(memory_space=space) for space in spaces],
+        out_specs=[pl.BlockSpec(memory_space=pltpu.VMEM) for _ in outs],
+        scratch_shapes=list(scratch),
+        compiler_params=pltpu.CompilerParams(vmem_limit_bytes=vmem_bytes),
+        cost_estimate=pl.CostEstimate(flops=flops, bytes_accessed=moved, transcendentals=0),
+    )(*operands)
+
+
+def bf16_array(*shape):
+    return jax.ShapeDtypeStruct(shape, jnp.bfloat16)
+
+
+def f32_array(*shape):
+    return jax.ShapeDtypeStruct(shape, jnp.float32)
+
+
+def dot_nn(a, b):
+    return lax.dot_general(a, b, (((1,), (0,)), ((), ())), preferred_element_type=jnp.float32)
+
+
+def dot_nt(a, b):
+    return lax.dot_general(a, b, (((1,), (1,)), ((), ())), preferred_element_type=jnp.float32)
+
+
+def dot_tn(a, b):
+    return lax.dot_general(a, b, (((0,), (0,)), ((), ())), preferred_element_type=jnp.float32)
+
+
+def place_kernel(panels, side, ids_ref, count_ref, coords_ref, tiles_ref, block_ref, sems):
+    block_ref[...] = jnp.zeros_like(block_ref)
+    quarter = panels // 4
+    core = ids_ref[2] % 2
+    count = count_ref[0]
+
+    def position(panel):
+        part = panel // quarter
+        half = jnp.bitwise_xor(part % 2, core)
+        return (half * 2 + part // 2) * quarter + panel % quarter
+
+    def tile_copy(slot):
+        row = pl.multiple_of(position(coords_ref[0, slot]) * side, side)
+        col = pl.multiple_of(position(coords_ref[1, slot]) * side, side)
+        return pltpu.make_async_copy(
+            tiles_ref.at[slot],
+            block_ref.at[pl.ds(row, side), pl.ds(col, side)],
+            sems.at[slot],
+        )
+
+    def begin(slot, carry):
+        tile_copy(slot).start()
+        return carry
+
+    def finish(slot, carry):
+        tile_copy(slot).wait()
+        return carry
+
+    lax.fori_loop(0, count, begin, 0)
+    lax.fori_loop(0, count, finish, 0)
+
+
+def first_kernel(ids_ref, own_ref, across_ref, pair_ref, swapped_ref, block_ref, out_ref, full):
+    width, nodes = own_ref.shape
+    odd = ids_ref[1] % 2 == 1
+    feat = ids_ref[2]
+    core = feat % 2
+    quarter = nodes // 4
+    half = nodes // 2
+
+    def keep(value, owner):
+        row = pl.multiple_of(owner * width, width)
+        for part in range(4):
+            lane = pl.multiple_of(
+                jnp.bitwise_xor(part % 2, core) * half + (part // 2) * quarter, quarter
+            )
+            full[pl.ds(row, width), pl.ds(lane, quarter)] = value[
+                :, part * quarter : (part + 1) * quarter
+            ]
+
+    keep(jnp.where(odd, across_ref[...], own_ref[...]), feat)
+    keep(pair_ref[...], jnp.bitwise_xor(feat, 2))
+    keep(swapped_ref[:width, :], jnp.bitwise_xor(feat, 1))
+    keep(swapped_ref[width:, :], jnp.bitwise_xor(feat, 3))
+    out_ref[...] = dot_nt(full[...], block_ref[:half, :]).astype(out_ref.dtype)
+
+
+def forward_kernel(own_ref, other_ref, block_ref, out_ref):
+    half = own_ref.shape[1]
+    total = dot_nt(own_ref[...], block_ref[:half, :half])
+    total += dot_nt(other_ref[...], block_ref[:half, half:])
+    out_ref[...] = total.astype(out_ref.dtype)
+
+
+def backward_kernel(own_ref, other_ref, block_ref, out_ref):
+    half = own_ref.shape[1]
+    width = out_ref.shape[1]
+    total = dot_nn(own_ref[...], block_ref[:half, :width])
+    total += dot_nn(other_ref[...], block_ref[half:, :width])
+    out_ref[...] = total.astype(out_ref.dtype)
+
+
+def summed(ids_ref, own_ref, near_ref, across_ref):
+    odd = ids_ref[1] % 2 == 1
+    second = jnp.where(odd, across_ref[...], own_ref[...])
+    return (near_ref[...].astype(jnp.float32) + second.astype(jnp.float32)).astype(jnp.bfloat16)
+
+
+def slope(value):
+    part = jax.nn.sigmoid(value)
+    return part * (1.0 + value * (1.0 - part))
+
+
+def layer_one_kernel(ids_ref, own_ref, near_ref, across_ref, weight_ref, mix_ref, h_ref):
+    mix = summed(ids_ref, own_ref, near_ref, across_ref)
+    mix_ref[...] = mix
+    z = dot_tn(weight_ref[...], mix)
+    h_ref[...] = (z * jax.nn.sigmoid(z)).astype(h_ref.dtype)
+
+
+def layer_two_kernel(
+    ids_ref, own_ref, near_ref, weight_ref, cot_ref, cot_pair_ref, mix_ref, dz_ref, dm_ref
+):
+    mix = (own_ref[...].astype(jnp.float32) + near_ref[...].astype(jnp.float32)).astype(
+        jnp.bfloat16
+    )
+    mix_ref[...] = mix
+    z = dot_tn(weight_ref[...], mix)
+    upper = ids_ref[2] // 2 == 1
+    mine, pair = cot_ref[...], cot_pair_ref[...]
+    quarter = mine.shape[1]
+    rate = slope(z)
+    low = (jnp.where(upper, pair, mine).astype(jnp.float32) * rate[:, :quarter]).astype(
+        jnp.bfloat16
+    )
+    high = (jnp.where(upper, mine, pair).astype(jnp.float32) * rate[:, quarter:]).astype(
+        jnp.bfloat16
+    )
+    dz_ref[:, :quarter] = low
+    dz_ref[:, quarter:] = high
+    dm_ref[...] = dot_nn(weight_ref[...], dz_ref[...]).astype(dm_ref.dtype)
+
+
+def slope_kernel(ids_ref, mix_ref, across_ref, weight_ref, own_mix_ref, slope_ref):
+    odd = ids_ref[1] % 2 == 1
+    mix = jnp.where(odd, across_ref[...], mix_ref[...])
+    own_mix_ref[...] = mix
+    slope_ref[...] = slope(dot_tn(weight_ref[...], mix))
+
+
+def back_one_kernel(
+    ids_ref, own_ref, near_ref, across_ref, slope_ref, weight_ref, dz_ref, dm_ref, send_ref
+):
+    dh = summed(ids_ref, own_ref, near_ref, across_ref)
+    dz = (dh.astype(jnp.float32) * slope_ref[...]).astype(jnp.bfloat16)
+    dz_ref[...] = dz
+    width = dm_ref.shape[0]
+    feat = ids_ref[2]
+    mine = pl.multiple_of(feat * width, width)
+    theirs = pl.multiple_of(jnp.bitwise_xor(feat, 1) * width, width)
+    dm_ref[...] = dot_nn(weight_ref[pl.ds(mine, width), :], dz).astype(dm_ref.dtype)
+    send_ref[...] = dot_nn(weight_ref[pl.ds(theirs, width), :], dz).astype(send_ref.dtype)
+
+
+def grad_kernel(mix_ref, slope_ref, out_ref):
+    out_ref[...] = dot_nt(mix_ref[...], slope_ref[...])
+
+
+def sum_kernel(ids_ref, own_ref, near_ref, across_ref, out_ref):
+    out_ref[...] = summed(ids_ref, own_ref, near_ref, across_ref)
+
+
+def last_kernel(ids_ref, own_ref, far_ref, out_ref):
+    core = ids_ref[2] % 2
+    nodes = own_ref.shape[1]
+    quarter = nodes // 4
+    half = nodes // 2
+    for part in range(4):
+        lane = pl.multiple_of(
+            jnp.bitwise_xor(part % 2, core) * half + (part // 2) * quarter, quarter
+        )
+        here = pl.ds(lane, quarter)
+        out_ref[:, part * quarter : (part + 1) * quarter] = own_ref[:, here] + far_ref[:, here]
+
+
+def grad_total(part, scale):
+    part = part + routed(part, to_other_core)
+    part = part + routed(part, to_other_loop)
+    return (part + routed(part, to_far_rep)) * scale
+
+
+def paired_shards(
+    features, tile_values, tile_coords, section_counts, weight_one, weight_two, cotangent
+):
+    hidden = weight_one.shape[0]
+    width, nodes = features.shape
+    side = tile_values.shape[-1]
+    panels = nodes // side
+    half = nodes // 2
+    scale = 1.0 / math.sqrt(nodes * lax.axis_size("loop"))
+    ids = jnp.stack([lax.axis_index(axis) for axis in mesh_axes]).astype(jnp.int32)
+    smem, vmem = pltpu.SMEM, pltpu.VMEM
+
+    across = routed(features, to_other_loop)
+    pair = routed(features, to_feature_pair)
+    cot_pair = routed(cotangent, to_other_pair)
+    (block,) = local_call(
+        functools.partial(place_kernel, panels, side),
+        [bf16_array(nodes, nodes)],
+        [ids, section_counts[0, 0], tile_coords[0, 0], tile_values[0, 0]],
+        [smem, smem, smem, pl.ANY],
+        [pltpu.SemaphoreType.DMA((panels * panels,))],
+        flops=4_000_000_000,
+    )
+    odd = lax.axis_index("rep") % 2 == 1
+    swapped = routed(
+        jnp.concatenate([jnp.where(odd, across, features), pair], axis=0), to_other_core
+    )
+    product_flops = 2 * hidden * nodes * half
+
+    (part_one,) = local_call(
+        first_kernel,
+        [bf16_array(hidden, half)],
+        [ids, features, across, pair, swapped, block],
+        [smem] + [vmem] * 5,
+        [pltpu.VMEM((hidden, nodes), jnp.bfloat16)],
+        flops=product_flops,
+    )
+    mix_one, h_one = local_call(
+        layer_one_kernel,
+        [bf16_array(hidden, half)] * 2,
+        [ids, part_one, routed(part_one, to_row_owner), routed(part_one, to_other_loop), weight_one],
+        [smem] + [vmem] * 4,
+    )
+    (part_two,) = local_call(
+        forward_kernel,
+        [bf16_array(hidden, half)],
+        [h_one, routed(h_one, to_other_core), block],
+        flops=product_flops,
+    )
+    mix_two, dz_two, dm_two = local_call(
+        layer_two_kernel,
+        [bf16_array(hidden, half)] * 3,
+        [ids, part_two, routed(part_two, to_other_rep), weight_two, cotangent, cot_pair],
+        [smem] + [vmem] * 5,
+    )
+    mix_here, slope_here = local_call(
+        slope_kernel,
+        [bf16_array(hidden, half), f32_array(hidden, half)],
+        [ids, mix_one, routed(mix_one, to_other_loop), weight_one],
+        [smem] + [vmem] * 3,
+    )
+    (part_three,) = local_call(
+        backward_kernel,
+        [bf16_array(hidden, half)],
+        [dm_two, routed(dm_two, to_other_core), block],
+        flops=product_flops,
+    )
+    (grad_two,) = local_call(grad_kernel, [f32_array(hidden, hidden)], [mix_two, dz_two])
+    grad_two = grad_total(grad_two, scale)
+    dz_one, dm_one, dm_send = local_call(
+        back_one_kernel,
+        [bf16_array(hidden, half), bf16_array(width, half), bf16_array(width, half)],
+        [
+            ids,
+            part_three,
+            routed(part_three, to_column_owner),
+            routed(part_three, to_other_loop),
+            slope_here,
+            weight_one,
+        ],
+        [smem] + [vmem] * 5,
+    )
+    (part_four,) = local_call(
+        backward_kernel,
+        [bf16_array(width, nodes)],
+        [dm_one, routed(dm_send, to_other_core), block],
+        flops=product_flops,
+    )
+    (grad_one,) = local_call(grad_kernel, [f32_array(hidden, hidden)], [mix_here, dz_one])
+    grad_one = grad_total(grad_one, scale)
+    (near_sum,) = local_call(
+        sum_kernel,
+        [bf16_array(width, nodes)],
+        [ids, part_four, routed(part_four, to_column_owner), routed(part_four, to_other_loop)],
+        [smem] + [vmem] * 3,
+    )
+    (input_grad,) = local_call(
+        last_kernel,
+        [bf16_array(width, nodes)],
+        [ids, near_sum, routed(near_sum, to_far_rep)],
+        [smem] + [vmem] * 2,
+    )
+    return (grad_one, grad_two, input_grad)
+
+
 def solution(mesh):
+    sizes = dict(mesh.shape)
+    paired = sizes["loop"] == 2 and sizes["rep"] == 4 and sizes["feat"] == 4
     return jax.shard_map(
-        shards,
+        paired_shards if paired else ring_shards,
         mesh=mesh,
         in_specs=(
             P("feat", "loop"),

time: 447 us -> 65.3 us (0.15)
  the two profiles are of different devices: /device:TPU:24 before, /device:TPU:0 now
where the time goes in v1:
time: 65.3 us; the launch traced here: 65.1 us
  waiting for transfers between devices  26.6 us (41%)
  starting transfers between devices  20.2 us (31%)
  Pallas kernels  11.9 us (18%)
  local copies, waits for them, and re-layouts  2.73 us (4%)
  other arithmetic  2.26 us (3%)
  between operations  1.5 us (2%)
    ppermute x22, waiting for transfers between devices, routed(): return lax.ppermute(value, mesh_axes, pairs)  26.6 us
    ppermute x22, starting transfers between devices, routed(): return lax.ppermute(value, mesh_axes, pairs)  20.2 us
    pallas_call x13, Pallas kernels, local_call(): pl.pallas_call(kernel, out_shape=list(outs), in_specs=[pl.BlockSpec(memor...  11.9 us
    unnamed x12, local copies, waits for them, and re-layouts  2.73 us
  transfers between devices with their start and end apart: 22, of which 12 were waited for; matrix products, arithmetic and copies ran while one was open for 2% of the time, Pallas kernels for 13%

profile of v1, /device:TPU:0, one launch (start us, length us, event | category | flops | bytes accessed | tf_op | source)
XLA Modules:
  0.0 65.1 jit_solution(14522293845719142168)
XLA Ops:
  0.6 3.0 %collective-permute-start.1 = (bf16[32,1024]{1,0:T(8,128)(2,1)}, bf16[32,1024]{1,0:T(8,128)(2,1)S(1)}, u32[]{:S(2)}, u32[]{:S(2)}) collective-permute-start(bf16[32,1024]{1,0:T(8,128)(2,1)} %own_ref.1), channel_id=1, source_target_pairs={{0,2},{1,3},{2,0},{3,1},{4,22},{5,23},{6,20},{7,21},{8,10},{9,11},... | collective-permute-start | bytes 196616 | tf_op jit(solution)/shard_map/ppermute | solution.py:189
  3.7 1.5 %collective-permute-start = (bf16[32,1024]{1,0:T(8,128)(2,1)}, bf16[32,1024]{1,0:T(8,128)(2,1)S(1)}, u32[]{:S(2)}, u32[]{:S(2)}) collective-permute-start(bf16[32,1024]{1,0:T(8,128)(2,1)} %own_ref.1), channel_id=1, source_target_pairs={{0,16},{1,17},{2,18},{3,19},{4,20},{5,21},{6,22},{7,23},{8,24},{9,... | collective-permute-start | bytes 196616 | tf_op jit(solution)/shard_map/ppermute | solution.py:189
  5.8 0.1 pad_add_fusion.ids_ref
  5.9 2.3 %collective-permute-done.across_ref = bf16[32,1024]{1,0:T(8,128)(2,1)S(1)} collective-permute-done((bf16[32,1024]{1,0:T(8,128)(2,1)}, bf16[32,1024]{1,0:T(8,128)(2,1)S(1)}, u32[]{:S(2)}, u32[]{:S(2)}) %collective-permute-start) | collective-permute-done | bytes 65568 | tf_op jit(solution)/shard_map/ppermute | solution.py:189
  8.1 0.8 %broadcast_select_fusion = bf16[32,1024]{1,0:T(8,128)(2,1)S(1)} fusion(bf16[32,1024]{1,0:T(8,128)(2,1)S(1)} %collective-permute-done.across_ref, bf16[32,1024]{1,0:T(8,128)(2,1)} %own_ref.1, pred[]{:T(512)S(6)} %eq.5), kind=kLoop, calls=%fused_computation.3 | loop fusion | flops 32768 | bytes 196609 | tf_op jit(solution)/shard_map/jit(_where)/select_n | solution.py:446
  9.0 0.1 collective-permute-start.2
  9.1 2.0 %copy-done.4 = bf16[1,1,112,128,128]{4,3,2,1,0:T(8,128)(2,1)S(1)} copy-done((bf16[1,1,112,128,128]{4,3,2,1,0:T(8,128)(2,1)S(1)}, bf16[1,1,112,128,128]{4,3,2,1,0:T(8,128)(2,1)}, u32[]{:S(2)}) %copy-start.4) | copy-done | bytes 3670040
  11.1 0.7 %copy-done.5 = s32[1,1,2,112]{3,2,1,0:T(2,128)S(1)} copy-done((s32[1,1,2,112]{3,2,1,0:T(2,128)S(1)}, s32[1,1,2,112]{3,2,1,0:T(2,128)}, u32[]{:S(2)}) %copy-start.5) | copy-done | bytes 920
  11.8 4.2 %shard_map.94.block_ref = bf16[1024,1024]{1,0:T(8,128)(2,1)S(1)} custom-call(s32[3]{0:T(128)S(1)} %pad_add_fusion.ids_ref, s32[1]{0:T(128)} %bitcast.6.count_ref, s32[2,112]{1,0:T(2,128)S(1)} %bitcast.8, bf16[112,128,128]{2,1,0:T(8,128)(2,1)S(1)} %bitcast.7), custom_call_target="tpu_custom_call" | custom-call | flops 4000000000 | bytes 7865232 | tf_op jit(solution)/shard_map/pallas_call | solution.py:229
  16.1 1.0 %shard_map.95.own_ref = bf16[128,512]{1,0:T(8,128)(2,1)S(1)} custom-call(s32[3]{0:T(128)S(1)} %pad_add_fusion.ids_ref, bf16[32,1024]{1,0:T(8,128)(2,1)S(1)} %copy-done.1, bf16[32,1024]{1,0:T(8,128)(2,1)S(1)} %collective-permute-done.across_ref, bf16[32,1024]{1,0:T(8,128)(2,1)S(1)} %collective-permute-done.1.pair_ref, ...), custom_call_target="tpu_custom_call" | custom-call | flops 134217728 | bytes 2686988 | tf_op jit(solution)/shard_map/pallas_call | solution.py:229
  17.1 1.6 %collective-permute-start.4 = (bf16[128,512]{1,0:T(8,128)(2,1)S(1)}, bf16[128,512]{1,0:T(8,128)(2,1)S(1)}, u32[]{:S(2)}, u32[]{:S(2)}) collective-permute-start(bf16[128,512]{1,0:T(8,128)(2,1)S(1)} %shard_map.95.own_ref), channel_id=1, source_target_pairs={{0,16},{1,17},{2,18},{3,19},{4,20},{5,21},{6,22},{7,23},{8,24},{9,... | collective-permute-start | bytes 393224 | tf_op jit(solution)/shard_map/ppermute | solution.py:189
  18.7 4.4 %collective-permute-done.4.across_ref = bf16[128,512]{1,0:T(8,128)(2,1)S(1)} collective-permute-done((bf16[128,512]{1,0:T(8,128)(2,1)S(1)}, bf16[128,512]{1,0:T(8,128)(2,1)S(1)}, u32[]{:S(2)}, u32[]{:S(2)}) %collective-permute-start.4) | collective-permute-done | bytes 131104 | tf_op jit(solution)/shard_map/ppermute | solution.py:189
  23.1 1.2 %collective-permute-done.3.near_ref = bf16[128,512]{1,0:T(8,128)(2,1)S(1)} collective-permute-done((bf16[128,512]{1,0:T(8,128)(2,1)S(1)}, bf16[128,512]{1,0:T(8,128)(2,1)S(1)}, u32[]{:S(2)}, u32[]{:S(2)}) %collective-permute-start.3) | collective-permute-done | bytes 131104 | tf_op jit(solution)/shard_map/ppermute | solution.py:189
  24.3 0.8 %shard_map.96 = (bf16[128,512]{1,0:T(8,128)(2,1)S(1)}, bf16[128,512]{1,0:T(8,128)(2,1)S(1)}) custom-call(s32[3]{0:T(128)S(1)} %pad_add_fusion.ids_ref, bf16[128,512]{1,0:T(8,128)(2,1)S(1)} %shard_map.95.own_ref, bf16[128,512]{1,0:T(8,128)(2,1)S(1)} %collective-permute-done.3.near_ref, bf16[128,512]{1,0:T(8,128)(2,1)S(1)} %collective-permute-done.4.across_ref, ...), custom_call_target="tpu_custom_call" | custom-call | bytes 950284 | tf_op jit(solution)/shard_map/pallas_call | solution.py:229
  25.1 1.3 %collective-permute-done.6.other_ref = bf16[128,512]{1,0:T(8,128)(2,1)S(1)} collective-permute-done((bf16[128,512]{1,0:T(8,128)(2,1)S(1)}, bf16[128,512]{1,0:T(8,128)(2,1)S(1)}, u32[]{:S(2)}, u32[]{:S(2)}) %collective-permute-start.6) | collective-permute-done | bytes 131104 | tf_op jit(solution)/shard_map/ppermute | solution.py:189
  26.5 0.5 shard_map.98.own_ref
  27.0 1.5 %collective-permute-start.7 = (bf16[128,512]{1,0:T(8,128)(2,1)S(1)}, bf16[128,512]{1,0:T(8,128)(2,1)S(1)}, u32[]{:S(2)}, u32[]{:S(2)}) collective-permute-start(bf16[128,512]{1,0:T(8,128)(2,1)S(1)} %shard_map.98.own_ref), channel_id=1, source_target_pairs={{0,4},{1,5},{2,6},{3,7},{4,0},{5,1},{6,2},{7,3},{8,12},{9,13},{10,... | collective-permute-start | bytes 393224 | tf_op jit(solution)/shard_map/ppermute | solution.py:189
  28.5 0.6 collective-permute-start.8
  29.0 3.7 %collective-permute-done.8.cot_pair_ref = bf16[128,256]{1,0:T(8,128)(2,1)S(1)} collective-permute-done((bf16[128,256]{1,0:T(8,128)(2,1)S(1)}, bf16[128,256]{1,0:T(8,128)(2,1)S(1)}, u32[]{:S(2)}, u32[]{:S(2)}) %collective-permute-start.8) | collective-permute-done | bytes 65568 | tf_op jit(solution)/shard_map/ppermute | solution.py:189
  32.7 1.0 %shard_map.99 = (bf16[128,512]{1,0:T(8,128)(2,1)S(1)}, bf16[128,512]{1,0:T(8,128)(2,1)S(1)}, bf16[128,512]{1,0:T(8,128)(2,1)S(1)}) custom-call(s32[3]{0:T(128)S(1)} %pad_add_fusion.ids_ref, bf16[128,512]{1,0:T(8,128)(2,1)S(1)} %shard_map.98.own_ref, bf16[128,512]{1,0:T(8,128)(2,1)S(1)} %collective-permute-done.7.near_ref, bf16[128,128]{1,0:T(8,128)(2,1)S(1)} %copy-done.3, ...), custom_call_target="tpu_custom_call" | custom-call | bytes 1212428 | tf_op jit(solution)/shard_map/pallas_call | solution.py:229
  33.7 0.1 collective-permute-start.9
  33.8 1.2 %collective-permute-start.5 = (bf16[128,512]{1,0:T(8,128)(2,1)S(1)}, bf16[128,512]{1,0:T(8,128)(2,1)S(1)}, u32[]{:S(2)}, u32[]{:S(2)}) collective-permute-start(bf16[128,512]{1,0:T(8,128)(2,1)S(1)} %get-tuple-element.13.mix_ref), channel_id=1, source_target_pairs={{0,16},{1,17},{2,18},{3,19},{4,20},{5,21},{6,22},{7,23},{8,24},{9,... | collective-permute-start | bytes 393224 | tf_op jit(solution)/shard_map/ppermute | solution.py:189
  35.0 0.1 collective-permute-done.9.other_ref
  35.1 0.3 shard_map.100.own_ref
  35.4 1.2 %collective-permute-start.11 = (bf16[128,512]{1,0:T(8,128)(2,1)S(1)}, bf16[128,512]{1,0:T(8,128)(2,1)S(1)}, u32[]{:S(2)}, u32[]{:S(2)}) collective-permute-start(bf16[128,512]{1,0:T(8,128)(2,1)S(1)} %shard_map.100.own_ref), channel_id=1, source_target_pairs={{0,16},{1,17},{2,18},{3,19},{4,20},{5,21},{6,22},{7,23},{8,24},{9,... | collective-permute-start | bytes 393224 | tf_op jit(solution)/shard_map/ppermute | solution.py:189
  36.7 1.3 %collective-permute-start.10 = (bf16[128,512]{1,0:T(8,128)(2,1)S(1)}, bf16[128,512]{1,0:T(8,128)(2,1)S(1)}, u32[]{:S(2)}, u32[]{:S(2)}) collective-permute-start(bf16[128,512]{1,0:T(8,128)(2,1)S(1)} %shard_map.100.own_ref), channel_id=1, source_target_pairs={{0,4},{1,5},{2,6},{3,7},{4,16},{5,17},{6,18},{7,19},{8,12},{9,13},... | collective-permute-start | bytes 393224 | tf_op jit(solution)/shard_map/ppermute | solution.py:189
  37.9 0.2 shard_map.103
  38.2 4.7 %collective-permute-done.5.across_ref = bf16[128,512]{1,0:T(8,128)(2,1)S(1)} collective-permute-done((bf16[128,512]{1,0:T(8,128)(2,1)S(1)}, bf16[128,512]{1,0:T(8,128)(2,1)S(1)}, u32[]{:S(2)}, u32[]{:S(2)}) %collective-permute-start.5) | collective-permute-done | bytes 131104 | tf_op jit(solution)/shard_map/ppermute | solution.py:189
  42.9 0.8 %shard_map.97 = (bf16[128,512]{1,0:T(8,128)(2,1)S(1)}, f32[128,512]{1,0:T(8,128)S(1)}) custom-call(s32[3]{0:T(128)S(1)} %pad_add_fusion.ids_ref, bf16[128,512]{1,0:T(8,128)(2,1)S(1)} %get-tuple-element.13.mix_ref, bf16[128,512]{1,0:T(8,128)(2,1)S(1)} %collective-permute-done.5.across_ref, bf16[128,128]{1,0:T(8,128)(2,1)S(1)} %copy-done), custom_call_target="tpu_custom_call" | custom-call | bytes 819212 | tf_op jit(solution)/shard_map/pallas_call | solution.py:229
  43.7 1.6 %collective-permute-done.11.across_ref = bf16[128,512]{1,0:T(8,128)(2,1)S(1)} collective-permute-done((bf16[128,512]{1,0:T(8,128)(2,1)S(1)}, bf16[128,512]{1,0:T(8,128)(2,1)S(1)}, u32[]{:S(2)}, u32[]{:S(2)}) %collective-permute-start.11) | collective-permute-done | bytes 131104 | tf_op jit(solution)/shard_map/ppermute | solution.py:189
  45.3 0.7 %shard_map.101 = (bf16[128,512]{1,0:T(8,128)(2,1)S(1)}, bf16[32,512]{1,0:T(8,128)(2,1)S(1)}, bf16[32,512]{1,0:T(8,128)(2,1)S(1)}) custom-call(s32[3]{0:T(128)S(1)} %pad_add_fusion.ids_ref, bf16[128,512]{1,0:T(8,128)(2,1)S(1)} %shard_map.100.own_ref, bf16[128,512]{1,0:T(8,128)(2,1)S(1)} %collective-permute-done.10.near_ref, ...), custom_call_target="tpu_custom_call" | custom-call | bytes 1081356 | tf_op jit(solution)/shard_map/pallas_call | solution.py:229
  46.1 0.2 shard_map.102
  46.4 1.2 %collective-permute-start.16 = (f32[128,128]{1,0:T(8,128)S(1)}, f32[128,128]{1,0:T(8,128)S(1)}, u32[]{:S(2)}, u32[]{:S(2)}) collective-permute-start(f32[128,128]{1,0:T(8,128)S(1)} %add.26), channel_id=1, source_target_pairs={{0,16},{1,17},{2,18},{3,19},{4,20},{5,21},{6,22},{7,23},{8,24},{9,... | collective-permute-start | bytes 196616 | tf_op jit(solution)/shard_map/ppermute | solution.py:189
  47.6 0.2 collective-permute-start.18
  47.8 1.0 %collective-permute-done.18.other_ref = bf16[32,512]{1,0:T(8,128)(2,1)S(1)} collective-permute-done((bf16[32,512]{1,0:T(8,128)(2,1)S(1)}, bf16[32,512]{1,0:T(8,128)(2,1)S(1)}, u32[]{:S(2)}, u32[]{:S(2)}) %collective-permute-start.18) | collective-permute-done | bytes 32800 | tf_op jit(solution)/shard_map/ppermute | solution.py:189
  48.8 0.5 shard_map.104.own_ref
  49.2 0.9 %collective-permute-start.20 = (bf16[32,1024]{1,0:T(8,128)(2,1)S(1)}, bf16[32,1024]{1,0:T(8,128)(2,1)S(1)}, u32[]{:S(2)}, u32[]{:S(2)}) collective-permute-start(bf16[32,1024]{1,0:T(8,128)(2,1)S(1)} %shard_map.104.own_ref), channel_id=1, source_target_pairs={{0,16},{1,17},{2,18},{3,19},{4,20},{5,21},{6,22},{7,23},{8,24},{9,... | collective-permute-start | bytes 196616 | tf_op jit(solution)/shard_map/ppermute | solution.py:189
  50.2 1.2 %collective-permute-start.13 = (f32[128,128]{1,0:T(8,128)S(1)}, f32[128,128]{1,0:T(8,128)S(1)}, u32[]{:S(2)}, u32[]{:S(2)}) collective-permute-start(f32[128,128]{1,0:T(8,128)S(1)} %add.23), channel_id=1, source_target_pairs={{0,16},{1,17},{2,18},{3,19},{4,20},{5,21},{6,22},{7,23},{8,24},{9,... | collective-permute-start | bytes 196616 | tf_op jit(solution)/shard_map/ppermute | solution.py:189
  51.4 1.4 %collective-permute-start.17 = (f32[128,128]{1,0:T(8,128)S(1)}, f32[128,128]{1,0:T(8,128)S(1)}, u32[]{:S(2)}, u32[]{:S(2)}) collective-permute-start(f32[128,128]{1,0:T(8,128)S(1)} %add.27), channel_id=1, source_target_pairs={{0,8},{1,9},{2,10},{3,11},{4,12},{5,13},{6,14},{7,15},{8,0},{9,1},... | collective-permute-start | bytes 196616 | tf_op jit(solution)/shard_map/ppermute | solution.py:189
  52.8 2.5 %collective-permute-done.20.across_ref = bf16[32,1024]{1,0:T(8,128)(2,1)S(1)} collective-permute-done((bf16[32,1024]{1,0:T(8,128)(2,1)S(1)}, bf16[32,1024]{1,0:T(8,128)(2,1)S(1)}, u32[]{:S(2)}, u32[]{:S(2)}) %collective-permute-start.20) | collective-permute-done | bytes 65568 | tf_op jit(solution)/shard_map/ppermute | solution.py:189
  55.3 0.8 %collective-permute-done.19.near_ref = bf16[32,1024]{1,0:T(8,128)(2,1)S(1)} collective-permute-done((bf16[32,1024]{1,0:T(8,128)(2,1)S(1)}, bf16[32,1024]{1,0:T(8,128)(2,1)S(1)}, u32[]{:S(2)}, u32[]{:S(2)}) %collective-permute-start.19) | collective-permute-done | bytes 65568 | tf_op jit(solution)/shard_map/ppermute | solution.py:189
  56.1 0.6 shard_map.105.own_ref
  56.7 0.8 %collective-permute-start.21 = (bf16[32,1024]{1,0:T(8,128)(2,1)S(1)}, bf16[32,1024]{1,0:T(8,128)(2,1)S(1)}, u32[]{:S(2)}, u32[]{:S(2)}) collective-permute-start(bf16[32,1024]{1,0:T(8,128)(2,1)S(1)} %shard_map.105.own_ref), channel_id=1, source_target_pairs={{0,8},{1,9},{2,10},{3,11},{4,12},{5,13},{6,14},{7,15},{8,0},{9,1},... | collective-permute-start | bytes 196616 | tf_op jit(solution)/shard_map/ppermute | solution.py:189
  57.5 2.3 %collective-permute-start.14 = (f32[128,128]{1,0:T(8,128)S(1)}, f32[128,128]{1,0:T(8,128)S(1)}, u32[]{:S(2)}, u32[]{:S(2)}) collective-permute-start(f32[128,128]{1,0:T(8,128)S(1)} %add.24), channel_id=1, source_target_pairs={{0,8},{1,9},{2,10},{3,11},{4,12},{5,13},{6,14},{7,15},{8,0},{9,1},... | collective-permute-start | bytes 196616 | tf_op jit(solution)/shard_map/ppermute | solution.py:189
  59.8 0.6 add_multiply_fusion
  60.4 2.9 %collective-permute-done.21.far_ref = bf16[32,1024]{1,0:T(8,128)(2,1)S(1)} collective-permute-done((bf16[32,1024]{1,0:T(8,128)(2,1)S(1)}, bf16[32,1024]{1,0:T(8,128)(2,1)S(1)}, u32[]{:S(2)}, u32[]{:S(2)}) %collective-permute-start.21) | collective-permute-done | bytes 65568 | tf_op jit(solution)/shard_map/ppermute | solution.py:189
  63.3 1.2 %shard_map.106 = bf16[32,1024]{1,0:T(8,128)(2,1)} custom-call(s32[3]{0:T(128)S(1)} %pad_add_fusion.ids_ref, bf16[32,1024]{1,0:T(8,128)(2,1)S(1)} %shard_map.105.own_ref, bf16[32,1024]{1,0:T(8,128)(2,1)S(1)} %collective-permute-done.21.far_ref), custom_call_target="tpu_custom_call" | custom-call | bytes 262156 | tf_op jit(solution)/shard_map/pallas_call | solution.py:229
  64.5 0.6 add_multiply_fusion.1
  (30 shorter events, 0.3 us)
Async XLA Ops:
  0.6 8.4 %collective-permute-start.1 = (bf16[32,1024]{1,0:T(8,128)(2,1)}, bf16[32,1024]{1,0:T(8,128)(2,1)S(1)}, u32[]{:S(2)}, u32[]{:S(2)}) collective-permute-start(bf16[32,1024]{1,0:T(8,128)(2,1)} %own_ref.1), channel_id=1, source_target_pairs={{0,2},{1,3},{2,0},{3,1},{4,22},{5,23},{6,20},{7,21},{8,10},{9,11},... | collective-permute-start | bytes 196616 | tf_op jit(solution)/shard_map/ppermute | solution.py:189
  3.7 4.5 %collective-permute-start = (bf16[32,1024]{1,0:T(8,128)(2,1)}, bf16[32,1024]{1,0:T(8,128)(2,1)S(1)}, u32[]{:S(2)}, u32[]{:S(2)}) collective-permute-start(bf16[32,1024]{1,0:T(8,128)(2,1)} %own_ref.1), channel_id=1, source_target_pairs={{0,16},{1,17},{2,18},{3,19},{4,20},{5,21},{6,22},{7,23},{8,24},{9,... | collective-permute-start | bytes 196616 | tf_op jit(solution)/shard_map/ppermute | solution.py:189
  9.0 7.1 %collective-permute-start.2 = (bf16[64,1024]{1,0:T(8,128)(2,1)S(1)}, bf16[64,1024]{1,0:T(8,128)(2,1)S(1)}, u32[]{:S(2)}, u32[]{:S(2)}) collective-permute-start(bf16[64,1024]{1,0:T(8,128)(2,1)S(1)} %pad_maximum_fusion), channel_id=1, source_target_pairs={{0,1},{1,0},{2,3},{3,2},{4,5},{5,4},{6,7},{7,6},{8,9},{9,8},{10,11... | collective-permute-start | bytes 393224 | tf_op jit(solution)/shard_map/ppermute | solution.py:189
  9.1 2.0 %copy-start.4 = (bf16[1,1,112,128,128]{4,3,2,1,0:T(8,128)(2,1)S(1)}, bf16[1,1,112,128,128]{4,3,2,1,0:T(8,128)(2,1)}, u32[]{:S(2)}) copy-start(bf16[1,1,112,128,128]{4,3,2,1,0:T(8,128)(2,1)} %param.8) | copy-start | bytes 11010052
  11.1 0.7 %copy-start.5 = (s32[1,1,2,112]{3,2,1,0:T(2,128)S(1)}, s32[1,1,2,112]{3,2,1,0:T(2,128)}, u32[]{:S(2)}) copy-start(s32[1,1,2,112]{3,2,1,0:T(2,128)} %param.9) | copy-start | bytes 2692
  11.8 4.3 %copy-start.1 = (bf16[32,1024]{1,0:T(8,128)(2,1)S(1)}, bf16[32,1024]{1,0:T(8,128)(2,1)}, u32[]{:S(2)}) copy-start(bf16[32,1024]{1,0:T(8,128)(2,1)} %own_ref.1) | copy-start | bytes 196612
  11.8 12.5 %copy-start = (bf16[128,128]{1,0:T(8,128)(2,1)S(1)}, bf16[128,128]{1,0:T(8,128)(2,1)}, u32[]{:S(2)}) copy-start(bf16[128,128]{1,0:T(8,128)(2,1)} %weight_ref.7) | copy-start | bytes 98308
  16.0 12.4 %copy-start.2 = (bf16[128,256]{1,0:T(8,128)(2,1)S(1)}, bf16[128,256]{1,0:T(8,128)(2,1)}, u32[]{:S(2)}) copy-start(bf16[128,256]{1,0:T(8,128)(2,1)} %cot_ref.1) | copy-start | bytes 196612
  16.1 16.7 %copy-start.3 = (bf16[128,128]{1,0:T(8,128)(2,1)S(1)}, bf16[128,128]{1,0:T(8,128)(2,1)}, u32[]{:S(2)}) copy-start(bf16[128,128]{1,0:T(8,128)(2,1)} %weight_ref.6) | copy-start | bytes 98308
  17.1 6.0 %collective-permute-start.4 = (bf16[128,512]{1,0:T(8,128)(2,1)S(1)}, bf16[128,512]{1,0:T(8,128)(2,1)S(1)}, u32[]{:S(2)}, u32[]{:S(2)}) collective-permute-start(bf16[128,512]{1,0:T(8,128)(2,1)S(1)} %shard_map.95.own_ref), channel_id=1, source_target_pairs={{0,16},{1,17},{2,18},{3,19},{4,20},{5,21},{6,22},{7,23},{8,24},{9,... | collective-permute-start | bytes 393224 | tf_op jit(solution)/shard_map/ppermute | solution.py:189
  18.7 5.6 %collective-permute-start.3 = (bf16[128,512]{1,0:T(8,128)(2,1)S(1)}, bf16[128,512]{1,0:T(8,128)(2,1)S(1)}, u32[]{:S(2)}, u32[]{:S(2)}) collective-permute-start(bf16[128,512]{1,0:T(8,128)(2,1)S(1)} %shard_map.95.own_ref), channel_id=1, source_target_pairs={{0,20},{1,21},{2,22},{3,23},{4,0},{5,1},{6,2},{7,3},{8,28},{9,29},... | collective-permute-start | bytes 393224 | tf_op jit(solution)/shard_map/ppermute | solution.py:189
  25.1 1.4 %collective-permute-start.6 = (bf16[128,512]{1,0:T(8,128)(2,1)S(1)}, bf16[128,512]{1,0:T(8,128)(2,1)S(1)}, u32[]{:S(2)}, u32[]{:S(2)}) collective-permute-start(bf16[128,512]{1,0:T(8,128)(2,1)S(1)} %get-tuple-element.15.own_ref), channel_id=1, source_target_pairs={{0,1},{1,0},{2,3},{3,2},{4,5},{5,4},{6,7},{7,6},{8,9},{9,8},{10,11... | collective-permute-start | bytes 393224 | tf_op jit(solution)/shard_map/ppermute | solution.py:189
  27.0 5.8 %collective-permute-start.7 = (bf16[128,512]{1,0:T(8,128)(2,1)S(1)}, bf16[128,512]{1,0:T(8,128)(2,1)S(1)}, u32[]{:S(2)}, u32[]{:S(2)}) collective-permute-start(bf16[128,512]{1,0:T(8,128)(2,1)S(1)} %shard_map.98.own_ref), channel_id=1, source_target_pairs={{0,4},{1,5},{2,6},{3,7},{4,0},{5,1},{6,2},{7,3},{8,12},{9,13},{10,... | collective-permute-start | bytes 393224 | tf_op jit(solution)/shard_map/ppermute | solution.py:189
  28.5 4.3 %collective-permute-start.8 = (bf16[128,256]{1,0:T(8,128)(2,1)S(1)}, bf16[128,256]{1,0:T(8,128)(2,1)S(1)}, u32[]{:S(2)}, u32[]{:S(2)}) collective-permute-start(bf16[128,256]{1,0:T(8,128)(2,1)S(1)} %copy-done.2), channel_id=1, source_target_pairs={{0,2},{1,3},{2,0},{3,1},{4,6},{5,7},{6,4},{7,5},{8,10},{9,11},{10,... | collective-permute-start | bytes 196616 | tf_op jit(solution)/shard_map/ppermute | solution.py:189
  33.7 1.4 %collective-permute-start.9 = (bf16[128,512]{1,0:T(8,128)(2,1)S(1)}, bf16[128,512]{1,0:T(8,128)(2,1)S(1)}, u32[]{:S(2)}, u32[]{:S(2)}) collective-permute-start(bf16[128,512]{1,0:T(8,128)(2,1)S(1)} %get-tuple-element.16.own_ref), channel_id=1, source_target_pairs={{0,1},{1,0},{2,3},{3,2},{4,5},{5,4},{6,7},{7,6},{8,9},{9,8},{10,11... | collective-permute-start | bytes 393224 | tf_op jit(solution)/shard_map/ppermute | solution.py:189
  33.8 9.2 %collective-permute-start.5 = (bf16[128,512]{1,0:T(8,128)(2,1)S(1)}, bf16[128,512]{1,0:T(8,128)(2,1)S(1)}, u32[]{:S(2)}, u32[]{:S(2)}) collective-permute-start(bf16[128,512]{1,0:T(8,128)(2,1)S(1)} %get-tuple-element.13.mix_ref), channel_id=1, source_target_pairs={{0,16},{1,17},{2,18},{3,19},{4,20},{5,21},{6,22},{7,23},{8,24},{9,... | collective-permute-start | bytes 393224 | tf_op jit(solution)/shard_map/ppermute | solution.py:189
  35.4 9.9 %collective-permute-start.11 = (bf16[128,512]{1,0:T(8,128)(2,1)S(1)}, bf16[128,512]{1,0:T(8,128)(2,1)S(1)}, u32[]{:S(2)}, u32[]{:S(2)}) collective-permute-start(bf16[128,512]{1,0:T(8,128)(2,1)S(1)} %shard_map.100.own_ref), channel_id=1, source_target_pairs={{0,16},{1,17},{2,18},{3,19},{4,20},{5,21},{6,22},{7,23},{8,24},{9,... | collective-permute-start | bytes 393224 | tf_op jit(solution)/shard_map/ppermute | solution.py:189
  36.7 8.7 %collective-permute-start.10 = (bf16[128,512]{1,0:T(8,128)(2,1)S(1)}, bf16[128,512]{1,0:T(8,128)(2,1)S(1)}, u32[]{:S(2)}, u32[]{:S(2)}) collective-permute-start(bf16[128,512]{1,0:T(8,128)(2,1)S(1)} %shard_map.100.own_ref), channel_id=1, source_target_pairs={{0,4},{1,5},{2,6},{3,7},{4,16},{5,17},{6,18},{7,19},{8,12},{9,13},... | collective-permute-start | bytes 393224 | tf_op jit(solution)/shard_map/ppermute | solution.py:189
  38.1 8.2 %collective-permute-start.15 = (f32[128,128]{1,0:T(8,128)S(1)}, f32[128,128]{1,0:T(8,128)S(1)}, u32[]{:S(2)}, u32[]{:S(2)}) collective-permute-start(f32[128,128]{1,0:T(8,128)S(1)} %shard_map.103), channel_id=1, source_target_pairs={{0,1},{1,0},{2,3},{3,2},{4,5},{5,4},{6,7},{7,6},{8,9},{9,8},{10,11... | collective-permute-start | bytes 196616 | tf_op jit(solution)/shard_map/ppermute | solution.py:189
  46.3 3.9 %collective-permute-start.12 = (f32[128,128]{1,0:T(8,128)S(1)}, f32[128,128]{1,0:T(8,128)S(1)}, u32[]{:S(2)}, u32[]{:S(2)}) collective-permute-start(f32[128,128]{1,0:T(8,128)S(1)} %shard_map.102), channel_id=1, source_target_pairs={{0,1},{1,0},{2,3},{3,2},{4,5},{5,4},{6,7},{7,6},{8,9},{9,8},{10,11... | collective-permute-start | bytes 196616 | tf_op jit(solution)/shard_map/ppermute | solution.py:189
  46.4 5.0 %collective-permute-start.16 = (f32[128,128]{1,0:T(8,128)S(1)}, f32[128,128]{1,0:T(8,128)S(1)}, u32[]{:S(2)}, u32[]{:S(2)}) collective-permute-start(f32[128,128]{1,0:T(8,128)S(1)} %add.26), channel_id=1, source_target_pairs={{0,16},{1,17},{2,18},{3,19},{4,20},{5,21},{6,22},{7,23},{8,24},{9,... | collective-permute-start | bytes 196616 | tf_op jit(solution)/shard_map/ppermute | solution.py:189
  47.6 1.2 %collective-permute-start.18 = (bf16[32,512]{1,0:T(8,128)(2,1)S(1)}, bf16[32,512]{1,0:T(8,128)(2,1)S(1)}, u32[]{:S(2)}, u32[]{:S(2)}) collective-permute-start(bf16[32,512]{1,0:T(8,128)(2,1)S(1)} %get-tuple-element.22), channel_id=1, source_target_pairs={{0,1},{1,0},{2,3},{3,2},{4,5},{5,4},{6,7},{7,6},{8,9},{9,8},{10,11... | collective-permute-start | bytes 98312 | tf_op jit(solution)/shard_map/ppermute | solution.py:189
  49.2 6.0 %collective-permute-start.20 = (bf16[32,1024]{1,0:T(8,128)(2,1)S(1)}, bf16[32,1024]{1,0:T(8,128)(2,1)S(1)}, u32[]{:S(2)}, u32[]{:S(2)}) collective-permute-start(bf16[32,1024]{1,0:T(8,128)(2,1)S(1)} %shard_map.104.own_ref), channel_id=1, source_target_pairs={{0,16},{1,17},{2,18},{3,19},{4,20},{5,21},{6,22},{7,23},{8,24},{9,... | collective-permute-start | bytes 196616 | tf_op jit(solution)/shard_map/ppermute | solution.py:189
  50.1 6.0 %collective-permute-start.19 = (bf16[32,1024]{1,0:T(8,128)(2,1)S(1)}, bf16[32,1024]{1,0:T(8,128)(2,1)S(1)}, u32[]{:S(2)}, u32[]{:S(2)}) collective-permute-start(bf16[32,1024]{1,0:T(8,128)(2,1)S(1)} %shard_map.104.own_ref), channel_id=1, source_target_pairs={{0,4},{1,5},{2,6},{3,7},{4,16},{5,17},{6,18},{7,19},{8,12},{9,13},... | collective-permute-start | bytes 196616 | tf_op jit(solution)/shard_map/ppermute | solution.py:189
  50.2 7.3 %collective-permute-start.13 = (f32[128,128]{1,0:T(8,128)S(1)}, f32[128,128]{1,0:T(8,128)S(1)}, u32[]{:S(2)}, u32[]{:S(2)}) collective-permute-start(f32[128,128]{1,0:T(8,128)S(1)} %add.23), channel_id=1, source_target_pairs={{0,16},{1,17},{2,18},{3,19},{4,20},{5,21},{6,22},{7,23},{8,24},{9,... | collective-permute-start | bytes 196616 | tf_op jit(solution)/shard_map/ppermute | solution.py:189
  51.4 8.4 %collective-permute-start.17 = (f32[128,128]{1,0:T(8,128)S(1)}, f32[128,128]{1,0:T(8,128)S(1)}, u32[]{:S(2)}, u32[]{:S(2)}) collective-permute-start(f32[128,128]{1,0:T(8,128)S(1)} %add.27), channel_id=1, source_target_pairs={{0,8},{1,9},{2,10},{3,11},{4,12},{5,13},{6,14},{7,15},{8,0},{9,1},... | collective-permute-start | bytes 196616 | tf_op jit(solution)/shard_map/ppermute | solution.py:189
  56.7 6.6 %collective-permute-start.21 = (bf16[32,1024]{1,0:T(8,128)(2,1)S(1)}, bf16[32,1024]{1,0:T(8,128)(2,1)S(1)}, u32[]{:S(2)}, u32[]{:S(2)}) collective-permute-start(bf16[32,1024]{1,0:T(8,128)(2,1)S(1)} %shard_map.105.own_ref), channel_id=1, source_target_pairs={{0,8},{1,9},{2,10},{3,11},{4,12},{5,13},{6,14},{7,15},{8,0},{9,1},... | collective-permute-start | bytes 196616 | tf_op jit(solution)/shard_map/ppermute | solution.py:189
  57.5 7.0 %collective-permute-start.14 = (f32[128,128]{1,0:T(8,128)S(1)}, f32[128,128]{1,0:T(8,128)S(1)}, u32[]{:S(2)}, u32[]{:S(2)}) collective-permute-start(f32[128,128]{1,0:T(8,128)S(1)} %add.24), channel_id=1, source_target_pairs={{0,8},{1,9},{2,10},{3,11},{4,12},{5,13},{6,14},{7,15},{8,0},{9,1},... | collective-permute-start | bytes 196616 | tf_op jit(solution)/shard_map/ppermute | solution.py:189

commit v2 on v1

--- a/solution.py
+++ b/solution.py
@@ -205,16 +205,20 @@
     return i, r ^ 1, f
 
 
-def to_far_rep(i, r, f):
-    return i, r ^ 2, f
-
-
 def to_row_owner(i, r, f):
     return (i, r - 1, f) if r % 2 else (1 - i, r + 1, f)
 
 
 def to_column_owner(i, r, f):
     return (1 - i, r - 1, f) if r % 2 else (i, r + 1, f)
+
+
+def to_far_column_owner(i, r, f):
+    return (1 - i if r % 2 else i), r ^ 2, f
+
+
+def to_last_column_owner(i, r, f):
+    return (1 - i if r % 2 else i), r ^ 3, f
 
 
 def to_feature_pair(i, r, f):
@@ -253,46 +257,79 @@
     return lax.dot_general(a, b, (((1,), (1,)), ((), ())), preferred_element_type=jnp.float32)
 
 
-def dot_tn(a, b):
-    return lax.dot_general(a, b, (((0,), (0,)), ((), ())), preferred_element_type=jnp.float32)
-
-
-def place_kernel(panels, side, ids_ref, count_ref, coords_ref, tiles_ref, block_ref, sems):
+def place_kernel(
+    panels,
+    side,
+    count_ref,
+    coords_ref,
+    tiles_ref,
+    block_ref,
+    coords,
+    list_sem,
+    sems,
+):
+    lists = pltpu.make_async_copy(coords_ref, coords, list_sem)
+    lists.start()
     block_ref[...] = jnp.zeros_like(block_ref)
     quarter = panels // 4
-    core = ids_ref[2] % 2
+    core = lax.axis_index("feat") % 2
+    lists.wait()
     count = count_ref[0]
 
-    def position(panel):
+    def start_of(panel):
         part = panel // quarter
         half = jnp.bitwise_xor(part % 2, core)
-        return (half * 2 + part // 2) * quarter + panel % quarter
+        return pl.multiple_of(((half * 2 + part // 2) * quarter + panel % quarter) * side, side)
 
     def tile_copy(slot):
-        row = pl.multiple_of(position(coords_ref[0, slot]) * side, side)
-        col = pl.multiple_of(position(coords_ref[1, slot]) * side, side)
         return pltpu.make_async_copy(
-            tiles_ref.at[slot],
-            block_ref.at[pl.ds(row, side), pl.ds(col, side)],
+            tiles_ref.at[0, 0, slot],
+            block_ref.at[
+                pl.ds(start_of(coords[0, 0, 0, slot]), side),
+                pl.ds(start_of(coords[0, 0, 1, slot]), side),
+            ],
             sems.at[slot],
         )
 
-    def begin(slot, carry):
-        tile_copy(slot).start()
-        return carry
-
-    def finish(slot, carry):
-        tile_copy(slot).wait()
-        return carry
-
-    lax.fori_loop(0, count, begin, 0)
-    lax.fori_loop(0, count, finish, 0)
-
-
-def first_kernel(ids_ref, own_ref, across_ref, pair_ref, swapped_ref, block_ref, out_ref, full):
+    def in_groups(act):
+        group = 8
+
+        def some(index, carry):
+            for offset in range(group):
+                act(index * group + offset)
+            return carry
+
+        def one(slot, carry):
+            act(slot)
+            return carry
+
+        whole = count // group
+        lax.fori_loop(0, whole, some, 0)
+        lax.fori_loop(whole * group, count, one, 0)
+
+    in_groups(lambda slot: tile_copy(slot).start())
+    in_groups(lambda slot: tile_copy(slot).wait())
+
+
+def turn_kernel(one_ref, two_ref, one_turned_ref, two_turned_ref):
+    one_turned_ref[...] = one_ref[...].T
+    two_turned_ref[...] = two_ref[...].T
+
+
+def first_kernel(
+    own_ref,
+    across_ref,
+    pair_ref,
+    own_swap_ref,
+    across_swap_ref,
+    pair_swap_ref,
+    block_ref,
+    out_ref,
+    full,
+):
     width, nodes = own_ref.shape
-    odd = ids_ref[1] % 2 == 1
-    feat = ids_ref[2]
+    odd = lax.axis_index("rep") % 2 == 1
+    feat = lax.axis_index("feat")
     core = feat % 2
     quarter = nodes // 4
     half = nodes // 2
@@ -308,9 +345,9 @@
             ]
 
     keep(jnp.where(odd, across_ref[...], own_ref[...]), feat)
+    keep(jnp.where(odd, across_swap_ref[...], own_swap_ref[...]), jnp.bitwise_xor(feat, 1))
     keep(pair_ref[...], jnp.bitwise_xor(feat, 2))
-    keep(swapped_ref[:width, :], jnp.bitwise_xor(feat, 1))
-    keep(swapped_ref[width:, :], jnp.bitwise_xor(feat, 3))
+    keep(pair_swap_ref[...], jnp.bitwise_xor(feat, 3))
     out_ref[...] = dot_nt(full[...], block_ref[:half, :]).astype(out_ref.dtype)
 
 
@@ -323,14 +360,13 @@
 
 def backward_kernel(own_ref, other_ref, block_ref, out_ref):
     half = own_ref.shape[1]
-    width = out_ref.shape[1]
-    total = dot_nn(own_ref[...], block_ref[:half, :width])
-    total += dot_nn(other_ref[...], block_ref[half:, :width])
+    total = dot_nn(own_ref[...], block_ref[:half, :half])
+    total += dot_nn(other_ref[...], block_ref[half:, :half])
     out_ref[...] = total.astype(out_ref.dtype)
 
 
-def summed(ids_ref, own_ref, near_ref, across_ref):
-    odd = ids_ref[1] % 2 == 1
+def summed(own_ref, near_ref, across_ref):
+    odd = lax.axis_index("rep") % 2 == 1
     second = jnp.where(odd, across_ref[...], own_ref[...])
     return (near_ref[...].astype(jnp.float32) + second.astype(jnp.float32)).astype(jnp.bfloat16)
 
@@ -340,82 +376,127 @@
     return part * (1.0 + value * (1.0 - part))
 
 
-def layer_one_kernel(ids_ref, own_ref, near_ref, across_ref, weight_ref, mix_ref, h_ref):
-    mix = summed(ids_ref, own_ref, near_ref, across_ref)
+def layer_one_kernel(own_ref, near_ref, across_ref, turned_ref, mix_ref, h_ref):
+    mix = summed(own_ref, near_ref, across_ref)
     mix_ref[...] = mix
-    z = dot_tn(weight_ref[...], mix)
+    z = dot_nn(turned_ref[...], mix)
     h_ref[...] = (z * jax.nn.sigmoid(z)).astype(h_ref.dtype)
 
 
 def layer_two_kernel(
-    ids_ref, own_ref, near_ref, weight_ref, cot_ref, cot_pair_ref, mix_ref, dz_ref, dm_ref
+    own_ref,
+    near_ref,
+    turned_ref,
+    weight_ref,
+    cot_ref,
+    cot_pair_ref,
+    mix_ref,
+    dz_ref,
+    dm_ref,
 ):
-    mix = (own_ref[...].astype(jnp.float32) + near_ref[...].astype(jnp.float32)).astype(
-        jnp.bfloat16
-    )
+    total = own_ref[...].astype(jnp.float32) + near_ref[...].astype(jnp.float32)
+    mix = total.astype(jnp.bfloat16)
     mix_ref[...] = mix
-    z = dot_tn(weight_ref[...], mix)
-    upper = ids_ref[2] // 2 == 1
+    rate = slope(dot_nn(turned_ref[...], mix))
+    upper = lax.axis_index("feat") // 2 == 1
     mine, pair = cot_ref[...], cot_pair_ref[...]
     quarter = mine.shape[1]
-    rate = slope(z)
-    low = (jnp.where(upper, pair, mine).astype(jnp.float32) * rate[:, :quarter]).astype(
-        jnp.bfloat16
-    )
-    high = (jnp.where(upper, mine, pair).astype(jnp.float32) * rate[:, quarter:]).astype(
-        jnp.bfloat16
-    )
-    dz_ref[:, :quarter] = low
-    dz_ref[:, quarter:] = high
+    low, high = jnp.where(upper, pair, mine), jnp.where(upper, mine, pair)
+    dz_ref[:, :quarter] = (low.astype(jnp.float32) * rate[:, :quarter]).astype(jnp.bfloat16)
+    dz_ref[:, quarter:] = (high.astype(jnp.float32) * rate[:, quarter:]).astype(jnp.bfloat16)
     dm_ref[...] = dot_nn(weight_ref[...], dz_ref[...]).astype(dm_ref.dtype)
 
 
-def slope_kernel(ids_ref, mix_ref, across_ref, weight_ref, own_mix_ref, slope_ref):
-    odd = ids_ref[1] % 2 == 1
+def slope_kernel(mix_ref, across_ref, turned_ref, here_ref, slope_ref):
+    odd = lax.axis_index("rep") % 2 == 1
     mix = jnp.where(odd, across_ref[...], mix_ref[...])
-    own_mix_ref[...] = mix
-    slope_ref[...] = slope(dot_tn(weight_ref[...], mix))
-
-
-def back_one_kernel(
-    ids_ref, own_ref, near_ref, across_ref, slope_ref, weight_ref, dz_ref, dm_ref, send_ref
-):
-    dh = summed(ids_ref, own_ref, near_ref, across_ref)
-    dz = (dh.astype(jnp.float32) * slope_ref[...]).astype(jnp.bfloat16)
-    dz_ref[...] = dz
-    width = dm_ref.shape[0]
-    feat = ids_ref[2]
-    mine = pl.multiple_of(feat * width, width)
-    theirs = pl.multiple_of(jnp.bitwise_xor(feat, 1) * width, width)
-    dm_ref[...] = dot_nn(weight_ref[pl.ds(mine, width), :], dz).astype(dm_ref.dtype)
-    send_ref[...] = dot_nn(weight_ref[pl.ds(theirs, width), :], dz).astype(send_ref.dtype)
+    here_ref[...] = mix
+    slope_ref[...] = slope(dot_nn(turned_ref[...], mix))
 
 
 def grad_kernel(mix_ref, slope_ref, out_ref):
     out_ref[...] = dot_nt(mix_ref[...], slope_ref[...])
 
 
-def sum_kernel(ids_ref, own_ref, near_ref, across_ref, out_ref):
-    out_ref[...] = summed(ids_ref, own_ref, near_ref, across_ref)
-
-
-def last_kernel(ids_ref, own_ref, far_ref, out_ref):
-    core = ids_ref[2] % 2
-    nodes = own_ref.shape[1]
+def back_one_kernel(own_ref, near_ref, across_ref, slope_ref, dz_ref):
+    dh = summed(own_ref, near_ref, across_ref)
+    dz_ref[...] = (dh.astype(jnp.float32) * slope_ref[...]).astype(dz_ref.dtype)
+
+
+def message_kernel(
+    dz_ref,
+    dz_swap_ref,
+    weight_ref,
+    block_ref,
+    mix_ref,
+    mix_swap_ref,
+    two_ref,
+    two_swap_ref,
+    out_ref,
+):
+    feat = lax.axis_index("feat")
+    width = out_ref.shape[0] // 2
+    hidden = weight_ref.shape[0]
+    half = dz_ref.shape[1]
+    mix, mix_swap, dz, dz_swap = mix_ref[...], mix_swap_ref[...], dz_ref[...], dz_swap_ref[...]
+    rows = weight_ref[pl.ds(pl.multiple_of(feat * width, width), width), :]
+    own = dot_nn(rows, dz).astype(jnp.bfloat16)
+    other = dot_nn(rows, dz_swap).astype(jnp.bfloat16)
+    total = dot_nn(own, block_ref[:half, :]) + dot_nn(other, block_ref[half:, :])
+    out_ref[:width, :] = total.astype(out_ref.dtype)
+    swap = feat % 2 == 1
+    one = dot_nt(jnp.where(swap, mix_swap, mix), jnp.where(swap, dz_swap, dz)) + dot_nt(
+        jnp.where(swap, mix, mix_swap), jnp.where(swap, dz, dz_swap)
+    )
+    two = two_ref[...] + two_swap_ref[...]
+    count = hidden // width
+    for index, grad in enumerate((one, two)):
+        grad = grad.astype(out_ref.dtype)
+        for part in range(count):
+            lane = (index * count + part) * hidden
+            out_ref[width:, lane : lane + hidden] = grad[part * width : (part + 1) * width, :]
+
+
+def last_kernel(
+    scale,
+    own_ref,
+    near_ref,
+    across_ref,
+    far_ref,
+    far_near_ref,
+    one_ref,
+    two_ref,
+    out_ref,
+):
+    odd = lax.axis_index("rep") % 2 == 1
+    core = lax.axis_index("feat") % 2
+    width, nodes = out_ref.shape
+    hidden = one_ref.shape[0]
     quarter = nodes // 4
     half = nodes // 2
+
+    def total(rows, columns):
+        refs = (near_ref, far_ref, far_near_ref)
+        value = jnp.where(odd, across_ref[rows, columns], own_ref[rows, columns])
+        value = value.astype(jnp.float32)
+        for ref in refs:
+            value += ref[rows, columns].astype(jnp.float32)
+        return value
+
     for part in range(4):
         lane = pl.multiple_of(
             jnp.bitwise_xor(part % 2, core) * half + (part // 2) * quarter, quarter
         )
-        here = pl.ds(lane, quarter)
-        out_ref[:, part * quarter : (part + 1) * quarter] = own_ref[:, here] + far_ref[:, here]
-
-
-def grad_total(part, scale):
-    part = part + routed(part, to_other_core)
-    part = part + routed(part, to_other_loop)
-    return (part + routed(part, to_far_rep)) * scale
+        out_ref[:, part * quarter : (part + 1) * quarter] = total(
+            pl.ds(0, width), pl.ds(lane, quarter)
+        ).astype(out_ref.dtype)
+    count = hidden // width
+    for index, grad_ref in enumerate((one_ref, two_ref)):
+        for part in range(count):
+            lane = (index * count + part) * hidden
+            grad_ref[part * width : (part + 1) * width, :] = (
+                total(pl.ds(width, width), pl.ds(lane, hidden)) * scale
+            )
 
 
 def paired_shards(
@@ -427,39 +508,57 @@
     panels = nodes // side
     half = nodes // 2
     scale = 1.0 / math.sqrt(nodes * lax.axis_size("loop"))
-    ids = jnp.stack([lax.axis_index(axis) for axis in mesh_axes]).astype(jnp.int32)
-    smem, vmem = pltpu.SMEM, pltpu.VMEM
+    product_flops = 2 * hidden * nodes * half
 
     across = routed(features, to_other_loop)
     pair = routed(features, to_feature_pair)
-    cot_pair = routed(cotangent, to_other_pair)
+    own_swap = routed(features, to_other_core)
     (block,) = local_call(
         functools.partial(place_kernel, panels, side),
         [bf16_array(nodes, nodes)],
-        [ids, section_counts[0, 0], tile_coords[0, 0], tile_values[0, 0]],
-        [smem, smem, smem, pl.ANY],
-        [pltpu.SemaphoreType.DMA((panels * panels,))],
+        [section_counts[0, 0]]
+        + [
+            pltpu.with_memory_space_constraint(value, pltpu.HBM)
+            for value in (tile_coords, tile_values)
+        ],
+        [pltpu.SMEM, pltpu.HBM, pltpu.HBM],
+        [
+            pltpu.SMEM(tile_coords.shape, jnp.int32),
+            pltpu.SemaphoreType.DMA,
+            pltpu.SemaphoreType.DMA((panels * panels,)),
+        ],
         flops=4_000_000_000,
     )
-    odd = lax.axis_index("rep") % 2 == 1
-    swapped = routed(
-        jnp.concatenate([jnp.where(odd, across, features), pair], axis=0), to_other_core
-    )
-    product_flops = 2 * hidden * nodes * half
-
+    one_turned, two_turned = local_call(
+        turn_kernel,
+        [bf16_array(hidden, hidden)] * 2,
+        [weight_one, lax.optimization_barrier((weight_two, block))[0]],
+    )
+    across, pair, block = lax.optimization_barrier((across, pair, block))
     (part_one,) = local_call(
         first_kernel,
         [bf16_array(hidden, half)],
-        [ids, features, across, pair, swapped, block],
-        [smem] + [vmem] * 5,
+        [
+            features,
+            across,
+            pair,
+            own_swap,
+            routed(across, to_other_core),
+            routed(pair, to_other_core),
+            block,
+        ],
+        None,
         [pltpu.VMEM((hidden, nodes), jnp.bfloat16)],
         flops=product_flops,
     )
+    cot_pair = routed(lax.optimization_barrier((cotangent, part_one))[0], to_other_pair)
+    near_one = routed(part_one, to_row_owner)
+    across_one = routed(part_one, to_other_loop)
     mix_one, h_one = local_call(
         layer_one_kernel,
         [bf16_array(hidden, half)] * 2,
-        [ids, part_one, routed(part_one, to_row_owner), routed(part_one, to_other_loop), weight_one],
-        [smem] + [vmem] * 4,
+        [part_one, near_one, across_one, one_turned],
+        None,
     )
     (part_two,) = local_call(
         forward_kernel,
@@ -467,17 +566,14 @@
         [h_one, routed(h_one, to_other_core), block],
         flops=product_flops,
     )
+    near_two, mix_across, cot_pair = lax.optimization_barrier(
+        (routed(part_two, to_other_rep), routed(mix_one, to_other_loop), cot_pair)
+    )
     mix_two, dz_two, dm_two = local_call(
         layer_two_kernel,
         [bf16_array(hidden, half)] * 3,
-        [ids, part_two, routed(part_two, to_other_rep), weight_two, cotangent, cot_pair],
-        [smem] + [vmem] * 5,
-    )
-    mix_here, slope_here = local_call(
-        slope_kernel,
-        [bf16_array(hidden, half), f32_array(hidden, half)],
-        [ids, mix_one, routed(mix_one, to_other_loop), weight_one],
-        [smem] + [vmem] * 3,
+        [part_two, near_two, two_turned, weight_two, cotangent, cot_pair],
+        None,
     )
     (part_three,) = local_call(
         backward_kernel,
@@ -486,41 +582,53 @@
         flops=product_flops,
     )
     (grad_two,) = local_call(grad_kernel, [f32_array(hidden, hidden)], [mix_two, dz_two])
-    grad_two = grad_total(grad_two, scale)
-    dz_one, dm_one, dm_send = local_call(
+    mix_here, slope_here = local_call(
+        slope_kernel,
+        [bf16_array(hidden, half), f32_array(hidden, half)],
+        [mix_one, lax.optimization_barrier((mix_across, part_three))[0], one_turned],
+        None,
+    )
+    (dz_one,) = local_call(
         back_one_kernel,
-        [bf16_array(hidden, half), bf16_array(width, half), bf16_array(width, half)],
+        [bf16_array(hidden, half)],
         [
-            ids,
             part_three,
             routed(part_three, to_column_owner),
             routed(part_three, to_other_loop),
             slope_here,
+        ],
+        None,
+    )
+    (message,) = local_call(
+        message_kernel,
+        [bf16_array(2 * width, nodes)],
+        [
+            dz_one,
+            routed(dz_one, to_other_core),
             weight_one,
+            block,
+            mix_here,
+            routed(mix_here, to_other_core),
+            grad_two,
+            routed(grad_two, to_other_core),
         ],
-        [smem] + [vmem] * 5,
-    )
-    (part_four,) = local_call(
-        backward_kernel,
-        [bf16_array(width, nodes)],
-        [dm_one, routed(dm_send, to_other_core), block],
+        None,
         flops=product_flops,
     )
-    (grad_one,) = local_call(grad_kernel, [f32_array(hidden, hidden)], [mix_here, dz_one])
-    grad_one = grad_total(grad_one, scale)
-    (near_sum,) = local_call(
-        sum_kernel,
-        [bf16_array(width, nodes)],
-        [ids, part_four, routed(part_four, to_column_owner), routed(part_four, to_other_loop)],
-        [smem] + [vmem] * 3,
-    )
-    (input_grad,) = local_call(
-        last_kernel,
-        [bf16_array(width, nodes)],
-        [ids, near_sum, routed(near_sum, to_far_rep)],
-        [smem] + [vmem] * 2,
-    )
-    return (grad_one, grad_two, input_grad)
+    return tuple(
+        local_call(
+            functools.partial(last_kernel, scale),
+            [f32_array(hidden, hidden), f32_array(hidden, hidden), bf16_array(width, nodes)],
+            [
+                    message,
+                routed(message, to_column_owner),
+                routed(message, to_other_loop),
+                routed(message, to_far_column_owner),
+                routed(message, to_last_column_owner),
+            ],
+            None,
+        )
+    )
 
 
 def solution(mesh):

time: 65.3 us -> 58.4 us (0.89)
  the two profiles are of different devices: /device:TPU:0 before, /device:TPU:17 now
where the time goes in v2:
time: 58.4 us; the launch traced here: 58 us
  waiting for transfers between devices  28.3 us (48%)
  starting transfers between devices  22.9 us (39%)
  Pallas kernels  5.22 us (9%)
  between operations  1.44 us (2%)
    ppermute x21, waiting for transfers between devices, routed(): return lax.ppermute(value, mesh_axes, pairs)  28.3 us
    ppermute x21, starting transfers between devices, routed(): return lax.ppermute(value, mesh_axes, pairs)  22.9 us
    pallas_call x12, Pallas kernels, local_call(): pl.pallas_call(kernel, out_shape=list(outs), in_specs=[pl.BlockSpec(memor...  5.22 us
  transfers between devices with their start and end apart: 21, of which 14 were waited for; matrix products, arithmetic and copies ran while one was open for 0% of the time, Pallas kernels for 4%

profile of v2, /device:TPU:17, one launch (start us, length us, event | category | flops | bytes accessed | tf_op | source)
XLA Modules:
  0.0 58.0 jit_solution(3773855945799313032)
XLA Ops:
  0.6 1.3 %collective-permute-start = (bf16[32,1024]{1,0:T(8,128)(2,1)}, bf16[32,1024]{1,0:T(8,128)(2,1)S(1)}, u32[]{:S(2)}, u32[]{:S(2)}) collective-permute-start(bf16[32,1024]{1,0:T(8,128)(2,1)} %own_ref.1), channel_id=1, source_target_pairs={{0,16},{1,17},{2,18},{3,19},{4,20},{5,21},{6,22},{7,23},{8,24},{9,... | collective-permute-start | bytes 196616 | tf_op jit(solution)/shard_map/ppermute | solution.py:189
  1.9 1.2 %collective-permute-start.1 = (bf16[32,1024]{1,0:T(8,128)(2,1)}, bf16[32,1024]{1,0:T(8,128)(2,1)S(1)}, u32[]{:S(2)}, u32[]{:S(2)}) collective-permute-start(bf16[32,1024]{1,0:T(8,128)(2,1)} %own_ref.1), channel_id=1, source_target_pairs={{0,2},{1,3},{2,0},{3,1},{4,22},{5,23},{6,20},{7,21},{8,10},{9,11},... | collective-permute-start | bytes 196616 | tf_op jit(solution)/shard_map/ppermute | solution.py:189
  3.1 1.2 %collective-permute-start.2 = (bf16[32,1024]{1,0:T(8,128)(2,1)}, bf16[32,1024]{1,0:T(8,128)(2,1)S(1)}, u32[]{:S(2)}, u32[]{:S(2)}) collective-permute-start(bf16[32,1024]{1,0:T(8,128)(2,1)} %own_ref.1), channel_id=1, source_target_pairs={{0,1},{1,0},{2,3},{3,2},{4,5},{5,4},{6,7},{7,6},{8,9},{9,8},{10,11... | collective-permute-start | bytes 196616 | tf_op jit(solution)/shard_map/ppermute | solution.py:189
  5.1 1.4 %shard_map.94.block_ref = bf16[1024,1024]{1,0:T(8,128)(2,1)S(1)} custom-call(s32[1]{0:T(128)} %bitcast.1.count_ref, s32[1,1,2,112]{3,2,1,0:T(2,128)} %coords_ref.1, bf16[1,1,112,128,128]{4,3,2,1,0:T(8,128)(2,1)} %tiles_ref.1), custom_call_target="tpu_custom_call" | custom-call | flops 4000000000 | bytes 7865220 | tf_op jit(solution)/shard_map/pallas_call | solution.py:233
  6.5 0.0 copy-start.3
  6.5 0.8 %collective-permute-start.3 = (bf16[32,1024]{1,0:T(8,128)(2,1)S(1)}, bf16[32,1024]{1,0:T(8,128)(2,1)S(1)}, u32[]{:S(2)}, u32[]{:S(2)}) collective-permute-start(bf16[32,1024]{1,0:T(8,128)(2,1)S(1)} %collective-permute-done.across_ref), channel_id=1, source_target_pairs={{0,1},{1,0},{2,3},{3,2},{4,5},{5,4},{6,7},{7,6},{8,9},{9,8},{10,11... | collective-permute-start | bytes 196616 | tf_op jit(solution)/shard_map/ppermute | solution.py:189
  7.3 0.0 collective-permute-start.4
  7.3 0.9 %collective-permute-done.3.across_swap_ref = bf16[32,1024]{1,0:T(8,128)(2,1)S(1)} collective-permute-done((bf16[32,1024]{1,0:T(8,128)(2,1)S(1)}, bf16[32,1024]{1,0:T(8,128)(2,1)S(1)}, u32[]{:S(2)}, u32[]{:S(2)}) %collective-permute-start.3) | collective-permute-done | bytes 65568 | tf_op jit(solution)/shard_map/ppermute | solution.py:189
  8.2 0.4 collective-permute-done.4.pair_swap_ref
  8.6 0.5 shard_map.95.own_ref
  9.1 2.7 %collective-permute-start.5 = (bf16[128,512]{1,0:T(8,128)(2,1)S(1)}, bf16[128,512]{1,0:T(8,128)(2,1)S(1)}, u32[]{:S(2)}, u32[]{:S(2)}) collective-permute-start(bf16[128,512]{1,0:T(8,128)(2,1)S(1)} %shard_map.95.own_ref), channel_id=1, source_target_pairs={{0,20},{1,21},{2,22},{3,23},{4,0},{5,1},{6,2},{7,3},{8,28},{9,29},... | collective-permute-start | bytes 393224 | tf_op jit(solution)/shard_map/ppermute | solution.py:189
  11.8 0.7 %collective-permute-start.6 = (bf16[128,512]{1,0:T(8,128)(2,1)S(1)}, bf16[128,512]{1,0:T(8,128)(2,1)S(1)}, u32[]{:S(2)}, u32[]{:S(2)}) collective-permute-start(bf16[128,512]{1,0:T(8,128)(2,1)S(1)} %shard_map.95.own_ref), channel_id=1, source_target_pairs={{0,16},{1,17},{2,18},{3,19},{4,20},{5,21},{6,22},{7,23},{8,24},{9,... | collective-permute-start | bytes 393224 | tf_op jit(solution)/shard_map/ppermute | solution.py:189
  12.5 0.1 shard_map.96
  12.6 2.5 %collective-permute-done.5.near_ref = bf16[128,512]{1,0:T(8,128)(2,1)S(1)} collective-permute-done((bf16[128,512]{1,0:T(8,128)(2,1)S(1)}, bf16[128,512]{1,0:T(8,128)(2,1)S(1)}, u32[]{:S(2)}, u32[]{:S(2)}) %collective-permute-start.5) | collective-permute-done | bytes 131104 | tf_op jit(solution)/shard_map/ppermute | solution.py:189
  15.1 1.4 %collective-permute-done.6.across_ref = bf16[128,512]{1,0:T(8,128)(2,1)S(1)} collective-permute-done((bf16[128,512]{1,0:T(8,128)(2,1)S(1)}, bf16[128,512]{1,0:T(8,128)(2,1)S(1)}, u32[]{:S(2)}, u32[]{:S(2)}) %collective-permute-start.6) | collective-permute-done | bytes 131104 | tf_op jit(solution)/shard_map/ppermute | solution.py:189
  16.4 0.2 shard_map.97
  16.7 1.3 %collective-permute-start.7 = (bf16[128,512]{1,0:T(8,128)(2,1)S(1)}, bf16[128,512]{1,0:T(8,128)(2,1)S(1)}, u32[]{:S(2)}, u32[]{:S(2)}) collective-permute-start(bf16[128,512]{1,0:T(8,128)(2,1)S(1)} %get-tuple-element.26.own_ref), channel_id=1, source_target_pairs={{0,1},{1,0},{2,3},{3,2},{4,5},{5,4},{6,7},{7,6},{8,9},{9,8},{10,11... | collective-permute-start | bytes 393224 | tf_op jit(solution)/shard_map/ppermute | solution.py:189
  18.0 0.7 %collective-permute-start.9 = (bf16[128,512]{1,0:T(8,128)(2,1)S(1)}, bf16[128,512]{1,0:T(8,128)(2,1)S(1)}, u32[]{:S(2)}, u32[]{:S(2)}) collective-permute-start(bf16[128,512]{1,0:T(8,128)(2,1)S(1)} %get-tuple-element.27.mix_ref), channel_id=1, source_target_pairs={{0,16},{1,17},{2,18},{3,19},{4,20},{5,21},{6,22},{7,23},{8,24},{9,... | collective-permute-start | bytes 393224 | tf_op jit(solution)/shard_map/ppermute | solution.py:189
  18.7 0.3 collective-permute-done.7.other_ref
  19.0 0.5 shard_map.98.own_ref
  19.5 2.5 %collective-permute-start.8 = (bf16[128,512]{1,0:T(8,128)(2,1)S(1)}, bf16[128,512]{1,0:T(8,128)(2,1)S(1)}, u32[]{:S(2)}, u32[]{:S(2)}) collective-permute-start(bf16[128,512]{1,0:T(8,128)(2,1)S(1)} %shard_map.98.own_ref), channel_id=1, source_target_pairs={{0,4},{1,5},{2,6},{3,7},{4,0},{5,1},{6,2},{7,3},{8,12},{9,13},{10,... | collective-permute-start | bytes 393224 | tf_op jit(solution)/shard_map/ppermute | solution.py:189
  22.0 1.2 %collective-permute-start.10 = (bf16[128,256]{1,0:T(8,128)(2,1)S(1)}, bf16[128,256]{1,0:T(8,128)(2,1)S(1)}, u32[]{:S(2)}, u32[]{:S(2)}) collective-permute-start(bf16[128,256]{1,0:T(8,128)(2,1)S(1)} %copy-done.3), channel_id=1, source_target_pairs={{0,2},{1,3},{2,0},{3,1},{4,6},{5,7},{6,4},{7,5},{8,10},{9,11},{10,... | collective-permute-start | bytes 196616 | tf_op jit(solution)/shard_map/ppermute | solution.py:189
  23.2 2.2 %collective-permute-done.10.cot_pair_ref = bf16[128,256]{1,0:T(8,128)(2,1)S(1)} collective-permute-done((bf16[128,256]{1,0:T(8,128)(2,1)S(1)}, bf16[128,256]{1,0:T(8,128)(2,1)S(1)}, u32[]{:S(2)}, u32[]{:S(2)}) %collective-permute-start.10) | collective-permute-done | bytes 65568 | tf_op jit(solution)/shard_map/ppermute | solution.py:189
  25.4 0.2 collective-permute-done.8.near_ref
  25.5 0.4 shard_map.99
  25.9 1.4 %collective-permute-start.11 = (bf16[128,512]{1,0:T(8,128)(2,1)S(1)}, bf16[128,512]{1,0:T(8,128)(2,1)S(1)}, u32[]{:S(2)}, u32[]{:S(2)}) collective-permute-start(bf16[128,512]{1,0:T(8,128)(2,1)S(1)} %get-tuple-element.32.own_ref), channel_id=1, source_target_pairs={{0,1},{1,0},{2,3},{3,2},{4,5},{5,4},{6,7},{7,6},{8,9},{9,8},{10,11... | collective-permute-start | bytes 393224 | tf_op jit(solution)/shard_map/ppermute | solution.py:189
  27.4 1.0 %collective-permute-done.11.other_ref = bf16[128,512]{1,0:T(8,128)(2,1)S(1)} collective-permute-done((bf16[128,512]{1,0:T(8,128)(2,1)S(1)}, bf16[128,512]{1,0:T(8,128)(2,1)S(1)}, u32[]{:S(2)}, u32[]{:S(2)}) %collective-permute-start.11) | collective-permute-done | bytes 131104 | tf_op jit(solution)/shard_map/ppermute | solution.py:189
  28.3 0.3 shard_map.100.own_ref
  28.7 1.0 %collective-permute-start.12 = (bf16[128,512]{1,0:T(8,128)(2,1)S(1)}, bf16[128,512]{1,0:T(8,128)(2,1)S(1)}, u32[]{:S(2)}, u32[]{:S(2)}) collective-permute-start(bf16[128,512]{1,0:T(8,128)(2,1)S(1)} %shard_map.100.own_ref), channel_id=1, source_target_pairs={{0,4},{1,5},{2,6},{3,7},{4,16},{5,17},{6,18},{7,19},{8,12},{9,13},... | collective-permute-start | bytes 393224 | tf_op jit(solution)/shard_map/ppermute | solution.py:189
  29.7 0.7 %collective-permute-start.13 = (bf16[128,512]{1,0:T(8,128)(2,1)S(1)}, bf16[128,512]{1,0:T(8,128)(2,1)S(1)}, u32[]{:S(2)}, u32[]{:S(2)}) collective-permute-start(bf16[128,512]{1,0:T(8,128)(2,1)S(1)} %shard_map.100.own_ref), channel_id=1, source_target_pairs={{0,16},{1,17},{2,18},{3,19},{4,20},{5,21},{6,22},{7,23},{8,24},{9,... | collective-permute-start | bytes 393224 | tf_op jit(solution)/shard_map/ppermute | solution.py:189
  30.4 0.2 shard_map.101
  30.7 1.0 %collective-permute-start.15 = (bf16[128,512]{1,0:T(8,128)(2,1)S(1)}, bf16[128,512]{1,0:T(8,128)(2,1)S(1)}, u32[]{:S(2)}, u32[]{:S(2)}) collective-permute-start(bf16[128,512]{1,0:T(8,128)(2,1)S(1)} %get-tuple-element.36.mix_ref), channel_id=1, source_target_pairs={{0,1},{1,0},{2,3},{3,2},{4,5},{5,4},{6,7},{7,6},{8,9},{9,8},{10,11... | collective-permute-start | bytes 393224 | tf_op jit(solution)/shard_map/ppermute | solution.py:189
  31.7 2.7 %collective-permute-done.12.near_ref = bf16[128,512]{1,0:T(8,128)(2,1)S(1)} collective-permute-done((bf16[128,512]{1,0:T(8,128)(2,1)S(1)}, bf16[128,512]{1,0:T(8,128)(2,1)S(1)}, u32[]{:S(2)}, u32[]{:S(2)}) %collective-permute-start.12) | collective-permute-done | bytes 131104 | tf_op jit(solution)/shard_map/ppermute | solution.py:189
  34.4 3.5 %collective-permute-done.13.across_ref = bf16[128,512]{1,0:T(8,128)(2,1)S(1)} collective-permute-done((bf16[128,512]{1,0:T(8,128)(2,1)S(1)}, bf16[128,512]{1,0:T(8,128)(2,1)S(1)}, u32[]{:S(2)}, u32[]{:S(2)}) %collective-permute-start.13) | collective-permute-done | bytes 131104 | tf_op jit(solution)/shard_map/ppermute | solution.py:189
  37.8 0.1 shard_map.102.dz_ref
  37.9 0.6 collective-permute-start.14
  38.5 0.2 shard_map.103.two_ref
  38.6 0.1 collective-permute-start.16
  38.7 1.2 %collective-permute-done.16.two_swap_ref = f32[128,128]{1,0:T(8,128)S(1)} collective-permute-done((f32[128,128]{1,0:T(8,128)S(1)}, f32[128,128]{1,0:T(8,128)S(1)}, u32[]{:S(2)}, u32[]{:S(2)}) %collective-permute-start.16) | collective-permute-done | bytes 65568 | tf_op jit(solution)/shard_map/ppermute | solution.py:189
  40.0 0.7 %shard_map.104.own_ref = bf16[64,1024]{1,0:T(8,128)(2,1)S(1)} custom-call(bf16[128,512]{1,0:T(8,128)(2,1)S(1)} %shard_map.102.dz_ref, bf16[128,512]{1,0:T(8,128)(2,1)S(1)} %collective-permute-done.14.dz_swap_ref, bf16[128,128]{1,0:T(8,128)(2,1)S(1)} %copy-done, bf16[1024,1024]{1,0:T(8,128)(2,1)S(1)} %shard_map.94.block_ref, ...), custom_call_target="tpu_custom_call" | custom-call | flops 134217728 | bytes 3047424 | tf_op jit(solution)/shard_map/pallas_call | solution.py:233
  40.6 0.1 collective-permute-start.17
  40.7 0.8 %collective-permute-start.18 = (bf16[64,1024]{1,0:T(8,128)(2,1)S(1)}, bf16[64,1024]{1,0:T(8,128)(2,1)S(1)}, u32[]{:S(2)}, u32[]{:S(2)}) collective-permute-start(bf16[64,1024]{1,0:T(8,128)(2,1)S(1)} %shard_map.104.own_ref), channel_id=1, source_target_pairs={{0,16},{1,17},{2,18},{3,19},{4,20},{5,21},{6,22},{7,23},{8,24},{9,... | collective-permute-start | bytes 393224 | tf_op jit(solution)/shard_map/ppermute | solution.py:189
  41.5 0.9 %collective-permute-start.19 = (bf16[64,1024]{1,0:T(8,128)(2,1)S(1)}, bf16[64,1024]{1,0:T(8,128)(2,1)S(1)}, u32[]{:S(2)}, u32[]{:S(2)}) collective-permute-start(bf16[64,1024]{1,0:T(8,128)(2,1)S(1)} %shard_map.104.own_ref), channel_id=1, source_target_pairs={{0,8},{1,9},{2,10},{3,11},{4,28},{5,29},{6,30},{7,31},{8,0},{9,1},... | collective-permute-start | bytes 393224 | tf_op jit(solution)/shard_map/ppermute | solution.py:189
  42.4 2.6 %collective-permute-start.20 = (bf16[64,1024]{1,0:T(8,128)(2,1)S(1)}, bf16[64,1024]{1,0:T(8,128)(2,1)S(1)}, u32[]{:S(2)}, u32[]{:S(2)}) collective-permute-start(bf16[64,1024]{1,0:T(8,128)(2,1)S(1)} %shard_map.104.own_ref), channel_id=1, source_target_pairs={{0,12},{1,13},{2,14},{3,15},{4,24},{5,25},{6,26},{7,27},{8,4},{9,5... | collective-permute-start | bytes 393224 | tf_op jit(solution)/shard_map/ppermute | solution.py:189
  45.0 1.6 %collective-permute-done.17.near_ref = bf16[64,1024]{1,0:T(8,128)(2,1)S(1)} collective-permute-done((bf16[64,1024]{1,0:T(8,128)(2,1)S(1)}, bf16[64,1024]{1,0:T(8,128)(2,1)S(1)}, u32[]{:S(2)}, u32[]{:S(2)}) %collective-permute-start.17) | collective-permute-done | bytes 131104 | tf_op jit(solution)/shard_map/ppermute | solution.py:189
  46.6 1.9 %collective-permute-done.18.across_ref = bf16[64,1024]{1,0:T(8,128)(2,1)S(1)} collective-permute-done((bf16[64,1024]{1,0:T(8,128)(2,1)S(1)}, bf16[64,1024]{1,0:T(8,128)(2,1)S(1)}, u32[]{:S(2)}, u32[]{:S(2)}) %collective-permute-start.18) | collective-permute-done | bytes 131104 | tf_op jit(solution)/shard_map/ppermute | solution.py:189
  48.5 8.7 %collective-permute-done.20.far_near_ref = bf16[64,1024]{1,0:T(8,128)(2,1)S(1)} collective-permute-done((bf16[64,1024]{1,0:T(8,128)(2,1)S(1)}, bf16[64,1024]{1,0:T(8,128)(2,1)S(1)}, u32[]{:S(2)}, u32[]{:S(2)}) %collective-permute-start.20) | collective-permute-done | bytes 131104 | tf_op jit(solution)/shard_map/ppermute | solution.py:189
  57.2 0.7 %shard_map.105 = (f32[128,128]{1,0:T(8,128)}, f32[128,128]{1,0:T(8,128)}, bf16[32,1024]{1,0:T(8,128)(2,1)}) custom-call(bf16[64,1024]{1,0:T(8,128)(2,1)S(1)} %shard_map.104.own_ref, bf16[64,1024]{1,0:T(8,128)(2,1)S(1)} %collective-permute-done.17.near_ref, bf16[64,1024]{1,0:T(8,128)(2,1)S(1)} %collective-permute-done.18.across_ref, ...), custom_call_target="tpu_custom_call" | custom-call | bytes 917504 | tf_op jit(solution)/shard_map/pallas_call | solution.py:233
  (14 shorter events, 0.0 us)
Async XLA Ops:
  0.6 5.9 %collective-permute-start = (bf16[32,1024]{1,0:T(8,128)(2,1)}, bf16[32,1024]{1,0:T(8,128)(2,1)S(1)}, u32[]{:S(2)}, u32[]{:S(2)}) collective-permute-start(bf16[32,1024]{1,0:T(8,128)(2,1)} %own_ref.1), channel_id=1, source_target_pairs={{0,16},{1,17},{2,18},{3,19},{4,20},{5,21},{6,22},{7,23},{8,24},{9,... | collective-permute-start | bytes 196616 | tf_op jit(solution)/shard_map/ppermute | solution.py:189
  1.9 4.6 %collective-permute-start.1 = (bf16[32,1024]{1,0:T(8,128)(2,1)}, bf16[32,1024]{1,0:T(8,128)(2,1)S(1)}, u32[]{:S(2)}, u32[]{:S(2)}) collective-permute-start(bf16[32,1024]{1,0:T(8,128)(2,1)} %own_ref.1), channel_id=1, source_target_pairs={{0,2},{1,3},{2,0},{3,1},{4,22},{5,23},{6,20},{7,21},{8,10},{9,11},... | collective-permute-start | bytes 196616 | tf_op jit(solution)/shard_map/ppermute | solution.py:189
  3.1 4.2 %collective-permute-start.2 = (bf16[32,1024]{1,0:T(8,128)(2,1)}, bf16[32,1024]{1,0:T(8,128)(2,1)S(1)}, u32[]{:S(2)}, u32[]{:S(2)}) collective-permute-start(bf16[32,1024]{1,0:T(8,128)(2,1)} %own_ref.1), channel_id=1, source_target_pairs={{0,1},{1,0},{2,3},{3,2},{4,5},{5,4},{6,7},{7,6},{8,9},{9,8},{10,11... | collective-permute-start | bytes 196616 | tf_op jit(solution)/shard_map/ppermute | solution.py:189
  5.0 3.6 %copy-start.2 = (bf16[32,1024]{1,0:T(8,128)(2,1)S(1)}, bf16[32,1024]{1,0:T(8,128)(2,1)}, u32[]{:S(2)}) copy-start(bf16[32,1024]{1,0:T(8,128)(2,1)} %own_ref.1) | copy-start | bytes 196612
  5.0 7.5 %copy-start = (bf16[128,128]{1,0:T(8,128)(2,1)S(1)}, bf16[128,128]{1,0:T(8,128)(2,1)}, u32[]{:S(2)}) copy-start(bf16[128,128]{1,0:T(8,128)(2,1)} %weight_ref.3) | copy-start | bytes 98308
  5.1 7.5 %copy-start.1 = (bf16[128,128]{1,0:T(8,128)(2,1)S(1)}, bf16[128,128]{1,0:T(8,128)(2,1)}, u32[]{:S(2)}) copy-start(bf16[128,128]{1,0:T(8,128)(2,1)} %weight_ref.2) | copy-start | bytes 98308
  6.5 15.5 %copy-start.3 = (bf16[128,256]{1,0:T(8,128)(2,1)S(1)}, bf16[128,256]{1,0:T(8,128)(2,1)}, u32[]{:S(2)}) copy-start(bf16[128,256]{1,0:T(8,128)(2,1)} %cot_ref.1) | copy-start | bytes 196612
  6.5 1.7 %collective-permute-start.3 = (bf16[32,1024]{1,0:T(8,128)(2,1)S(1)}, bf16[32,1024]{1,0:T(8,128)(2,1)S(1)}, u32[]{:S(2)}, u32[]{:S(2)}) collective-permute-start(bf16[32,1024]{1,0:T(8,128)(2,1)S(1)} %collective-permute-done.across_ref), channel_id=1, source_target_pairs={{0,1},{1,0},{2,3},{3,2},{4,5},{5,4},{6,7},{7,6},{8,9},{9,8},{10,11... | collective-permute-start | bytes 196616 | tf_op jit(solution)/shard_map/ppermute | solution.py:189
  7.3 1.3 %collective-permute-start.4 = (bf16[32,1024]{1,0:T(8,128)(2,1)S(1)}, bf16[32,1024]{1,0:T(8,128)(2,1)S(1)}, u32[]{:S(2)}, u32[]{:S(2)}) collective-permute-start(bf16[32,1024]{1,0:T(8,128)(2,1)S(1)} %collective-permute-done.1.pair_ref), channel_id=1, source_target_pairs={{0,1},{1,0},{2,3},{3,2},{4,5},{5,4},{6,7},{7,6},{8,9},{9,8},{10,11... | collective-permute-start | bytes 196616 | tf_op jit(solution)/shard_map/ppermute | solution.py:189
  9.1 6.0 %collective-permute-start.5 = (bf16[128,512]{1,0:T(8,128)(2,1)S(1)}, bf16[128,512]{1,0:T(8,128)(2,1)S(1)}, u32[]{:S(2)}, u32[]{:S(2)}) collective-permute-start(bf16[128,512]{1,0:T(8,128)(2,1)S(1)} %shard_map.95.own_ref), channel_id=1, source_target_pairs={{0,20},{1,21},{2,22},{3,23},{4,0},{5,1},{6,2},{7,3},{8,28},{9,29},... | collective-permute-start | bytes 393224 | tf_op jit(solution)/shard_map/ppermute | solution.py:189
  11.8 4.6 %collective-permute-start.6 = (bf16[128,512]{1,0:T(8,128)(2,1)S(1)}, bf16[128,512]{1,0:T(8,128)(2,1)S(1)}, u32[]{:S(2)}, u32[]{:S(2)}) collective-permute-start(bf16[128,512]{1,0:T(8,128)(2,1)S(1)} %shard_map.95.own_ref), channel_id=1, source_target_pairs={{0,16},{1,17},{2,18},{3,19},{4,20},{5,21},{6,22},{7,23},{8,24},{9,... | collective-permute-start | bytes 393224 | tf_op jit(solution)/shard_map/ppermute | solution.py:189
  16.7 2.3 %collective-permute-start.7 = (bf16[128,512]{1,0:T(8,128)(2,1)S(1)}, bf16[128,512]{1,0:T(8,128)(2,1)S(1)}, u32[]{:S(2)}, u32[]{:S(2)}) collective-permute-start(bf16[128,512]{1,0:T(8,128)(2,1)S(1)} %get-tuple-element.26.own_ref), channel_id=1, source_target_pairs={{0,1},{1,0},{2,3},{3,2},{4,5},{5,4},{6,7},{7,6},{8,9},{9,8},{10,11... | collective-permute-start | bytes 393224 | tf_op jit(solution)/shard_map/ppermute | solution.py:189
  18.0 7.4 %collective-permute-start.9 = (bf16[128,512]{1,0:T(8,128)(2,1)S(1)}, bf16[128,512]{1,0:T(8,128)(2,1)S(1)}, u32[]{:S(2)}, u32[]{:S(2)}) collective-permute-start(bf16[128,512]{1,0:T(8,128)(2,1)S(1)} %get-tuple-element.27.mix_ref), channel_id=1, source_target_pairs={{0,16},{1,17},{2,18},{3,19},{4,20},{5,21},{6,22},{7,23},{8,24},{9,... | collective-permute-start | bytes 393224 | tf_op jit(solution)/shard_map/ppermute | solution.py:189
  19.5 6.1 %collective-permute-start.8 = (bf16[128,512]{1,0:T(8,128)(2,1)S(1)}, bf16[128,512]{1,0:T(8,128)(2,1)S(1)}, u32[]{:S(2)}, u32[]{:S(2)}) collective-permute-start(bf16[128,512]{1,0:T(8,128)(2,1)S(1)} %shard_map.98.own_ref), channel_id=1, source_target_pairs={{0,4},{1,5},{2,6},{3,7},{4,0},{5,1},{6,2},{7,3},{8,12},{9,13},{10,... | collective-permute-start | bytes 393224 | tf_op jit(solution)/shard_map/ppermute | solution.py:189
  22.0 3.4 %collective-permute-start.10 = (bf16[128,256]{1,0:T(8,128)(2,1)S(1)}, bf16[128,256]{1,0:T(8,128)(2,1)S(1)}, u32[]{:S(2)}, u32[]{:S(2)}) collective-permute-start(bf16[128,256]{1,0:T(8,128)(2,1)S(1)} %copy-done.3), channel_id=1, source_target_pairs={{0,2},{1,3},{2,0},{3,1},{4,6},{5,7},{6,4},{7,5},{8,10},{9,11},{10,... | collective-permute-start | bytes 196616 | tf_op jit(solution)/shard_map/ppermute | solution.py:189
  25.9 2.4 %collective-permute-start.11 = (bf16[128,512]{1,0:T(8,128)(2,1)S(1)}, bf16[128,512]{1,0:T(8,128)(2,1)S(1)}, u32[]{:S(2)}, u32[]{:S(2)}) collective-permute-start(bf16[128,512]{1,0:T(8,128)(2,1)S(1)} %get-tuple-element.32.own_ref), channel_id=1, source_target_pairs={{0,1},{1,0},{2,3},{3,2},{4,5},{5,4},{6,7},{7,6},{8,9},{9,8},{10,11... | collective-permute-start | bytes 393224 | tf_op jit(solution)/shard_map/ppermute | solution.py:189
  28.7 5.7 %collective-permute-start.12 = (bf16[128,512]{1,0:T(8,128)(2,1)S(1)}, bf16[128,512]{1,0:T(8,128)(2,1)S(1)}, u32[]{:S(2)}, u32[]{:S(2)}) collective-permute-start(bf16[128,512]{1,0:T(8,128)(2,1)S(1)} %shard_map.100.own_ref), channel_id=1, source_target_pairs={{0,4},{1,5},{2,6},{3,7},{4,16},{5,17},{6,18},{7,19},{8,12},{9,13},... | collective-permute-start | bytes 393224 | tf_op jit(solution)/shard_map/ppermute | solution.py:189
  29.7 8.1 %collective-permute-start.13 = (bf16[128,512]{1,0:T(8,128)(2,1)S(1)}, bf16[128,512]{1,0:T(8,128)(2,1)S(1)}, u32[]{:S(2)}, u32[]{:S(2)}) collective-permute-start(bf16[128,512]{1,0:T(8,128)(2,1)S(1)} %shard_map.100.own_ref), channel_id=1, source_target_pairs={{0,16},{1,17},{2,18},{3,19},{4,20},{5,21},{6,22},{7,23},{8,24},{9,... | collective-permute-start | bytes 393224 | tf_op jit(solution)/shard_map/ppermute | solution.py:189
  30.7 9.3 %collective-permute-start.15 = (bf16[128,512]{1,0:T(8,128)(2,1)S(1)}, bf16[128,512]{1,0:T(8,128)(2,1)S(1)}, u32[]{:S(2)}, u32[]{:S(2)}) collective-permute-start(bf16[128,512]{1,0:T(8,128)(2,1)S(1)} %get-tuple-element.36.mix_ref), channel_id=1, source_target_pairs={{0,1},{1,0},{2,3},{3,2},{4,5},{5,4},{6,7},{7,6},{8,9},{9,8},{10,11... | collective-permute-start | bytes 393224 | tf_op jit(solution)/shard_map/ppermute | solution.py:189
  37.9 2.1 %collective-permute-start.14 = (bf16[128,512]{1,0:T(8,128)(2,1)S(1)}, bf16[128,512]{1,0:T(8,128)(2,1)S(1)}, u32[]{:S(2)}, u32[]{:S(2)}) collective-permute-start(bf16[128,512]{1,0:T(8,128)(2,1)S(1)} %shard_map.102.dz_ref), channel_id=1, source_target_pairs={{0,1},{1,0},{2,3},{3,2},{4,5},{5,4},{6,7},{7,6},{8,9},{9,8},{10,11... | collective-permute-start | bytes 393224 | tf_op jit(solution)/shard_map/ppermute | solution.py:189
  38.6 1.3 %collective-permute-start.16 = (f32[128,128]{1,0:T(8,128)S(1)}, f32[128,128]{1,0:T(8,128)S(1)}, u32[]{:S(2)}, u32[]{:S(2)}) collective-permute-start(f32[128,128]{1,0:T(8,128)S(1)} %shard_map.103.two_ref), channel_id=1, source_target_pairs={{0,1},{1,0},{2,3},{3,2},{4,5},{5,4},{6,7},{7,6},{8,9},{9,8},{10,11... | collective-permute-start | bytes 196616 | tf_op jit(solution)/shard_map/ppermute | solution.py:189
  40.6 6.0 %collective-permute-start.17 = (bf16[64,1024]{1,0:T(8,128)(2,1)S(1)}, bf16[64,1024]{1,0:T(8,128)(2,1)S(1)}, u32[]{:S(2)}, u32[]{:S(2)}) collective-permute-start(bf16[64,1024]{1,0:T(8,128)(2,1)S(1)} %shard_map.104.own_ref), channel_id=1, source_target_pairs={{0,4},{1,5},{2,6},{3,7},{4,16},{5,17},{6,18},{7,19},{8,12},{9,13},... | collective-permute-start | bytes 393224 | tf_op jit(solution)/shard_map/ppermute | solution.py:189
  40.7 7.8 %collective-permute-start.18 = (bf16[64,1024]{1,0:T(8,128)(2,1)S(1)}, bf16[64,1024]{1,0:T(8,128)(2,1)S(1)}, u32[]{:S(2)}, u32[]{:S(2)}) collective-permute-start(bf16[64,1024]{1,0:T(8,128)(2,1)S(1)} %shard_map.104.own_ref), channel_id=1, source_target_pairs={{0,16},{1,17},{2,18},{3,19},{4,20},{5,21},{6,22},{7,23},{8,24},{9,... | collective-permute-start | bytes 393224 | tf_op jit(solution)/shard_map/ppermute | solution.py:189
  41.5 7.0 %collective-permute-start.19 = (bf16[64,1024]{1,0:T(8,128)(2,1)S(1)}, bf16[64,1024]{1,0:T(8,128)(2,1)S(1)}, u32[]{:S(2)}, u32[]{:S(2)}) collective-permute-start(bf16[64,1024]{1,0:T(8,128)(2,1)S(1)} %shard_map.104.own_ref), channel_id=1, source_target_pairs={{0,8},{1,9},{2,10},{3,11},{4,28},{5,29},{6,30},{7,31},{8,0},{9,1},... | collective-permute-start | bytes 393224 | tf_op jit(solution)/shard_map/ppermute | solution.py:189
  42.4 14.8 %collective-permute-start.20 = (bf16[64,1024]{1,0:T(8,128)(2,1)S(1)}, bf16[64,1024]{1,0:T(8,128)(2,1)S(1)}, u32[]{:S(2)}, u32[]{:S(2)}) collective-permute-start(bf16[64,1024]{1,0:T(8,128)(2,1)S(1)} %shard_map.104.own_ref), channel_id=1, source_target_pairs={{0,12},{1,13},{2,14},{3,15},{4,24},{5,25},{6,26},{7,27},{8,4},{9,5... | collective-permute-start | bytes 393224 | tf_op jit(solution)/shard_map/ppermute | solution.py:189

commit v3 on v2

--- a/solution.py
+++ b/solution.py
@@ -176,13 +176,16 @@
 vmem_bytes = 24 * 1024 * 1024
 
 
-def routed(value, target):
+def routed(value, target, outward=False):
     loops, reps, feats = (lax.axis_size(axis) for axis in mesh_axes)
     pairs = []
     for i in range(loops):
         for r in range(reps):
             for f in range(feats):
-                to_loop, to_rep, to_feat = target(i, r, f)
+                idle = r >= loops
+                if idle and outward:
+                    continue
+                to_loop, to_rep, to_feat = to_other_core(i, r, f) if idle else target(i, r, f)
                 pairs.append(
                     ((i * reps + r) * feats + f, (to_loop * reps + to_rep) * feats + to_feat)
                 )
@@ -201,6 +204,10 @@
     return 1 - i, r, f
 
 
+def to_odd_across(i, r, f):
+    return (1 - i, r, f) if r % 2 else (i, r, f ^ 1)
+
+
 def to_other_rep(i, r, f):
     return i, r ^ 1, f
 
@@ -211,6 +218,10 @@
 
 def to_column_owner(i, r, f):
     return (1 - i, r - 1, f) if r % 2 else (i, r + 1, f)
+
+
+def to_far_rep(i, r, f):
+    return i, r ^ 2, f
 
 
 def to_far_column_owner(i, r, f):
@@ -265,11 +276,21 @@
     tiles_ref,
     block_ref,
     coords,
+    held,
     list_sem,
     sems,
 ):
+    chunks = sems.shape[0]
+    size = held.shape[0] // chunks
     lists = pltpu.make_async_copy(coords_ref, coords, list_sem)
     lists.start()
+    copies = []
+    for chunk in range(chunks):
+        here = pl.ds(chunk * size, size)
+        copies.append(
+            pltpu.make_async_copy(tiles_ref.at[0, 0, here], held.at[here], sems.at[chunk])
+        )
+        copies[-1].start()
     block_ref[...] = jnp.zeros_like(block_ref)
     quarter = panels // 4
     core = lax.axis_index("feat") % 2
@@ -281,34 +302,25 @@
         half = jnp.bitwise_xor(part % 2, core)
         return pl.multiple_of(((half * 2 + part // 2) * quarter + panel % quarter) * side, side)
 
-    def tile_copy(slot):
-        return pltpu.make_async_copy(
-            tiles_ref.at[0, 0, slot],
-            block_ref.at[
-                pl.ds(start_of(coords[0, 0, 0, slot]), side),
-                pl.ds(start_of(coords[0, 0, 1, slot]), side),
-            ],
-            sems.at[slot],
-        )
-
-    def in_groups(act):
-        group = 8
-
-        def some(index, carry):
-            for offset in range(group):
-                act(index * group + offset)
-            return carry
-
-        def one(slot, carry):
-            act(slot)
-            return carry
-
-        whole = count // group
-        lax.fori_loop(0, whole, some, 0)
-        lax.fori_loop(whole * group, count, one, 0)
-
-    in_groups(lambda slot: tile_copy(slot).start())
-    in_groups(lambda slot: tile_copy(slot).wait())
+    def place(slot, carry):
+        rows = pl.ds(start_of(coords[0, 0, 0, slot]), side)
+        columns = pl.ds(start_of(coords[0, 0, 1, slot]), side)
+        block_ref[rows, columns] = held[slot]
+        return carry
+
+    group = 4
+
+    def place_group(index, carry):
+        for offset in range(group):
+            place(index * group + offset, carry)
+        return carry
+
+    for chunk in range(chunks):
+        copies[chunk].wait()
+        end = jnp.minimum(count, (chunk + 1) * size)
+        whole = end // group
+        lax.fori_loop(chunk * size // group, whole, place_group, 0)
+        lax.fori_loop(jnp.maximum(whole * group, chunk * size), end, place, 0)
 
 
 def turn_kernel(one_ref, two_ref, one_turned_ref, two_turned_ref):
@@ -457,46 +469,31 @@
             out_ref[width:, lane : lane + hidden] = grad[part * width : (part + 1) * width, :]
 
 
-def last_kernel(
-    scale,
-    own_ref,
-    near_ref,
-    across_ref,
-    far_ref,
-    far_near_ref,
-    one_ref,
-    two_ref,
-    out_ref,
-):
-    odd = lax.axis_index("rep") % 2 == 1
+def near_kernel(own_ref, near_ref, across_ref, out_ref):
+    out_ref[...] = summed(own_ref, near_ref, across_ref)
+
+
+def last_kernel(scale, own_ref, far_ref, one_ref, two_ref, out_ref):
     core = lax.axis_index("feat") % 2
     width, nodes = out_ref.shape
     hidden = one_ref.shape[0]
     quarter = nodes // 4
     half = nodes // 2
-
-    def total(rows, columns):
-        refs = (near_ref, far_ref, far_near_ref)
-        value = jnp.where(odd, across_ref[rows, columns], own_ref[rows, columns])
-        value = value.astype(jnp.float32)
-        for ref in refs:
-            value += ref[rows, columns].astype(jnp.float32)
-        return value
-
     for part in range(4):
         lane = pl.multiple_of(
             jnp.bitwise_xor(part % 2, core) * half + (part // 2) * quarter, quarter
         )
-        out_ref[:, part * quarter : (part + 1) * quarter] = total(
-            pl.ds(0, width), pl.ds(lane, quarter)
-        ).astype(out_ref.dtype)
+        columns = pl.ds(lane, quarter)
+        out_ref[:, part * quarter : (part + 1) * quarter] = (
+            own_ref[:width, columns] + far_ref[:width, columns]
+        )
     count = hidden // width
     for index, grad_ref in enumerate((one_ref, two_ref)):
         for part in range(count):
             lane = (index * count + part) * hidden
-            grad_ref[part * width : (part + 1) * width, :] = (
-                total(pl.ds(width, width), pl.ds(lane, hidden)) * scale
-            )
+            total = own_ref[width:, lane : lane + hidden].astype(jnp.float32)
+            total += far_ref[width:, lane : lane + hidden].astype(jnp.float32)
+            grad_ref[part * width : (part + 1) * width, :] = total * scale
 
 
 def paired_shards(
@@ -524,8 +521,9 @@
         [pltpu.SMEM, pltpu.HBM, pltpu.HBM],
         [
             pltpu.SMEM(tile_coords.shape, jnp.int32),
+            pltpu.VMEM((panels * panels, side, side), jnp.bfloat16),
             pltpu.SemaphoreType.DMA,
-            pltpu.SemaphoreType.DMA((panels * panels,)),
+            pltpu.SemaphoreType.DMA((4,)),
         ],
         flops=4_000_000_000,
     )
@@ -551,9 +549,8 @@
         [pltpu.VMEM((hidden, nodes), jnp.bfloat16)],
         flops=product_flops,
     )
-    cot_pair = routed(lax.optimization_barrier((cotangent, part_one))[0], to_other_pair)
     near_one = routed(part_one, to_row_owner)
-    across_one = routed(part_one, to_other_loop)
+    across_one = routed(part_one, to_odd_across)
     mix_one, h_one = local_call(
         layer_one_kernel,
         [bf16_array(hidden, half)] * 2,
@@ -566,38 +563,45 @@
         [h_one, routed(h_one, to_other_core), block],
         flops=product_flops,
     )
-    near_two, mix_across, cot_pair = lax.optimization_barrier(
-        (routed(part_two, to_other_rep), routed(mix_one, to_other_loop), cot_pair)
-    )
+    cot_pair = routed(lax.optimization_barrier((cotangent, h_one))[0], to_other_pair)
+    near_two, cot_pair = lax.optimization_barrier((routed(part_two, to_other_rep), cot_pair))
     mix_two, dz_two, dm_two = local_call(
         layer_two_kernel,
         [bf16_array(hidden, half)] * 3,
         [part_two, near_two, two_turned, weight_two, cotangent, cot_pair],
         None,
     )
+    mix_across = routed(lax.optimization_barrier((mix_one, part_two))[0], to_odd_across)
+    dm_swap, mix_across = lax.optimization_barrier((routed(dm_two, to_other_core), mix_across))
     (part_three,) = local_call(
         backward_kernel,
         [bf16_array(hidden, half)],
-        [dm_two, routed(dm_two, to_other_core), block],
+        [dm_two, dm_swap, block],
         flops=product_flops,
     )
-    (grad_two,) = local_call(grad_kernel, [f32_array(hidden, hidden)], [mix_two, dz_two])
+    (grad_two,) = local_call(
+        grad_kernel,
+        [f32_array(hidden, hidden)],
+        [lax.optimization_barrier((mix_two, part_three))[0], dz_two],
+    )
     mix_here, slope_here = local_call(
         slope_kernel,
         [bf16_array(hidden, half), f32_array(hidden, half)],
         [mix_one, lax.optimization_barrier((mix_across, part_three))[0], one_turned],
         None,
     )
+    near_three, across_three, grad_two_swap, mix_swap = lax.optimization_barrier(
+        (
+            routed(part_three, to_column_owner),
+            routed(part_three, to_odd_across),
+            routed(grad_two, to_other_core),
+            routed(mix_here, to_other_core),
+        )
+    )
     (dz_one,) = local_call(
         back_one_kernel,
         [bf16_array(hidden, half)],
-        [
-            part_three,
-            routed(part_three, to_column_owner),
-            routed(part_three, to_other_loop),
-            slope_here,
-        ],
-        None,
+        [part_three, near_three, across_three, slope_here],
     )
     (message,) = local_call(
         message_kernel,
@@ -608,25 +612,23 @@
             weight_one,
             block,
             mix_here,
-            routed(mix_here, to_other_core),
+            mix_swap,
             grad_two,
-            routed(grad_two, to_other_core),
+            grad_two_swap,
         ],
         None,
         flops=product_flops,
+    )
+    (near_sum,) = local_call(
+        near_kernel,
+        [bf16_array(2 * width, nodes)],
+        [message, routed(message, to_column_owner), routed(message, to_odd_across)],
     )
     return tuple(
         local_call(
             functools.partial(last_kernel, scale),
             [f32_array(hidden, hidden), f32_array(hidden, hidden), bf16_array(width, nodes)],
-            [
-                    message,
-                routed(message, to_column_owner),
-                routed(message, to_other_loop),
-                routed(message, to_far_column_owner),
-                routed(message, to_last_column_owner),
-            ],
-            None,
+            [near_sum, routed(near_sum, to_far_rep, True)],
         )
     )
 

time: 58.4 us -> 51.6 us (0.88)
  the two profiles are of different devices: /device:TPU:17 before, /device:TPU:24 now
where the time goes in v3:
time: 51.6 us; the launch traced here: 51.5 us
  waiting for transfers between devices  37.8 us (73%)
  starting transfers between devices  6.74 us (13%)
  Pallas kernels  5.41 us (10%)
  between operations  1.46 us (3%)
    ppermute x20, waiting for transfers between devices, routed(): return lax.ppermute(value, mesh_axes, pairs)  37.8 us
    ppermute x20, starting transfers between devices, routed(): return lax.ppermute(value, mesh_axes, pairs)  6.74 us
    pallas_call x13, Pallas kernels, local_call(): pl.pallas_call(kernel, out_shape=list(outs), in_specs=[pl.BlockSpec(memor...  5.41 us
  transfers between devices with their start and end apart: 20, of which 12 were waited for; matrix products, arithmetic and copies ran while one was open for 0% of the time, Pallas kernels for 4%

profile of v3, /device:TPU:24, one launch (start us, length us, event | category | flops | bytes accessed | tf_op | source)
XLA Modules:
  0.0 51.5 jit_solution(16955798416985065295)
XLA Ops:
  0.6 0.1 collective-permute-start.1
  0.7 0.5 collective-permute-start
  1.2 0.1 collective-permute-start.2
  2.0 1.6 %shard_map.94.block_ref = bf16[1024,1024]{1,0:T(8,128)(2,1)S(1)} custom-call(s32[1]{0:T(128)} %bitcast.1.count_ref, s32[1,1,2,112]{3,2,1,0:T(2,128)} %coords_ref.1, bf16[1,1,112,128,128]{4,3,2,1,0:T(8,128)(2,1)} %tiles_ref.1), custom_call_target="tpu_custom_call" | custom-call | flops 4000000000 | bytes 7865220 | tf_op jit(solution)/shard_map/pallas_call | solution.py:244
  3.6 0.0 copy-start.3
  3.6 0.0 collective-permute-done.1.pair_ref
  3.6 0.5 collective-permute-start.3
  4.1 0.1 collective-permute-start.4
  4.2 0.0 collective-permute-done.2.own_swap_ref
  4.2 0.8 %collective-permute-done.3.across_swap_ref = bf16[32,1024]{1,0:T(8,128)(2,1)S(1)} collective-permute-done((bf16[32,1024]{1,0:T(8,128)(2,1)S(1)}, bf16[32,1024]{1,0:T(8,128)(2,1)S(1)}, u32[]{:S(2)}, u32[]{:S(2)}) %collective-permute-start.3) | collective-permute-done | bytes 65568 | tf_op jit(solution)/shard_map/ppermute | solution.py:192
  5.0 0.4 collective-permute-done.4.pair_swap_ref
  5.4 0.5 shard_map.95.own_ref
  5.8 0.2 collective-permute-start.6
  6.1 0.4 collective-permute-start.5
  6.4 0.1 shard_map.96
  6.5 0.8 %collective-permute-done.6.across_ref = bf16[128,512]{1,0:T(8,128)(2,1)S(1)} collective-permute-done((bf16[128,512]{1,0:T(8,128)(2,1)S(1)}, bf16[128,512]{1,0:T(8,128)(2,1)S(1)}, u32[]{:S(2)}, u32[]{:S(2)}) %collective-permute-start.6) | collective-permute-done | bytes 131104 | tf_op jit(solution)/shard_map/ppermute | solution.py:192
  7.3 0.2 collective-permute-done.5.near_ref
  7.4 0.2 shard_map.97
  7.7 0.4 collective-permute-start.7
  8.1 1.0 %collective-permute-done.7.other_ref = bf16[128,512]{1,0:T(8,128)(2,1)S(1)} collective-permute-done((bf16[128,512]{1,0:T(8,128)(2,1)S(1)}, bf16[128,512]{1,0:T(8,128)(2,1)S(1)}, u32[]{:S(2)}, u32[]{:S(2)}) %collective-permute-start.7) | collective-permute-done | bytes 131104 | tf_op jit(solution)/shard_map/ppermute | solution.py:192
  9.1 0.5 shard_map.98.own_ref
  9.6 0.4 collective-permute-start.8
  10.0 0.2 collective-permute-start.9
  10.1 0.3 collective-permute-start.11
  10.5 0.7 %collective-permute-done.9.cot_pair_ref = bf16[128,256]{1,0:T(8,128)(2,1)S(1)} collective-permute-done((bf16[128,256]{1,0:T(8,128)(2,1)S(1)}, bf16[128,256]{1,0:T(8,128)(2,1)S(1)}, u32[]{:S(2)}, u32[]{:S(2)}) %collective-permute-start.9) | collective-permute-done | bytes 65568 | tf_op jit(solution)/shard_map/ppermute | solution.py:192
  11.2 0.4 shard_map.99
  11.6 0.2 collective-permute-start.10
  11.9 0.0 collective-permute-done.11.across_ref
  11.9 1.2 %collective-permute-done.10.other_ref = bf16[128,512]{1,0:T(8,128)(2,1)S(1)} collective-permute-done((bf16[128,512]{1,0:T(8,128)(2,1)S(1)}, bf16[128,512]{1,0:T(8,128)(2,1)S(1)}, u32[]{:S(2)}, u32[]{:S(2)}) %collective-permute-start.10) | collective-permute-done | bytes 131104 | tf_op jit(solution)/shard_map/ppermute | solution.py:192
  13.0 0.3 shard_map.100.own_ref
  13.4 0.2 shard_map.102
  13.6 0.2 collective-permute-start.15
  13.8 0.3 collective-permute-start.13
  14.2 0.2 collective-permute-start.12
  14.4 0.2 shard_map.101.two_ref
  14.5 0.4 collective-permute-start.14
  14.9 0.9 %collective-permute-done.14.two_swap_ref = f32[128,128]{1,0:T(8,128)S(1)} collective-permute-done((f32[128,128]{1,0:T(8,128)S(1)}, f32[128,128]{1,0:T(8,128)S(1)}, u32[]{:S(2)}, u32[]{:S(2)}) %collective-permute-start.14) | collective-permute-done | bytes 65568 | tf_op jit(solution)/shard_map/ppermute | solution.py:192
  15.9 0.1 shard_map.103.dz_ref
  16.0 0.4 collective-permute-start.16
  16.3 1.0 %collective-permute-done.16.dz_swap_ref = bf16[128,512]{1,0:T(8,128)(2,1)S(1)} collective-permute-done((bf16[128,512]{1,0:T(8,128)(2,1)S(1)}, bf16[128,512]{1,0:T(8,128)(2,1)S(1)}, u32[]{:S(2)}, u32[]{:S(2)}) %collective-permute-start.16) | collective-permute-done | bytes 131104 | tf_op jit(solution)/shard_map/ppermute | solution.py:192
  17.4 0.7 %shard_map.104.own_ref = bf16[64,1024]{1,0:T(8,128)(2,1)S(1)} custom-call(bf16[128,512]{1,0:T(8,128)(2,1)S(1)} %shard_map.103.dz_ref, bf16[128,512]{1,0:T(8,128)(2,1)S(1)} %collective-permute-done.16.dz_swap_ref, bf16[128,128]{1,0:T(8,128)(2,1)S(1)} %copy-done, bf16[1024,1024]{1,0:T(8,128)(2,1)S(1)} %shard_map.94.block_ref, ...), custom_call_target="tpu_custom_call" | custom-call | flops 134217728 | bytes 3047424 | tf_op jit(solution)/shard_map/pallas_call | solution.py:244
  18.0 0.4 collective-permute-start.18
  18.4 0.2 collective-permute-start.17
  18.6 0.8 %collective-permute-done.18.across_ref = bf16[64,1024]{1,0:T(8,128)(2,1)S(1)} collective-permute-done((bf16[64,1024]{1,0:T(8,128)(2,1)S(1)}, bf16[64,1024]{1,0:T(8,128)(2,1)S(1)}, u32[]{:S(2)}, u32[]{:S(2)}) %collective-permute-start.18) | collective-permute-done | bytes 131104 | tf_op jit(solution)/shard_map/ppermute | solution.py:192
  19.4 0.3 collective-permute-done.17.near_ref
  19.8 1.3 %collective-permute-start.19 = (bf16[64,1024]{1,0:T(8,128)(2,1)S(1)}, bf16[64,1024]{1,0:T(8,128)(2,1)S(1)}, u32[]{:S(2)}, u32[]{:S(2)}) collective-permute-start(bf16[64,1024]{1,0:T(8,128)(2,1)S(1)} %shard_map.105.own_ref), channel_id=1, source_target_pairs={{0,8},{1,9},{2,10},{3,11},{4,12},{5,13},{6,14},{7,15},{16,24},{17,... | collective-permute-start | bytes 393224 | tf_op jit(solution)/shard_map/ppermute | solution.py:192
  21.1 29.6 %collective-permute-done.19.far_ref = bf16[64,1024]{1,0:T(8,128)(2,1)S(1)} collective-permute-done((bf16[64,1024]{1,0:T(8,128)(2,1)S(1)}, bf16[64,1024]{1,0:T(8,128)(2,1)S(1)}, u32[]{:S(2)}, u32[]{:S(2)}) %collective-permute-start.19) | collective-permute-done | bytes 131104 | tf_op jit(solution)/shard_map/ppermute | solution.py:192
  50.8 0.7 %shard_map.106 = (f32[128,128]{1,0:T(8,128)}, f32[128,128]{1,0:T(8,128)}, bf16[32,1024]{1,0:T(8,128)(2,1)}) custom-call(bf16[64,1024]{1,0:T(8,128)(2,1)S(1)} %shard_map.105.own_ref, bf16[64,1024]{1,0:T(8,128)(2,1)S(1)} %collective-permute-done.19.far_ref), custom_call_target="tpu_custom_call" | custom-call | bytes 524288 | tf_op jit(solution)/shard_map/pallas_call | solution.py:244
  (13 shorter events, 0.1 us)
Async XLA Ops:
  0.6 2.9 %collective-permute-start.1 = (bf16[32,1024]{1,0:T(8,128)(2,1)}, bf16[32,1024]{1,0:T(8,128)(2,1)S(1)}, u32[]{:S(2)}, u32[]{:S(2)}) collective-permute-start(bf16[32,1024]{1,0:T(8,128)(2,1)} %own_ref.1), channel_id=1, source_target_pairs={{0,2},{1,3},{2,0},{3,1},{4,22},{5,23},{6,20},{7,21},{8,9},{9,8},{1... | collective-permute-start | bytes 196616 | tf_op jit(solution)/shard_map/ppermute | solution.py:192
  0.7 2.9 %collective-permute-start = (bf16[32,1024]{1,0:T(8,128)(2,1)}, bf16[32,1024]{1,0:T(8,128)(2,1)S(1)}, u32[]{:S(2)}, u32[]{:S(2)}) collective-permute-start(bf16[32,1024]{1,0:T(8,128)(2,1)} %own_ref.1), channel_id=1, source_target_pairs={{0,16},{1,17},{2,18},{3,19},{4,20},{5,21},{6,22},{7,23},{8,9},{9,8... | collective-permute-start | bytes 196616 | tf_op jit(solution)/shard_map/ppermute | solution.py:192
  1.2 3.0 %collective-permute-start.2 = (bf16[32,1024]{1,0:T(8,128)(2,1)}, bf16[32,1024]{1,0:T(8,128)(2,1)S(1)}, u32[]{:S(2)}, u32[]{:S(2)}) collective-permute-start(bf16[32,1024]{1,0:T(8,128)(2,1)} %own_ref.1), channel_id=1, source_target_pairs={{0,1},{1,0},{2,3},{3,2},{4,5},{5,4},{6,7},{7,6},{8,9},{9,8},{10,11... | collective-permute-start | bytes 196616 | tf_op jit(solution)/shard_map/ppermute | solution.py:192
  1.9 3.4 %copy-start.2 = (bf16[32,1024]{1,0:T(8,128)(2,1)S(1)}, bf16[32,1024]{1,0:T(8,128)(2,1)}, u32[]{:S(2)}) copy-start(bf16[32,1024]{1,0:T(8,128)(2,1)} %own_ref.1) | copy-start | bytes 196612
  1.9 4.5 %copy-start = (bf16[128,128]{1,0:T(8,128)(2,1)S(1)}, bf16[128,128]{1,0:T(8,128)(2,1)}, u32[]{:S(2)}) copy-start(bf16[128,128]{1,0:T(8,128)(2,1)} %weight_ref.3) | copy-start | bytes 98308
  2.0 4.5 %copy-start.1 = (bf16[128,128]{1,0:T(8,128)(2,1)S(1)}, bf16[128,128]{1,0:T(8,128)(2,1)}, u32[]{:S(2)}) copy-start(bf16[128,128]{1,0:T(8,128)(2,1)} %weight_ref.2) | copy-start | bytes 98308
  3.6 6.4 %copy-start.3 = (bf16[128,256]{1,0:T(8,128)(2,1)S(1)}, bf16[128,256]{1,0:T(8,128)(2,1)}, u32[]{:S(2)}) copy-start(bf16[128,256]{1,0:T(8,128)(2,1)} %cot_ref.1) | copy-start | bytes 196612
  3.6 1.4 %collective-permute-start.3 = (bf16[32,1024]{1,0:T(8,128)(2,1)S(1)}, bf16[32,1024]{1,0:T(8,128)(2,1)S(1)}, u32[]{:S(2)}, u32[]{:S(2)}) collective-permute-start(bf16[32,1024]{1,0:T(8,128)(2,1)S(1)} %collective-permute-done.across_ref), channel_id=1, source_target_pairs={{0,1},{1,0},{2,3},{3,2},{4,5},{5,4},{6,7},{7,6},{8,9},{9,8},{10,11... | collective-permute-start | bytes 196616 | tf_op jit(solution)/shard_map/ppermute | solution.py:192
  4.1 1.3 %collective-permute-start.4 = (bf16[32,1024]{1,0:T(8,128)(2,1)S(1)}, bf16[32,1024]{1,0:T(8,128)(2,1)S(1)}, u32[]{:S(2)}, u32[]{:S(2)}) collective-permute-start(bf16[32,1024]{1,0:T(8,128)(2,1)S(1)} %collective-permute-done.1.pair_ref), channel_id=1, source_target_pairs={{0,1},{1,0},{2,3},{3,2},{4,5},{5,4},{6,7},{7,6},{8,9},{9,8},{10,11... | collective-permute-start | bytes 196616 | tf_op jit(solution)/shard_map/ppermute | solution.py:192
  5.8 1.4 %collective-permute-start.6 = (bf16[128,512]{1,0:T(8,128)(2,1)S(1)}, bf16[128,512]{1,0:T(8,128)(2,1)S(1)}, u32[]{:S(2)}, u32[]{:S(2)}) collective-permute-start(bf16[128,512]{1,0:T(8,128)(2,1)S(1)} %shard_map.95.own_ref), channel_id=1, source_target_pairs={{0,1},{1,0},{2,3},{3,2},{4,20},{5,21},{6,22},{7,23},{8,9},{9,8},{1... | collective-permute-start | bytes 393224 | tf_op jit(solution)/shard_map/ppermute | solution.py:192
  6.1 1.4 %collective-permute-start.5 = (bf16[128,512]{1,0:T(8,128)(2,1)S(1)}, bf16[128,512]{1,0:T(8,128)(2,1)S(1)}, u32[]{:S(2)}, u32[]{:S(2)}) collective-permute-start(bf16[128,512]{1,0:T(8,128)(2,1)S(1)} %shard_map.95.own_ref), channel_id=1, source_target_pairs={{0,20},{1,21},{2,22},{3,23},{4,0},{5,1},{6,2},{7,3},{8,9},{9,8},{1... | collective-permute-start | bytes 393224 | tf_op jit(solution)/shard_map/ppermute | solution.py:192
  7.7 1.4 %collective-permute-start.7 = (bf16[128,512]{1,0:T(8,128)(2,1)S(1)}, bf16[128,512]{1,0:T(8,128)(2,1)S(1)}, u32[]{:S(2)}, u32[]{:S(2)}) collective-permute-start(bf16[128,512]{1,0:T(8,128)(2,1)S(1)} %get-tuple-element.33.own_ref), channel_id=1, source_target_pairs={{0,1},{1,0},{2,3},{3,2},{4,5},{5,4},{6,7},{7,6},{8,9},{9,8},{10,11... | collective-permute-start | bytes 393224 | tf_op jit(solution)/shard_map/ppermute | solution.py:192
  9.6 1.7 %collective-permute-start.8 = (bf16[128,512]{1,0:T(8,128)(2,1)S(1)}, bf16[128,512]{1,0:T(8,128)(2,1)S(1)}, u32[]{:S(2)}, u32[]{:S(2)}) collective-permute-start(bf16[128,512]{1,0:T(8,128)(2,1)S(1)} %shard_map.98.own_ref), channel_id=1, source_target_pairs={{0,4},{1,5},{2,6},{3,7},{4,0},{5,1},{6,2},{7,3},{8,9},{9,8},{10,11... | collective-permute-start | bytes 393224 | tf_op jit(solution)/shard_map/ppermute | solution.py:192
  10.0 1.3 %collective-permute-start.9 = (bf16[128,256]{1,0:T(8,128)(2,1)S(1)}, bf16[128,256]{1,0:T(8,128)(2,1)S(1)}, u32[]{:S(2)}, u32[]{:S(2)}) collective-permute-start(bf16[128,256]{1,0:T(8,128)(2,1)S(1)} %copy-done.3), channel_id=1, source_target_pairs={{0,2},{1,3},{2,0},{3,1},{4,6},{5,7},{6,4},{7,5},{8,9},{9,8},{10,11... | collective-permute-start | bytes 196616 | tf_op jit(solution)/shard_map/ppermute | solution.py:192
  10.1 1.7 %collective-permute-start.11 = (bf16[128,512]{1,0:T(8,128)(2,1)S(1)}, bf16[128,512]{1,0:T(8,128)(2,1)S(1)}, u32[]{:S(2)}, u32[]{:S(2)}) collective-permute-start(bf16[128,512]{1,0:T(8,128)(2,1)S(1)} %get-tuple-element.40.mix_ref), channel_id=1, source_target_pairs={{0,1},{1,0},{2,3},{3,2},{4,20},{5,21},{6,22},{7,23},{8,9},{9,8},{1... | collective-permute-start | bytes 393224 | tf_op jit(solution)/shard_map/ppermute | solution.py:192
  11.6 1.4 %collective-permute-start.10 = (bf16[128,512]{1,0:T(8,128)(2,1)S(1)}, bf16[128,512]{1,0:T(8,128)(2,1)S(1)}, u32[]{:S(2)}, u32[]{:S(2)}) collective-permute-start(bf16[128,512]{1,0:T(8,128)(2,1)S(1)} %get-tuple-element.38.own_ref), channel_id=1, source_target_pairs={{0,1},{1,0},{2,3},{3,2},{4,5},{5,4},{6,7},{7,6},{8,9},{9,8},{10,11... | collective-permute-start | bytes 393224 | tf_op jit(solution)/shard_map/ppermute | solution.py:192
  13.6 2.3 %collective-permute-start.15 = (bf16[128,512]{1,0:T(8,128)(2,1)S(1)}, bf16[128,512]{1,0:T(8,128)(2,1)S(1)}, u32[]{:S(2)}, u32[]{:S(2)}) collective-permute-start(bf16[128,512]{1,0:T(8,128)(2,1)S(1)} %get-tuple-element.47.mix_ref), channel_id=1, source_target_pairs={{0,1},{1,0},{2,3},{3,2},{4,5},{5,4},{6,7},{7,6},{8,9},{9,8},{10,11... | collective-permute-start | bytes 393224 | tf_op jit(solution)/shard_map/ppermute | solution.py:192
  13.8 2.0 %collective-permute-start.13 = (bf16[128,512]{1,0:T(8,128)(2,1)S(1)}, bf16[128,512]{1,0:T(8,128)(2,1)S(1)}, u32[]{:S(2)}, u32[]{:S(2)}) collective-permute-start(bf16[128,512]{1,0:T(8,128)(2,1)S(1)} %shard_map.100.own_ref), channel_id=1, source_target_pairs={{0,1},{1,0},{2,3},{3,2},{4,20},{5,21},{6,22},{7,23},{8,9},{9,8},{1... | collective-permute-start | bytes 393224 | tf_op jit(solution)/shard_map/ppermute | solution.py:192
  14.2 1.7 %collective-permute-start.12 = (bf16[128,512]{1,0:T(8,128)(2,1)S(1)}, bf16[128,512]{1,0:T(8,128)(2,1)S(1)}, u32[]{:S(2)}, u32[]{:S(2)}) collective-permute-start(bf16[128,512]{1,0:T(8,128)(2,1)S(1)} %shard_map.100.own_ref), channel_id=1, source_target_pairs={{0,4},{1,5},{2,6},{3,7},{4,16},{5,17},{6,18},{7,19},{8,9},{9,8},{1... | collective-permute-start | bytes 393224 | tf_op jit(solution)/shard_map/ppermute | solution.py:192
  14.5 1.3 %collective-permute-start.14 = (f32[128,128]{1,0:T(8,128)S(1)}, f32[128,128]{1,0:T(8,128)S(1)}, u32[]{:S(2)}, u32[]{:S(2)}) collective-permute-start(f32[128,128]{1,0:T(8,128)S(1)} %shard_map.101.two_ref), channel_id=1, source_target_pairs={{0,1},{1,0},{2,3},{3,2},{4,5},{5,4},{6,7},{7,6},{8,9},{9,8},{10,11... | collective-permute-start | bytes 196616 | tf_op jit(solution)/shard_map/ppermute | solution.py:192
  16.0 1.4 %collective-permute-start.16 = (bf16[128,512]{1,0:T(8,128)(2,1)S(1)}, bf16[128,512]{1,0:T(8,128)(2,1)S(1)}, u32[]{:S(2)}, u32[]{:S(2)}) collective-permute-start(bf16[128,512]{1,0:T(8,128)(2,1)S(1)} %shard_map.103.dz_ref), channel_id=1, source_target_pairs={{0,1},{1,0},{2,3},{3,2},{4,5},{5,4},{6,7},{7,6},{8,9},{9,8},{10,11... | collective-permute-start | bytes 393224 | tf_op jit(solution)/shard_map/ppermute | solution.py:192
  18.0 1.4 %collective-permute-start.18 = (bf16[64,1024]{1,0:T(8,128)(2,1)S(1)}, bf16[64,1024]{1,0:T(8,128)(2,1)S(1)}, u32[]{:S(2)}, u32[]{:S(2)}) collective-permute-start(bf16[64,1024]{1,0:T(8,128)(2,1)S(1)} %shard_map.104.own_ref), channel_id=1, source_target_pairs={{0,1},{1,0},{2,3},{3,2},{4,20},{5,21},{6,22},{7,23},{8,9},{9,8},{1... | collective-permute-start | bytes 393224 | tf_op jit(solution)/shard_map/ppermute | solution.py:192
  18.4 1.3 %collective-permute-start.17 = (bf16[64,1024]{1,0:T(8,128)(2,1)S(1)}, bf16[64,1024]{1,0:T(8,128)(2,1)S(1)}, u32[]{:S(2)}, u32[]{:S(2)}) collective-permute-start(bf16[64,1024]{1,0:T(8,128)(2,1)S(1)} %shard_map.104.own_ref), channel_id=1, source_target_pairs={{0,4},{1,5},{2,6},{3,7},{4,16},{5,17},{6,18},{7,19},{8,9},{9,8},{1... | collective-permute-start | bytes 393224 | tf_op jit(solution)/shard_map/ppermute | solution.py:192
  19.8 30.9 %collective-permute-start.19 = (bf16[64,1024]{1,0:T(8,128)(2,1)S(1)}, bf16[64,1024]{1,0:T(8,128)(2,1)S(1)}, u32[]{:S(2)}, u32[]{:S(2)}) collective-permute-start(bf16[64,1024]{1,0:T(8,128)(2,1)S(1)} %shard_map.105.own_ref), channel_id=1, source_target_pairs={{0,8},{1,9},{2,10},{3,11},{4,12},{5,13},{6,14},{7,15},{16,24},{17,... | collective-permute-start | bytes 393224 | tf_op jit(solution)/shard_map/ppermute | solution.py:192

commit v4 on v3

--- a/solution.py
+++ b/solution.py
@@ -275,6 +275,7 @@
     coords_ref,
     tiles_ref,
     block_ref,
+    starts,
     coords,
     held,
     list_sem,
@@ -297,10 +298,14 @@
     lists.wait()
     count = count_ref[0]
 
+    for panel in range(panels):
+        part, rest = divmod(panel, quarter)
+        first = ((part % 2) * 2 + part // 2) * quarter + rest
+        second = ((1 - part % 2) * 2 + part // 2) * quarter + rest
+        starts[panel] = jnp.where(core == 0, first, second) * side
+
     def start_of(panel):
-        part = panel // quarter
-        half = jnp.bitwise_xor(part % 2, core)
-        return pl.multiple_of(((half * 2 + part // 2) * quarter + panel % quarter) * side, side)
+        return pl.multiple_of(starts[panel], side)
 
     def place(slot, carry):
         rows = pl.ds(start_of(coords[0, 0, 0, slot]), side)
@@ -308,7 +313,7 @@
         block_ref[rows, columns] = held[slot]
         return carry
 
-    group = 4
+    group = 8
 
     def place_group(index, carry):
         for offset in range(group):
@@ -363,17 +368,25 @@
     out_ref[...] = dot_nt(full[...], block_ref[:half, :]).astype(out_ref.dtype)
 
 
-def forward_kernel(own_ref, other_ref, block_ref, out_ref):
+def forward_own_kernel(own_ref, block_ref, total_ref):
     half = own_ref.shape[1]
-    total = dot_nt(own_ref[...], block_ref[:half, :half])
-    total += dot_nt(other_ref[...], block_ref[:half, half:])
+    total_ref[...] = dot_nt(own_ref[...], block_ref[:half, :half])
+
+
+def forward_other_kernel(total_ref, other_ref, block_ref, out_ref):
+    half = other_ref.shape[1]
+    total = total_ref[...] + dot_nt(other_ref[...], block_ref[:half, half:])
     out_ref[...] = total.astype(out_ref.dtype)
 
 
-def backward_kernel(own_ref, other_ref, block_ref, out_ref):
+def backward_own_kernel(own_ref, block_ref, total_ref):
     half = own_ref.shape[1]
-    total = dot_nn(own_ref[...], block_ref[:half, :half])
-    total += dot_nn(other_ref[...], block_ref[half:, :half])
+    total_ref[...] = dot_nn(own_ref[...], block_ref[:half, :half])
+
+
+def backward_other_kernel(total_ref, other_ref, block_ref, out_ref):
+    half = other_ref.shape[1]
+    total = total_ref[...] + dot_nn(other_ref[...], block_ref[half:, :half])
     out_ref[...] = total.astype(out_ref.dtype)
 
 
@@ -435,31 +448,39 @@
     dz_ref[...] = (dh.astype(jnp.float32) * slope_ref[...]).astype(dz_ref.dtype)
 
 
+def feature_rows(weight_ref, width):
+    first = pl.multiple_of(lax.axis_index("feat") * width, width)
+    return weight_ref[pl.ds(first, width), :]
+
+
+def last_own_kernel(dz_ref, weight_ref, block_ref, mix_ref, total_ref, grad_ref):
+    half = dz_ref.shape[1]
+    own = dot_nn(feature_rows(weight_ref, total_ref.shape[0]), dz_ref[...]).astype(jnp.bfloat16)
+    total_ref[...] = dot_nn(own, block_ref[:half, :])
+    grad_ref[...] = dot_nt(mix_ref[...], dz_ref[...])
+
+
 def message_kernel(
-    dz_ref,
+    total_ref,
+    grad_ref,
     dz_swap_ref,
     weight_ref,
     block_ref,
-    mix_ref,
     mix_swap_ref,
     two_ref,
     two_swap_ref,
     out_ref,
 ):
-    feat = lax.axis_index("feat")
-    width = out_ref.shape[0] // 2
+    width = total_ref.shape[0]
     hidden = weight_ref.shape[0]
-    half = dz_ref.shape[1]
-    mix, mix_swap, dz, dz_swap = mix_ref[...], mix_swap_ref[...], dz_ref[...], dz_swap_ref[...]
-    rows = weight_ref[pl.ds(pl.multiple_of(feat * width, width), width), :]
-    own = dot_nn(rows, dz).astype(jnp.bfloat16)
-    other = dot_nn(rows, dz_swap).astype(jnp.bfloat16)
-    total = dot_nn(own, block_ref[:half, :]) + dot_nn(other, block_ref[half:, :])
+    half = dz_swap_ref.shape[1]
+    dz_swap = dz_swap_ref[...]
+    other = dot_nn(feature_rows(weight_ref, width), dz_swap).astype(jnp.bfloat16)
+    total = total_ref[...] + dot_nn(other, block_ref[half:, :])
     out_ref[:width, :] = total.astype(out_ref.dtype)
-    swap = feat % 2 == 1
-    one = dot_nt(jnp.where(swap, mix_swap, mix), jnp.where(swap, dz_swap, dz)) + dot_nt(
-        jnp.where(swap, mix, mix_swap), jnp.where(swap, dz, dz_swap)
-    )
+    second = lax.axis_index("feat") % 2 == 1
+    grad, grad_swap = grad_ref[...], dot_nt(mix_swap_ref[...], dz_swap)
+    one = jnp.where(second, grad_swap, grad) + jnp.where(second, grad, grad_swap)
     two = two_ref[...] + two_swap_ref[...]
     count = hidden // width
     for index, grad in enumerate((one, two)):
@@ -507,7 +528,7 @@
     scale = 1.0 / math.sqrt(nodes * lax.axis_size("loop"))
     product_flops = 2 * hidden * nodes * half
 
-    across = routed(features, to_other_loop)
+    across = routed(features, to_odd_across)
     pair = routed(features, to_feature_pair)
     own_swap = routed(features, to_other_core)
     (block,) = local_call(
@@ -520,6 +541,7 @@
         ],
         [pltpu.SMEM, pltpu.HBM, pltpu.HBM],
         [
+            pltpu.SMEM((panels,), jnp.int32),
             pltpu.SMEM(tile_coords.shape, jnp.int32),
             pltpu.VMEM((panels * panels, side, side), jnp.bfloat16),
             pltpu.SemaphoreType.DMA,
@@ -557,11 +579,15 @@
         [part_one, near_one, across_one, one_turned],
         None,
     )
+    h_swap = routed(h_one, to_other_core)
+    (total_two,) = local_call(
+        forward_own_kernel, [f32_array(hidden, half)], [h_one, block], flops=product_flops // 2
+    )
     (part_two,) = local_call(
-        forward_kernel,
+        forward_other_kernel,
         [bf16_array(hidden, half)],
-        [h_one, routed(h_one, to_other_core), block],
-        flops=product_flops,
+        [total_two, h_swap, block],
+        flops=product_flops // 2,
     )
     cot_pair = routed(lax.optimization_barrier((cotangent, h_one))[0], to_other_pair)
     near_two, cot_pair = lax.optimization_barrier((routed(part_two, to_other_rep), cot_pair))
@@ -572,23 +598,27 @@
         None,
     )
     mix_across = routed(lax.optimization_barrier((mix_one, part_two))[0], to_odd_across)
-    dm_swap, mix_across = lax.optimization_barrier((routed(dm_two, to_other_core), mix_across))
+    mix_here, slope_here = local_call(
+        slope_kernel,
+        [bf16_array(hidden, half), f32_array(hidden, half)],
+        [mix_one, lax.optimization_barrier((mix_across, dm_two))[0], one_turned],
+    )
+    (total_three,) = local_call(
+        backward_own_kernel, [f32_array(hidden, half)], [dm_two, block], flops=product_flops // 2
+    )
+    dm_swap, slope_here, total_three = lax.optimization_barrier(
+        (routed(dm_two, to_other_core), slope_here, total_three)
+    )
     (part_three,) = local_call(
-        backward_kernel,
+        backward_other_kernel,
         [bf16_array(hidden, half)],
-        [dm_two, dm_swap, block],
-        flops=product_flops,
+        [total_three, dm_swap, block],
+        flops=product_flops // 2,
     )
     (grad_two,) = local_call(
         grad_kernel,
         [f32_array(hidden, hidden)],
         [lax.optimization_barrier((mix_two, part_three))[0], dz_two],
-    )
-    mix_here, slope_here = local_call(
-        slope_kernel,
-        [bf16_array(hidden, half), f32_array(hidden, half)],
-        [mix_one, lax.optimization_barrier((mix_across, part_three))[0], one_turned],
-        None,
     )
     near_three, across_three, grad_two_swap, mix_swap = lax.optimization_barrier(
         (
@@ -603,21 +633,28 @@
         [bf16_array(hidden, half)],
         [part_three, near_three, across_three, slope_here],
     )
+    dz_swap = routed(dz_one, to_other_core)
+    total_four, grad_one = local_call(
+        last_own_kernel,
+        [f32_array(width, nodes), f32_array(hidden, hidden)],
+        [dz_one, weight_one, block, mix_here],
+        flops=product_flops // 2,
+    )
+    dz_swap, total_four = lax.optimization_barrier((dz_swap, total_four))
     (message,) = local_call(
         message_kernel,
         [bf16_array(2 * width, nodes)],
         [
-            dz_one,
-            routed(dz_one, to_other_core),
+            total_four,
+            grad_one,
+            dz_swap,
             weight_one,
             block,
-            mix_here,
             mix_swap,
             grad_two,
             grad_two_swap,
         ],
-        None,
-        flops=product_flops,
+        flops=product_flops // 2,
     )
     (near_sum,) = local_call(
         near_kernel,

time: 51.6 us -> 50.8 us (0.984)
  waiting for transfers between devices: 37.8 us -> 36.7 us
    ppermute x20, waiting for transfers between devices: 37.8 us -> 36.7 us  [routed(): return lax.ppermute(value, mesh_axes, pairs)]
    pallas_call x13 -> x16, Pallas kernels: 5.41 us -> 5.89 us  [local_call(): pl.pallas_call(kernel, out_shape=list(outs), in_specs=[pl.BlockSpec(memor...]
  transfers between devices with their start and end apart: 20 -> 20, of which waited for: 12 -> 12; matrix products, arithmetic and copies ran while one was open for 0% -> 0% of each run, Pallas kernels for 4% -> 7%
where the time goes in v4:
time: 50.8 us; the launch traced here: 50.7 us
  waiting for transfers between devices  36.7 us (72%)
  starting transfers between devices  6.61 us (13%)
  Pallas kernels  5.89 us (12%)
  between operations  1.47 us (3%)
    ppermute x20, waiting for transfers between devices, routed(): return lax.ppermute(value, mesh_axes, pairs)  36.7 us
    ppermute x20, starting transfers between devices, routed(): return lax.ppermute(value, mesh_axes, pairs)  6.61 us
    pallas_call x16, Pallas kernels, local_call(): pl.pallas_call(kernel, out_shape=list(outs), in_specs=[pl.BlockSpec(memor...  5.89 us
  transfers between devices with their start and end apart: 20, of which 12 were waited for; matrix products, arithmetic and copies ran while one was open for 0% of the time, Pallas kernels for 7%

profile of v4, /device:TPU:24, one launch (start us, length us, event | category | flops | bytes accessed | tf_op | source)
XLA Modules:
  0.0 50.7 jit_solution(1515488015091814017)
XLA Ops:
  0.6 0.1 collective-permute-start
  0.7 0.5 collective-permute-start.1
  1.2 0.1 collective-permute-start.2
  2.0 1.6 %shard_map.94.block_ref = bf16[1024,1024]{1,0:T(8,128)(2,1)S(1)} custom-call(s32[1]{0:T(128)} %bitcast.1.count_ref, s32[1,1,2,112]{3,2,1,0:T(2,128)} %coords_ref.1, bf16[1,1,112,128,128]{4,3,2,1,0:T(8,128)(2,1)} %tiles_ref.1), custom_call_target="tpu_custom_call" | custom-call | flops 4000000000 | bytes 7865220 | tf_op jit(solution)/shard_map/pallas_call | solution.py:244
  3.6 0.0 copy-start.3
  3.6 0.5 collective-permute-start.3
  4.1 0.1 collective-permute-start.4
  4.2 0.8 %collective-permute-done.3.across_swap_ref = bf16[32,1024]{1,0:T(8,128)(2,1)S(1)} collective-permute-done((bf16[32,1024]{1,0:T(8,128)(2,1)S(1)}, bf16[32,1024]{1,0:T(8,128)(2,1)S(1)}, u32[]{:S(2)}, u32[]{:S(2)}) %collective-permute-start.3) | collective-permute-done | bytes 65568 | tf_op jit(solution)/shard_map/ppermute | solution.py:192
  5.0 0.4 collective-permute-done.4.pair_swap_ref
  5.4 0.5 shard_map.95.own_ref
  5.8 0.2 collective-permute-start.5
  6.0 0.4 collective-permute-start.6
  6.4 0.1 shard_map.96
  6.5 0.8 %collective-permute-done.5.near_ref = bf16[128,512]{1,0:T(8,128)(2,1)S(1)} collective-permute-done((bf16[128,512]{1,0:T(8,128)(2,1)S(1)}, bf16[128,512]{1,0:T(8,128)(2,1)S(1)}, u32[]{:S(2)}, u32[]{:S(2)}) %collective-permute-start.5) | collective-permute-done | bytes 131104 | tf_op jit(solution)/shard_map/ppermute | solution.py:192
  7.2 0.2 collective-permute-done.6.across_ref
  7.4 0.2 shard_map.97
  7.6 0.4 collective-permute-start.7
  8.0 0.3 shard_map.98.total_ref
  8.3 0.7 %collective-permute-done.7.other_ref = bf16[128,512]{1,0:T(8,128)(2,1)S(1)} collective-permute-done((bf16[128,512]{1,0:T(8,128)(2,1)S(1)}, bf16[128,512]{1,0:T(8,128)(2,1)S(1)}, u32[]{:S(2)}, u32[]{:S(2)}) %collective-permute-start.7) | collective-permute-done | bytes 131104 | tf_op jit(solution)/shard_map/ppermute | solution.py:192
  9.1 0.3 shard_map.99.own_ref
  9.4 0.4 collective-permute-start.8
  9.8 0.2 collective-permute-start.9
  9.9 0.3 collective-permute-start.11
  10.3 0.7 %collective-permute-done.9.cot_pair_ref = bf16[128,256]{1,0:T(8,128)(2,1)S(1)} collective-permute-done((bf16[128,256]{1,0:T(8,128)(2,1)S(1)}, bf16[128,256]{1,0:T(8,128)(2,1)S(1)}, u32[]{:S(2)}, u32[]{:S(2)}) %collective-permute-start.9) | collective-permute-done | bytes 65568 | tf_op jit(solution)/shard_map/ppermute | solution.py:192
  11.0 0.4 shard_map.100
  11.4 0.2 collective-permute-start.10
  11.7 0.2 shard_map.101
  11.9 0.4 collective-permute-start.15
  12.3 0.2 shard_map.102.total_ref
  12.5 0.3 collective-permute-done.10.other_ref
  12.8 0.2 shard_map.103.own_ref
  13.1 0.2 collective-permute-start.12
  13.3 0.3 collective-permute-start.13
  13.6 0.2 shard_map.104.two_ref
  13.8 0.3 collective-permute-start.14
  14.1 1.1 %collective-permute-done.14.two_swap_ref = f32[128,128]{1,0:T(8,128)S(1)} collective-permute-done((f32[128,128]{1,0:T(8,128)S(1)}, f32[128,128]{1,0:T(8,128)S(1)}, u32[]{:S(2)}, u32[]{:S(2)}) %collective-permute-start.14) | collective-permute-done | bytes 65568 | tf_op jit(solution)/shard_map/ppermute | solution.py:192
  15.1 0.1 shard_map.105.dz_ref
  15.2 0.3 collective-permute-start.16
  15.5 0.4 shard_map.106
  15.9 0.7 %collective-permute-done.16.dz_swap_ref = bf16[128,512]{1,0:T(8,128)(2,1)S(1)} collective-permute-done((bf16[128,512]{1,0:T(8,128)(2,1)S(1)}, bf16[128,512]{1,0:T(8,128)(2,1)S(1)}, u32[]{:S(2)}, u32[]{:S(2)}) %collective-permute-start.16) | collective-permute-done | bytes 131104 | tf_op jit(solution)/shard_map/ppermute | solution.py:192
  16.6 0.4 shard_map.107.own_ref
  17.1 0.2 collective-permute-start.17
  17.3 0.3 collective-permute-start.18
  17.6 0.8 %collective-permute-done.17.near_ref = bf16[64,1024]{1,0:T(8,128)(2,1)S(1)} collective-permute-done((bf16[64,1024]{1,0:T(8,128)(2,1)S(1)}, bf16[64,1024]{1,0:T(8,128)(2,1)S(1)}, u32[]{:S(2)}, u32[]{:S(2)}) %collective-permute-start.17) | collective-permute-done | bytes 131104 | tf_op jit(solution)/shard_map/ppermute | solution.py:192
  18.5 0.2 collective-permute-done.18.across_ref
  18.7 1.3 %collective-permute-start.19 = (bf16[64,1024]{1,0:T(8,128)(2,1)S(1)}, bf16[64,1024]{1,0:T(8,128)(2,1)S(1)}, u32[]{:S(2)}, u32[]{:S(2)}) collective-permute-start(bf16[64,1024]{1,0:T(8,128)(2,1)S(1)} %shard_map.108.own_ref), channel_id=1, source_target_pairs={{0,8},{1,9},{2,10},{3,11},{4,12},{5,13},{6,14},{7,15},{16,24},{17,... | collective-permute-start | bytes 393224 | tf_op jit(solution)/shard_map/ppermute | solution.py:192
  20.0 30.0 %collective-permute-done.19.far_ref = bf16[64,1024]{1,0:T(8,128)(2,1)S(1)} collective-permute-done((bf16[64,1024]{1,0:T(8,128)(2,1)S(1)}, bf16[64,1024]{1,0:T(8,128)(2,1)S(1)}, u32[]{:S(2)}, u32[]{:S(2)}) %collective-permute-start.19) | collective-permute-done | bytes 131104 | tf_op jit(solution)/shard_map/ppermute | solution.py:192
  50.0 0.7 %shard_map.109 = (f32[128,128]{1,0:T(8,128)}, f32[128,128]{1,0:T(8,128)}, bf16[32,1024]{1,0:T(8,128)(2,1)}) custom-call(bf16[64,1024]{1,0:T(8,128)(2,1)S(1)} %shard_map.108.own_ref, bf16[64,1024]{1,0:T(8,128)(2,1)S(1)} %collective-permute-done.19.far_ref), custom_call_target="tpu_custom_call" | custom-call | bytes 524288 | tf_op jit(solution)/shard_map/pallas_call | solution.py:244
  (16 shorter events, 0.1 us)
Async XLA Ops:
  0.6 2.9 %collective-permute-start = (bf16[32,1024]{1,0:T(8,128)(2,1)}, bf16[32,1024]{1,0:T(8,128)(2,1)S(1)}, u32[]{:S(2)}, u32[]{:S(2)}) collective-permute-start(bf16[32,1024]{1,0:T(8,128)(2,1)} %own_ref.1), channel_id=1, source_target_pairs={{0,1},{1,0},{2,3},{3,2},{4,20},{5,21},{6,22},{7,23},{8,9},{9,8},{1... | collective-permute-start | bytes 196616 | tf_op jit(solution)/shard_map/ppermute | solution.py:192
  0.7 2.9 %collective-permute-start.1 = (bf16[32,1024]{1,0:T(8,128)(2,1)}, bf16[32,1024]{1,0:T(8,128)(2,1)S(1)}, u32[]{:S(2)}, u32[]{:S(2)}) collective-permute-start(bf16[32,1024]{1,0:T(8,128)(2,1)} %own_ref.1), channel_id=1, source_target_pairs={{0,2},{1,3},{2,0},{3,1},{4,22},{5,23},{6,20},{7,21},{8,9},{9,8},{1... | collective-permute-start | bytes 196616 | tf_op jit(solution)/shard_map/ppermute | solution.py:192
  1.2 3.0 %collective-permute-start.2 = (bf16[32,1024]{1,0:T(8,128)(2,1)}, bf16[32,1024]{1,0:T(8,128)(2,1)S(1)}, u32[]{:S(2)}, u32[]{:S(2)}) collective-permute-start(bf16[32,1024]{1,0:T(8,128)(2,1)} %own_ref.1), channel_id=1, source_target_pairs={{0,1},{1,0},{2,3},{3,2},{4,5},{5,4},{6,7},{7,6},{8,9},{9,8},{10,11... | collective-permute-start | bytes 196616 | tf_op jit(solution)/shard_map/ppermute | solution.py:192
  1.9 3.4 %copy-start.2 = (bf16[32,1024]{1,0:T(8,128)(2,1)S(1)}, bf16[32,1024]{1,0:T(8,128)(2,1)}, u32[]{:S(2)}) copy-start(bf16[32,1024]{1,0:T(8,128)(2,1)} %own_ref.1) | copy-start | bytes 196612
  1.9 4.5 %copy-start = (bf16[128,128]{1,0:T(8,128)(2,1)S(1)}, bf16[128,128]{1,0:T(8,128)(2,1)}, u32[]{:S(2)}) copy-start(bf16[128,128]{1,0:T(8,128)(2,1)} %weight_ref.5) | copy-start | bytes 98308
  2.0 4.4 %copy-start.1 = (bf16[128,128]{1,0:T(8,128)(2,1)S(1)}, bf16[128,128]{1,0:T(8,128)(2,1)}, u32[]{:S(2)}) copy-start(bf16[128,128]{1,0:T(8,128)(2,1)} %weight_ref.3) | copy-start | bytes 98308
  3.6 6.2 %copy-start.3 = (bf16[128,256]{1,0:T(8,128)(2,1)S(1)}, bf16[128,256]{1,0:T(8,128)(2,1)}, u32[]{:S(2)}) copy-start(bf16[128,256]{1,0:T(8,128)(2,1)} %cot_ref.1) | copy-start | bytes 196612
  3.6 1.4 %collective-permute-start.3 = (bf16[32,1024]{1,0:T(8,128)(2,1)S(1)}, bf16[32,1024]{1,0:T(8,128)(2,1)S(1)}, u32[]{:S(2)}, u32[]{:S(2)}) collective-permute-start(bf16[32,1024]{1,0:T(8,128)(2,1)S(1)} %collective-permute-done.across_ref), channel_id=1, source_target_pairs={{0,1},{1,0},{2,3},{3,2},{4,5},{5,4},{6,7},{7,6},{8,9},{9,8},{10,11... | collective-permute-start | bytes 196616 | tf_op jit(solution)/shard_map/ppermute | solution.py:192
  4.1 1.3 %collective-permute-start.4 = (bf16[32,1024]{1,0:T(8,128)(2,1)S(1)}, bf16[32,1024]{1,0:T(8,128)(2,1)S(1)}, u32[]{:S(2)}, u32[]{:S(2)}) collective-permute-start(bf16[32,1024]{1,0:T(8,128)(2,1)S(1)} %collective-permute-done.1.pair_ref), channel_id=1, source_target_pairs={{0,1},{1,0},{2,3},{3,2},{4,5},{5,4},{6,7},{7,6},{8,9},{9,8},{10,11... | collective-permute-start | bytes 196616 | tf_op jit(solution)/shard_map/ppermute | solution.py:192
  5.8 1.4 %collective-permute-start.5 = (bf16[128,512]{1,0:T(8,128)(2,1)S(1)}, bf16[128,512]{1,0:T(8,128)(2,1)S(1)}, u32[]{:S(2)}, u32[]{:S(2)}) collective-permute-start(bf16[128,512]{1,0:T(8,128)(2,1)S(1)} %shard_map.95.own_ref), channel_id=1, source_target_pairs={{0,20},{1,21},{2,22},{3,23},{4,0},{5,1},{6,2},{7,3},{8,9},{9,8},{1... | collective-permute-start | bytes 393224 | tf_op jit(solution)/shard_map/ppermute | solution.py:192
  6.0 1.4 %collective-permute-start.6 = (bf16[128,512]{1,0:T(8,128)(2,1)S(1)}, bf16[128,512]{1,0:T(8,128)(2,1)S(1)}, u32[]{:S(2)}, u32[]{:S(2)}) collective-permute-start(bf16[128,512]{1,0:T(8,128)(2,1)S(1)} %shard_map.95.own_ref), channel_id=1, source_target_pairs={{0,1},{1,0},{2,3},{3,2},{4,20},{5,21},{6,22},{7,23},{8,9},{9,8},{1... | collective-permute-start | bytes 393224 | tf_op jit(solution)/shard_map/ppermute | solution.py:192
  7.6 1.4 %collective-permute-start.7 = (bf16[128,512]{1,0:T(8,128)(2,1)S(1)}, bf16[128,512]{1,0:T(8,128)(2,1)S(1)}, u32[]{:S(2)}, u32[]{:S(2)}) collective-permute-start(bf16[128,512]{1,0:T(8,128)(2,1)S(1)} %get-tuple-element.38.own_ref), channel_id=1, source_target_pairs={{0,1},{1,0},{2,3},{3,2},{4,5},{5,4},{6,7},{7,6},{8,9},{9,8},{10,11... | collective-permute-start | bytes 393224 | tf_op jit(solution)/shard_map/ppermute | solution.py:192
  9.4 1.7 %collective-permute-start.8 = (bf16[128,512]{1,0:T(8,128)(2,1)S(1)}, bf16[128,512]{1,0:T(8,128)(2,1)S(1)}, u32[]{:S(2)}, u32[]{:S(2)}) collective-permute-start(bf16[128,512]{1,0:T(8,128)(2,1)S(1)} %shard_map.99.own_ref), channel_id=1, source_target_pairs={{0,4},{1,5},{2,6},{3,7},{4,0},{5,1},{6,2},{7,3},{8,9},{9,8},{10,11... | collective-permute-start | bytes 393224 | tf_op jit(solution)/shard_map/ppermute | solution.py:192
  9.8 1.3 %collective-permute-start.9 = (bf16[128,256]{1,0:T(8,128)(2,1)S(1)}, bf16[128,256]{1,0:T(8,128)(2,1)S(1)}, u32[]{:S(2)}, u32[]{:S(2)}) collective-permute-start(bf16[128,256]{1,0:T(8,128)(2,1)S(1)} %copy-done.3), channel_id=1, source_target_pairs={{0,2},{1,3},{2,0},{3,1},{4,6},{5,7},{6,4},{7,5},{8,9},{9,8},{10,11... | collective-permute-start | bytes 196616 | tf_op jit(solution)/shard_map/ppermute | solution.py:192
  9.9 1.7 %collective-permute-start.11 = (bf16[128,512]{1,0:T(8,128)(2,1)S(1)}, bf16[128,512]{1,0:T(8,128)(2,1)S(1)}, u32[]{:S(2)}, u32[]{:S(2)}) collective-permute-start(bf16[128,512]{1,0:T(8,128)(2,1)S(1)} %get-tuple-element.45.mix_ref), channel_id=1, source_target_pairs={{0,1},{1,0},{2,3},{3,2},{4,20},{5,21},{6,22},{7,23},{8,9},{9,8},{1... | collective-permute-start | bytes 393224 | tf_op jit(solution)/shard_map/ppermute | solution.py:192
  11.4 1.4 %collective-permute-start.10 = (bf16[128,512]{1,0:T(8,128)(2,1)S(1)}, bf16[128,512]{1,0:T(8,128)(2,1)S(1)}, u32[]{:S(2)}, u32[]{:S(2)}) collective-permute-start(bf16[128,512]{1,0:T(8,128)(2,1)S(1)} %get-tuple-element.43.own_ref), channel_id=1, source_target_pairs={{0,1},{1,0},{2,3},{3,2},{4,5},{5,4},{6,7},{7,6},{8,9},{9,8},{10,11... | collective-permute-start | bytes 393224 | tf_op jit(solution)/shard_map/ppermute | solution.py:192
  11.9 2.2 %collective-permute-start.15 = (bf16[128,512]{1,0:T(8,128)(2,1)S(1)}, bf16[128,512]{1,0:T(8,128)(2,1)S(1)}, u32[]{:S(2)}, u32[]{:S(2)}) collective-permute-start(bf16[128,512]{1,0:T(8,128)(2,1)S(1)} %get-tuple-element.53.mix_ref), channel_id=1, source_target_pairs={{0,1},{1,0},{2,3},{3,2},{4,5},{5,4},{6,7},{7,6},{8,9},{9,8},{10,11... | collective-permute-start | bytes 393224 | tf_op jit(solution)/shard_map/ppermute | solution.py:192
  13.1 2.1 %collective-permute-start.12 = (bf16[128,512]{1,0:T(8,128)(2,1)S(1)}, bf16[128,512]{1,0:T(8,128)(2,1)S(1)}, u32[]{:S(2)}, u32[]{:S(2)}) collective-permute-start(bf16[128,512]{1,0:T(8,128)(2,1)S(1)} %shard_map.103.own_ref), channel_id=1, source_target_pairs={{0,4},{1,5},{2,6},{3,7},{4,16},{5,17},{6,18},{7,19},{8,9},{9,8},{1... | collective-permute-start | bytes 393224 | tf_op jit(solution)/shard_map/ppermute | solution.py:192
  13.3 1.8 %collective-permute-start.13 = (bf16[128,512]{1,0:T(8,128)(2,1)S(1)}, bf16[128,512]{1,0:T(8,128)(2,1)S(1)}, u32[]{:S(2)}, u32[]{:S(2)}) collective-permute-start(bf16[128,512]{1,0:T(8,128)(2,1)S(1)} %shard_map.103.own_ref), channel_id=1, source_target_pairs={{0,1},{1,0},{2,3},{3,2},{4,20},{5,21},{6,22},{7,23},{8,9},{9,8},{1... | collective-permute-start | bytes 393224 | tf_op jit(solution)/shard_map/ppermute | solution.py:192
  13.8 1.3 %collective-permute-start.14 = (f32[128,128]{1,0:T(8,128)S(1)}, f32[128,128]{1,0:T(8,128)S(1)}, u32[]{:S(2)}, u32[]{:S(2)}) collective-permute-start(f32[128,128]{1,0:T(8,128)S(1)} %shard_map.104.two_ref), channel_id=1, source_target_pairs={{0,1},{1,0},{2,3},{3,2},{4,5},{5,4},{6,7},{7,6},{8,9},{9,8},{10,11... | collective-permute-start | bytes 196616 | tf_op jit(solution)/shard_map/ppermute | solution.py:192
  15.2 1.4 %collective-permute-start.16 = (bf16[128,512]{1,0:T(8,128)(2,1)S(1)}, bf16[128,512]{1,0:T(8,128)(2,1)S(1)}, u32[]{:S(2)}, u32[]{:S(2)}) collective-permute-start(bf16[128,512]{1,0:T(8,128)(2,1)S(1)} %shard_map.105.dz_ref), channel_id=1, source_target_pairs={{0,1},{1,0},{2,3},{3,2},{4,5},{5,4},{6,7},{7,6},{8,9},{9,8},{10,11... | collective-permute-start | bytes 393224 | tf_op jit(solution)/shard_map/ppermute | solution.py:192
  17.1 1.4 %collective-permute-start.17 = (bf16[64,1024]{1,0:T(8,128)(2,1)S(1)}, bf16[64,1024]{1,0:T(8,128)(2,1)S(1)}, u32[]{:S(2)}, u32[]{:S(2)}) collective-permute-start(bf16[64,1024]{1,0:T(8,128)(2,1)S(1)} %shard_map.107.own_ref), channel_id=1, source_target_pairs={{0,4},{1,5},{2,6},{3,7},{4,16},{5,17},{6,18},{7,19},{8,9},{9,8},{1... | collective-permute-start | bytes 393224 | tf_op jit(solution)/shard_map/ppermute | solution.py:192
  17.3 1.3 %collective-permute-start.18 = (bf16[64,1024]{1,0:T(8,128)(2,1)S(1)}, bf16[64,1024]{1,0:T(8,128)(2,1)S(1)}, u32[]{:S(2)}, u32[]{:S(2)}) collective-permute-start(bf16[64,1024]{1,0:T(8,128)(2,1)S(1)} %shard_map.107.own_ref), channel_id=1, source_target_pairs={{0,1},{1,0},{2,3},{3,2},{4,20},{5,21},{6,22},{7,23},{8,9},{9,8},{1... | collective-permute-start | bytes 393224 | tf_op jit(solution)/shard_map/ppermute | solution.py:192
  18.7 31.3 %collective-permute-start.19 = (bf16[64,1024]{1,0:T(8,128)(2,1)S(1)}, bf16[64,1024]{1,0:T(8,128)(2,1)S(1)}, u32[]{:S(2)}, u32[]{:S(2)}) collective-permute-start(bf16[64,1024]{1,0:T(8,128)(2,1)S(1)} %shard_map.108.own_ref), channel_id=1, source_target_pairs={{0,8},{1,9},{2,10},{3,11},{4,12},{5,13},{6,14},{7,15},{16,24},{17,... | collective-permute-start | bytes 393224 | tf_op jit(solution)/shard_map/ppermute | solution.py:192

commit v5 on v4

--- a/solution.py
+++ b/solution.py
@@ -571,8 +571,13 @@
         [pltpu.VMEM((hidden, nodes), jnp.bfloat16)],
         flops=product_flops,
     )
-    near_one = routed(part_one, to_row_owner)
-    across_one = routed(part_one, to_odd_across)
+    near_one, across_one, cot_pair = lax.optimization_barrier(
+        (
+            routed(part_one, to_row_owner),
+            routed(part_one, to_odd_across),
+            routed(lax.optimization_barrier((cotangent, part_one))[0], to_other_pair),
+        )
+    )
     mix_one, h_one = local_call(
         layer_one_kernel,
         [bf16_array(hidden, half)] * 2,
@@ -589,8 +594,7 @@
         [total_two, h_swap, block],
         flops=product_flops // 2,
     )
-    cot_pair = routed(lax.optimization_barrier((cotangent, h_one))[0], to_other_pair)
-    near_two, cot_pair = lax.optimization_barrier((routed(part_two, to_other_rep), cot_pair))
+    near_two = routed(part_two, to_other_rep)
     mix_two, dz_two, dm_two = local_call(
         layer_two_kernel,
         [bf16_array(hidden, half)] * 3,

time: 50.8 us -> 50.4 us (level)
  transfers between devices with their start and end apart: 20 -> 20, of which waited for: 12 -> 11; matrix products, arithmetic and copies ran while one was open for 0% -> 0% of each run, Pallas kernels for 7% -> 7%
where the time goes in v5:
time: 50.4 us; the launch traced here: 50.2 us
  waiting for transfers between devices  36.5 us (72%)
  starting transfers between devices  6.28 us (12%)
  Pallas kernels  5.91 us (12%)
  between operations  1.47 us (3%)
    ppermute x20, waiting for transfers between devices, routed(): return lax.ppermute(value, mesh_axes, pairs)  36.5 us
    ppermute x20, starting transfers between devices, routed(): return lax.ppermute(value, mesh_axes, pairs)  6.28 us
    pallas_call x16, Pallas kernels, local_call(): pl.pallas_call(kernel, out_shape=list(outs), in_specs=[pl.BlockSpec(memor...  5.91 us
  transfers between devices with their start and end apart: 20, of which 11 were waited for; matrix products, arithmetic and copies ran while one was open for 0% of the time, Pallas kernels for 7%

profile of v5, /device:TPU:24, one launch (start us, length us, event | category | flops | bytes accessed | tf_op | source)
XLA Modules:
  0.0 50.2 jit_solution(347973689136175435)
XLA Ops:
  0.6 0.1 collective-permute-start
  0.7 0.5 collective-permute-start.1
  1.2 0.1 collective-permute-start.2
  2.0 1.6 %shard_map.94.block_ref = bf16[1024,1024]{1,0:T(8,128)(2,1)S(1)} custom-call(s32[1]{0:T(128)} %bitcast.1.count_ref, s32[1,1,2,112]{3,2,1,0:T(2,128)} %coords_ref.1, bf16[1,1,112,128,128]{4,3,2,1,0:T(8,128)(2,1)} %tiles_ref.1), custom_call_target="tpu_custom_call" | custom-call | flops 4000000000 | bytes 7865220 | tf_op jit(solution)/shard_map/pallas_call | solution.py:244
  3.6 0.0 collective-permute-done.1.pair_ref
  3.6 0.5 collective-permute-start.3
  4.1 0.1 collective-permute-start.4
  4.2 0.0 collective-permute-done.2.own_swap_ref
  4.2 0.8 %collective-permute-done.3.across_swap_ref = bf16[32,1024]{1,0:T(8,128)(2,1)S(1)} collective-permute-done((bf16[32,1024]{1,0:T(8,128)(2,1)S(1)}, bf16[32,1024]{1,0:T(8,128)(2,1)S(1)}, u32[]{:S(2)}, u32[]{:S(2)}) %collective-permute-start.3) | collective-permute-done | bytes 65568 | tf_op jit(solution)/shard_map/ppermute | solution.py:192
  5.0 0.4 collective-permute-done.4.pair_swap_ref
  5.4 0.5 shard_map.95.own_ref
  5.9 0.2 collective-permute-start.5
  6.1 0.4 collective-permute-start.6
  6.4 0.2 collective-permute-start.7
  6.6 0.1 shard_map.96
  6.7 1.0 %collective-permute-done.7.cot_pair_ref = bf16[128,256]{1,0:T(8,128)(2,1)S(1)} collective-permute-done((bf16[128,256]{1,0:T(8,128)(2,1)S(1)}, bf16[128,256]{1,0:T(8,128)(2,1)S(1)}, u32[]{:S(2)}, u32[]{:S(2)}) %collective-permute-start.7) | collective-permute-done | bytes 65568 | tf_op jit(solution)/shard_map/ppermute | solution.py:192
  7.7 0.2 shard_map.97
  7.9 0.2 collective-permute-start.8
  8.1 0.3 shard_map.98.total_ref
  8.5 0.9 %collective-permute-done.8.other_ref = bf16[128,512]{1,0:T(8,128)(2,1)S(1)} collective-permute-done((bf16[128,512]{1,0:T(8,128)(2,1)S(1)}, bf16[128,512]{1,0:T(8,128)(2,1)S(1)}, u32[]{:S(2)}, u32[]{:S(2)}) %collective-permute-start.8) | collective-permute-done | bytes 131104 | tf_op jit(solution)/shard_map/ppermute | solution.py:192
  9.3 0.3 shard_map.99.own_ref
  9.6 0.2 collective-permute-start.9
  9.9 0.3 collective-permute-start.11
  10.2 0.8 %collective-permute-done.9.near_ref = bf16[128,512]{1,0:T(8,128)(2,1)S(1)} collective-permute-done((bf16[128,512]{1,0:T(8,128)(2,1)S(1)}, bf16[128,512]{1,0:T(8,128)(2,1)S(1)}, u32[]{:S(2)}, u32[]{:S(2)}) %collective-permute-start.9) | collective-permute-done | bytes 131104 | tf_op jit(solution)/shard_map/ppermute | solution.py:192
  11.0 0.4 shard_map.100
  11.5 0.2 collective-permute-start.10
  11.7 0.2 shard_map.101
  11.9 0.4 collective-permute-start.15
  12.3 0.2 shard_map.102.total_ref
  12.6 0.3 collective-permute-done.10.other_ref
  12.9 0.2 shard_map.103.own_ref
  13.1 0.2 collective-permute-start.12
  13.3 0.3 collective-permute-start.13
  13.7 0.2 shard_map.104.two_ref
  13.8 0.2 collective-permute-start.14
  14.1 1.1 %collective-permute-done.14.two_swap_ref = f32[128,128]{1,0:T(8,128)S(1)} collective-permute-done((f32[128,128]{1,0:T(8,128)S(1)}, f32[128,128]{1,0:T(8,128)S(1)}, u32[]{:S(2)}, u32[]{:S(2)}) %collective-permute-start.14) | collective-permute-done | bytes 65568 | tf_op jit(solution)/shard_map/ppermute | solution.py:192
  15.2 0.1 shard_map.105.dz_ref
  15.2 0.2 collective-permute-start.16
  15.5 0.4 shard_map.106
  15.9 0.7 %collective-permute-done.16.dz_swap_ref = bf16[128,512]{1,0:T(8,128)(2,1)S(1)} collective-permute-done((bf16[128,512]{1,0:T(8,128)(2,1)S(1)}, bf16[128,512]{1,0:T(8,128)(2,1)S(1)}, u32[]{:S(2)}, u32[]{:S(2)}) %collective-permute-start.16) | collective-permute-done | bytes 131104 | tf_op jit(solution)/shard_map/ppermute | solution.py:192
  16.7 0.4 shard_map.107.own_ref
  17.1 0.2 collective-permute-start.17
  17.3 0.3 collective-permute-start.18
  17.7 0.8 %collective-permute-done.17.near_ref = bf16[64,1024]{1,0:T(8,128)(2,1)S(1)} collective-permute-done((bf16[64,1024]{1,0:T(8,128)(2,1)S(1)}, bf16[64,1024]{1,0:T(8,128)(2,1)S(1)}, u32[]{:S(2)}, u32[]{:S(2)}) %collective-permute-start.17) | collective-permute-done | bytes 131104 | tf_op jit(solution)/shard_map/ppermute | solution.py:192
  18.5 0.2 collective-permute-done.18.across_ref
  18.7 1.3 %collective-permute-start.19 = (bf16[64,1024]{1,0:T(8,128)(2,1)S(1)}, bf16[64,1024]{1,0:T(8,128)(2,1)S(1)}, u32[]{:S(2)}, u32[]{:S(2)}) collective-permute-start(bf16[64,1024]{1,0:T(8,128)(2,1)S(1)} %shard_map.108.own_ref), channel_id=1, source_target_pairs={{0,8},{1,9},{2,10},{3,11},{4,12},{5,13},{6,14},{7,15},{16,24},{17,... | collective-permute-start | bytes 393224 | tf_op jit(solution)/shard_map/ppermute | solution.py:192
  20.0 29.5 %collective-permute-done.19.far_ref = bf16[64,1024]{1,0:T(8,128)(2,1)S(1)} collective-permute-done((bf16[64,1024]{1,0:T(8,128)(2,1)S(1)}, bf16[64,1024]{1,0:T(8,128)(2,1)S(1)}, u32[]{:S(2)}, u32[]{:S(2)}) %collective-permute-start.19) | collective-permute-done | bytes 131104 | tf_op jit(solution)/shard_map/ppermute | solution.py:192
  49.5 0.7 %shard_map.109 = (f32[128,128]{1,0:T(8,128)}, f32[128,128]{1,0:T(8,128)}, bf16[32,1024]{1,0:T(8,128)(2,1)}) custom-call(bf16[64,1024]{1,0:T(8,128)(2,1)S(1)} %shard_map.108.own_ref, bf16[64,1024]{1,0:T(8,128)(2,1)S(1)} %collective-permute-done.19.far_ref), custom_call_target="tpu_custom_call" | custom-call | bytes 524288 | tf_op jit(solution)/shard_map/pallas_call | solution.py:244
  (16 shorter events, 0.1 us)
Async XLA Ops:
  0.6 3.0 %collective-permute-start = (bf16[32,1024]{1,0:T(8,128)(2,1)}, bf16[32,1024]{1,0:T(8,128)(2,1)S(1)}, u32[]{:S(2)}, u32[]{:S(2)}) collective-permute-start(bf16[32,1024]{1,0:T(8,128)(2,1)} %own_ref.1), channel_id=1, source_target_pairs={{0,1},{1,0},{2,3},{3,2},{4,20},{5,21},{6,22},{7,23},{8,9},{9,8},{1... | collective-permute-start | bytes 196616 | tf_op jit(solution)/shard_map/ppermute | solution.py:192
  0.7 2.9 %collective-permute-start.1 = (bf16[32,1024]{1,0:T(8,128)(2,1)}, bf16[32,1024]{1,0:T(8,128)(2,1)S(1)}, u32[]{:S(2)}, u32[]{:S(2)}) collective-permute-start(bf16[32,1024]{1,0:T(8,128)(2,1)} %own_ref.1), channel_id=1, source_target_pairs={{0,2},{1,3},{2,0},{3,1},{4,22},{5,23},{6,20},{7,21},{8,9},{9,8},{1... | collective-permute-start | bytes 196616 | tf_op jit(solution)/shard_map/ppermute | solution.py:192
  1.2 3.0 %collective-permute-start.2 = (bf16[32,1024]{1,0:T(8,128)(2,1)}, bf16[32,1024]{1,0:T(8,128)(2,1)S(1)}, u32[]{:S(2)}, u32[]{:S(2)}) collective-permute-start(bf16[32,1024]{1,0:T(8,128)(2,1)} %own_ref.1), channel_id=1, source_target_pairs={{0,1},{1,0},{2,3},{3,2},{4,5},{5,4},{6,7},{7,6},{8,9},{9,8},{10,11... | collective-permute-start | bytes 196616 | tf_op jit(solution)/shard_map/ppermute | solution.py:192
  1.9 3.4 %copy-start.2 = (bf16[32,1024]{1,0:T(8,128)(2,1)S(1)}, bf16[32,1024]{1,0:T(8,128)(2,1)}, u32[]{:S(2)}) copy-start(bf16[32,1024]{1,0:T(8,128)(2,1)} %own_ref.1) | copy-start | bytes 196612
  1.9 4.5 %copy-start.3 = (bf16[128,256]{1,0:T(8,128)(2,1)S(1)}, bf16[128,256]{1,0:T(8,128)(2,1)}, u32[]{:S(2)}) copy-start(bf16[128,256]{1,0:T(8,128)(2,1)} %cot_ref.1) | copy-start | bytes 196612
  2.0 4.6 %copy-start = (bf16[128,128]{1,0:T(8,128)(2,1)S(1)}, bf16[128,128]{1,0:T(8,128)(2,1)}, u32[]{:S(2)}) copy-start(bf16[128,128]{1,0:T(8,128)(2,1)} %weight_ref.5) | copy-start | bytes 98308
  2.0 4.6 %copy-start.1 = (bf16[128,128]{1,0:T(8,128)(2,1)S(1)}, bf16[128,128]{1,0:T(8,128)(2,1)}, u32[]{:S(2)}) copy-start(bf16[128,128]{1,0:T(8,128)(2,1)} %weight_ref.3) | copy-start | bytes 98308
  3.6 1.4 %collective-permute-start.3 = (bf16[32,1024]{1,0:T(8,128)(2,1)S(1)}, bf16[32,1024]{1,0:T(8,128)(2,1)S(1)}, u32[]{:S(2)}, u32[]{:S(2)}) collective-permute-start(bf16[32,1024]{1,0:T(8,128)(2,1)S(1)} %collective-permute-done.across_ref), channel_id=1, source_target_pairs={{0,1},{1,0},{2,3},{3,2},{4,5},{5,4},{6,7},{7,6},{8,9},{9,8},{10,11... | collective-permute-start | bytes 196616 | tf_op jit(solution)/shard_map/ppermute | solution.py:192
  4.1 1.3 %collective-permute-start.4 = (bf16[32,1024]{1,0:T(8,128)(2,1)S(1)}, bf16[32,1024]{1,0:T(8,128)(2,1)S(1)}, u32[]{:S(2)}, u32[]{:S(2)}) collective-permute-start(bf16[32,1024]{1,0:T(8,128)(2,1)S(1)} %collective-permute-done.1.pair_ref), channel_id=1, source_target_pairs={{0,1},{1,0},{2,3},{3,2},{4,5},{5,4},{6,7},{7,6},{8,9},{9,8},{10,11... | collective-permute-start | bytes 196616 | tf_op jit(solution)/shard_map/ppermute | solution.py:192
  5.9 1.8 %collective-permute-start.5 = (bf16[128,512]{1,0:T(8,128)(2,1)S(1)}, bf16[128,512]{1,0:T(8,128)(2,1)S(1)}, u32[]{:S(2)}, u32[]{:S(2)}) collective-permute-start(bf16[128,512]{1,0:T(8,128)(2,1)S(1)} %shard_map.95.own_ref), channel_id=1, source_target_pairs={{0,20},{1,21},{2,22},{3,23},{4,0},{5,1},{6,2},{7,3},{8,9},{9,8},{1... | collective-permute-start | bytes 393224 | tf_op jit(solution)/shard_map/ppermute | solution.py:192
  6.1 1.6 %collective-permute-start.6 = (bf16[128,512]{1,0:T(8,128)(2,1)S(1)}, bf16[128,512]{1,0:T(8,128)(2,1)S(1)}, u32[]{:S(2)}, u32[]{:S(2)}) collective-permute-start(bf16[128,512]{1,0:T(8,128)(2,1)S(1)} %shard_map.95.own_ref), channel_id=1, source_target_pairs={{0,1},{1,0},{2,3},{3,2},{4,20},{5,21},{6,22},{7,23},{8,9},{9,8},{1... | collective-permute-start | bytes 393224 | tf_op jit(solution)/shard_map/ppermute | solution.py:192
  6.4 1.3 %collective-permute-start.7 = (bf16[128,256]{1,0:T(8,128)(2,1)S(1)}, bf16[128,256]{1,0:T(8,128)(2,1)S(1)}, u32[]{:S(2)}, u32[]{:S(2)}) collective-permute-start(bf16[128,256]{1,0:T(8,128)(2,1)S(1)} %copy-done.3), channel_id=1, source_target_pairs={{0,2},{1,3},{2,0},{3,1},{4,6},{5,7},{6,4},{7,5},{8,9},{9,8},{10,11... | collective-permute-start | bytes 196616 | tf_op jit(solution)/shard_map/ppermute | solution.py:192
  7.9 1.4 %collective-permute-start.8 = (bf16[128,512]{1,0:T(8,128)(2,1)S(1)}, bf16[128,512]{1,0:T(8,128)(2,1)S(1)}, u32[]{:S(2)}, u32[]{:S(2)}) collective-permute-start(bf16[128,512]{1,0:T(8,128)(2,1)S(1)} %get-tuple-element.42.own_ref), channel_id=1, source_target_pairs={{0,1},{1,0},{2,3},{3,2},{4,5},{5,4},{6,7},{7,6},{8,9},{9,8},{10,11... | collective-permute-start | bytes 393224 | tf_op jit(solution)/shard_map/ppermute | solution.py:192
  9.6 1.4 %collective-permute-start.9 = (bf16[128,512]{1,0:T(8,128)(2,1)S(1)}, bf16[128,512]{1,0:T(8,128)(2,1)S(1)}, u32[]{:S(2)}, u32[]{:S(2)}) collective-permute-start(bf16[128,512]{1,0:T(8,128)(2,1)S(1)} %shard_map.99.own_ref), channel_id=1, source_target_pairs={{0,4},{1,5},{2,6},{3,7},{4,0},{5,1},{6,2},{7,3},{8,9},{9,8},{10,11... | collective-permute-start | bytes 393224 | tf_op jit(solution)/shard_map/ppermute | solution.py:192
  9.9 1.8 %collective-permute-start.11 = (bf16[128,512]{1,0:T(8,128)(2,1)S(1)}, bf16[128,512]{1,0:T(8,128)(2,1)S(1)}, u32[]{:S(2)}, u32[]{:S(2)}) collective-permute-start(bf16[128,512]{1,0:T(8,128)(2,1)S(1)} %get-tuple-element.47.mix_ref), channel_id=1, source_target_pairs={{0,1},{1,0},{2,3},{3,2},{4,20},{5,21},{6,22},{7,23},{8,9},{9,8},{1... | collective-permute-start | bytes 393224 | tf_op jit(solution)/shard_map/ppermute | solution.py:192
  11.5 1.4 %collective-permute-start.10 = (bf16[128,512]{1,0:T(8,128)(2,1)S(1)}, bf16[128,512]{1,0:T(8,128)(2,1)S(1)}, u32[]{:S(2)}, u32[]{:S(2)}) collective-permute-start(bf16[128,512]{1,0:T(8,128)(2,1)S(1)} %get-tuple-element.45.own_ref), channel_id=1, source_target_pairs={{0,1},{1,0},{2,3},{3,2},{4,5},{5,4},{6,7},{7,6},{8,9},{9,8},{10,11... | collective-permute-start | bytes 393224 | tf_op jit(solution)/shard_map/ppermute | solution.py:192
  11.9 2.2 %collective-permute-start.15 = (bf16[128,512]{1,0:T(8,128)(2,1)S(1)}, bf16[128,512]{1,0:T(8,128)(2,1)S(1)}, u32[]{:S(2)}, u32[]{:S(2)}) collective-permute-start(bf16[128,512]{1,0:T(8,128)(2,1)S(1)} %get-tuple-element.55.mix_ref), channel_id=1, source_target_pairs={{0,1},{1,0},{2,3},{3,2},{4,5},{5,4},{6,7},{7,6},{8,9},{9,8},{10,11... | collective-permute-start | bytes 393224 | tf_op jit(solution)/shard_map/ppermute | solution.py:192
  13.1 2.1 %collective-permute-start.12 = (bf16[128,512]{1,0:T(8,128)(2,1)S(1)}, bf16[128,512]{1,0:T(8,128)(2,1)S(1)}, u32[]{:S(2)}, u32[]{:S(2)}) collective-permute-start(bf16[128,512]{1,0:T(8,128)(2,1)S(1)} %shard_map.103.own_ref), channel_id=1, source_target_pairs={{0,4},{1,5},{2,6},{3,7},{4,16},{5,17},{6,18},{7,19},{8,9},{9,8},{1... | collective-permute-start | bytes 393224 | tf_op jit(solution)/shard_map/ppermute | solution.py:192
  13.3 1.8 %collective-permute-start.13 = (bf16[128,512]{1,0:T(8,128)(2,1)S(1)}, bf16[128,512]{1,0:T(8,128)(2,1)S(1)}, u32[]{:S(2)}, u32[]{:S(2)}) collective-permute-start(bf16[128,512]{1,0:T(8,128)(2,1)S(1)} %shard_map.103.own_ref), channel_id=1, source_target_pairs={{0,1},{1,0},{2,3},{3,2},{4,20},{5,21},{6,22},{7,23},{8,9},{9,8},{1... | collective-permute-start | bytes 393224 | tf_op jit(solution)/shard_map/ppermute | solution.py:192
  13.8 1.3 %collective-permute-start.14 = (f32[128,128]{1,0:T(8,128)S(1)}, f32[128,128]{1,0:T(8,128)S(1)}, u32[]{:S(2)}, u32[]{:S(2)}) collective-permute-start(f32[128,128]{1,0:T(8,128)S(1)} %shard_map.104.two_ref), channel_id=1, source_target_pairs={{0,1},{1,0},{2,3},{3,2},{4,5},{5,4},{6,7},{7,6},{8,9},{9,8},{10,11... | collective-permute-start | bytes 196616 | tf_op jit(solution)/shard_map/ppermute | solution.py:192
  15.2 1.4 %collective-permute-start.16 = (bf16[128,512]{1,0:T(8,128)(2,1)S(1)}, bf16[128,512]{1,0:T(8,128)(2,1)S(1)}, u32[]{:S(2)}, u32[]{:S(2)}) collective-permute-start(bf16[128,512]{1,0:T(8,128)(2,1)S(1)} %shard_map.105.dz_ref), channel_id=1, source_target_pairs={{0,1},{1,0},{2,3},{3,2},{4,5},{5,4},{6,7},{7,6},{8,9},{9,8},{10,11... | collective-permute-start | bytes 393224 | tf_op jit(solution)/shard_map/ppermute | solution.py:192
  17.1 1.4 %collective-permute-start.17 = (bf16[64,1024]{1,0:T(8,128)(2,1)S(1)}, bf16[64,1024]{1,0:T(8,128)(2,1)S(1)}, u32[]{:S(2)}, u32[]{:S(2)}) collective-permute-start(bf16[64,1024]{1,0:T(8,128)(2,1)S(1)} %shard_map.107.own_ref), channel_id=1, source_target_pairs={{0,4},{1,5},{2,6},{3,7},{4,16},{5,17},{6,18},{7,19},{8,9},{9,8},{1... | collective-permute-start | bytes 393224 | tf_op jit(solution)/shard_map/ppermute | solution.py:192
  17.3 1.4 %collective-permute-start.18 = (bf16[64,1024]{1,0:T(8,128)(2,1)S(1)}, bf16[64,1024]{1,0:T(8,128)(2,1)S(1)}, u32[]{:S(2)}, u32[]{:S(2)}) collective-permute-start(bf16[64,1024]{1,0:T(8,128)(2,1)S(1)} %shard_map.107.own_ref), channel_id=1, source_target_pairs={{0,1},{1,0},{2,3},{3,2},{4,20},{5,21},{6,22},{7,23},{8,9},{9,8},{1... | collective-permute-start | bytes 393224 | tf_op jit(solution)/shard_map/ppermute | solution.py:192
  18.7 30.8 %collective-permute-start.19 = (bf16[64,1024]{1,0:T(8,128)(2,1)S(1)}, bf16[64,1024]{1,0:T(8,128)(2,1)S(1)}, u32[]{:S(2)}, u32[]{:S(2)}) collective-permute-start(bf16[64,1024]{1,0:T(8,128)(2,1)S(1)} %shard_map.108.own_ref), channel_id=1, source_target_pairs={{0,8},{1,9},{2,10},{3,11},{4,12},{5,13},{6,14},{7,15},{16,24},{17,... | collective-permute-start | bytes 393224 | tf_op jit(solution)/shard_map/ppermute | solution.py:192

commit v6 on v5

--- a/solution.py
+++ b/solution.py
@@ -482,22 +482,41 @@
     grad, grad_swap = grad_ref[...], dot_nt(mix_swap_ref[...], dz_swap)
     one = jnp.where(second, grad_swap, grad) + jnp.where(second, grad, grad_swap)
     two = two_ref[...] + two_swap_ref[...]
-    count = hidden // width
-    for index, grad in enumerate((one, two)):
-        grad = grad.astype(out_ref.dtype)
-        for part in range(count):
-            lane = (index * count + part) * hidden
-            out_ref[width:, lane : lane + hidden] = grad[part * width : (part + 1) * width, :]
+    grad = jnp.where(second, two, one).astype(out_ref.dtype)
+    lines = out_ref.shape[0] - width
+    for part in range(hidden // lines):
+        out_ref[width:, part * hidden : (part + 1) * hidden] = grad[
+            part * lines : (part + 1) * lines, :
+        ]
 
 
 def near_kernel(own_ref, near_ref, across_ref, out_ref):
     out_ref[...] = summed(own_ref, near_ref, across_ref)
 
 
-def last_kernel(scale, own_ref, far_ref, one_ref, two_ref, out_ref):
+def split_kernel(own_ref, far_ref, grad_ref):
+    lines = grad_ref.shape[0]
+    width = own_ref.shape[0] - lines
+    grad_ref[...] = own_ref[width:, :] + far_ref[width:, :]
+
+
+def total_kernel(scale, own_ref, swap_ref, one_ref, two_ref):
+    second = lax.axis_index("feat") % 2 == 1
+    hidden = one_ref.shape[0]
+    lines = own_ref.shape[0]
+    own, swap = own_ref[...], swap_ref[...]
+    values = (jnp.where(second, swap, own), jnp.where(second, own, swap))
+    for value, grad_ref in zip(values, (one_ref, two_ref)):
+        value = value.astype(jnp.float32) * scale
+        for part in range(hidden // lines):
+            grad_ref[part * lines : (part + 1) * lines, :] = value[
+                :, part * hidden : (part + 1) * hidden
+            ]
+
+
+def last_kernel(own_ref, far_ref, out_ref):
     core = lax.axis_index("feat") % 2
     width, nodes = out_ref.shape
-    hidden = one_ref.shape[0]
     quarter = nodes // 4
     half = nodes // 2
     for part in range(4):
@@ -508,13 +527,6 @@
         out_ref[:, part * quarter : (part + 1) * quarter] = (
             own_ref[:width, columns] + far_ref[:width, columns]
         )
-    count = hidden // width
-    for index, grad_ref in enumerate((one_ref, two_ref)):
-        for part in range(count):
-            lane = (index * count + part) * hidden
-            total = own_ref[width:, lane : lane + hidden].astype(jnp.float32)
-            total += far_ref[width:, lane : lane + hidden].astype(jnp.float32)
-            grad_ref[part * width : (part + 1) * width, :] = total * scale
 
 
 def paired_shards(
@@ -645,9 +657,10 @@
         flops=product_flops // 2,
     )
     dz_swap, total_four = lax.optimization_barrier((dz_swap, total_four))
+    lines = hidden * hidden // nodes
     (message,) = local_call(
         message_kernel,
-        [bf16_array(2 * width, nodes)],
+        [bf16_array(width + lines, nodes)],
         [
             total_four,
             grad_one,
@@ -662,16 +675,19 @@
     )
     (near_sum,) = local_call(
         near_kernel,
-        [bf16_array(2 * width, nodes)],
+        [bf16_array(width + lines, nodes)],
         [message, routed(message, to_column_owner), routed(message, to_odd_across)],
     )
-    return tuple(
-        local_call(
-            functools.partial(last_kernel, scale),
-            [f32_array(hidden, hidden), f32_array(hidden, hidden), bf16_array(width, nodes)],
-            [near_sum, routed(near_sum, to_far_rep, True)],
-        )
-    )
+    far_sum = routed(near_sum, to_far_rep, True)
+    (grad,) = local_call(split_kernel, [bf16_array(lines, nodes)], [near_sum, far_sum])
+    grad_swap = routed(grad, to_other_core)
+    (input_grad,) = local_call(last_kernel, [bf16_array(width, nodes)], [near_sum, far_sum])
+    grad_one, grad_two = local_call(
+        functools.partial(total_kernel, scale),
+        [f32_array(hidden, hidden)] * 2,
+        [grad, grad_swap],
+    )
+    return (grad_one, grad_two, input_grad)
 
 
 def solution(mesh):

time: 50.4 us -> 49.8 us (0.988)
  waiting for transfers between devices: 36.5 us -> 35 us
  Pallas kernels: 5.91 us -> 6.54 us
    ppermute x20 -> x21, waiting for transfers between devices: 36.5 us -> 35 us  [routed(): return lax.ppermute(value, mesh_axes, pairs)]
    pallas_call x16 -> x18, Pallas kernels: 5.91 us -> 6.54 us  [local_call(): pl.pallas_call(kernel, out_shape=list(outs), in_specs=[pl.BlockSpec(memor...]
    ppermute x20 -> x21, starting transfers between devices: 6.28 us -> 6.28 us  [routed(): return lax.ppermute(value, mesh_axes, pairs)]
  transfers between devices with their start and end apart: 20 -> 21, of which waited for: 11 -> 12; matrix products, arithmetic and copies ran while one was open for 0% -> 0% of each run, Pallas kernels for 7% -> 9%
where the time goes in v6:
time: 49.8 us; the launch traced here: 49.3 us
  waiting for transfers between devices  35 us (70%)
  Pallas kernels  6.54 us (13%)
  starting transfers between devices  6.28 us (13%)
  between operations  1.48 us (3%)
    ppermute x21, waiting for transfers between devices, routed(): return lax.ppermute(value, mesh_axes, pairs)  35 us
    pallas_call x18, Pallas kernels, local_call(): pl.pallas_call(kernel, out_shape=list(outs), in_specs=[pl.BlockSpec(memor...  6.54 us
    ppermute x21, starting transfers between devices, routed(): return lax.ppermute(value, mesh_axes, pairs)  6.28 us
  transfers between devices with their start and end apart: 21, of which 12 were waited for; matrix products, arithmetic and copies ran while one was open for 0% of the time, Pallas kernels for 9%

profile of v6, /device:TPU:24, one launch (start us, length us, event | category | flops | bytes accessed | tf_op | source)
XLA Modules:
  0.0 49.3 jit_solution(9171001802575072837)
XLA Ops:
  0.6 0.1 collective-permute-start
  0.7 0.5 %collective-permute-start.1 = (bf16[32,1024]{1,0:T(8,128)(2,1)}, bf16[32,1024]{1,0:T(8,128)(2,1)S(1)}, u32[]{:S(2)}, u32[]{:S(2)}) collective-permute-start(bf16[32,1024]{1,0:T(8,128)(2,1)} %own_ref.1), channel_id=1, source_target_pairs={{0,2},{1,3},{2,0},{3,1},{4,22},{5,23},{6,20},{7,21},{8,9},{9,8},{1... | collective-permute-start | bytes 196616 | tf_op jit(solution)/shard_map/ppermute | solution.py:192
  1.2 0.1 collective-permute-start.2
  2.0 1.6 %shard_map.94.block_ref = bf16[1024,1024]{1,0:T(8,128)(2,1)S(1)} custom-call(s32[1]{0:T(128)} %bitcast.1.count_ref, s32[1,1,2,112]{3,2,1,0:T(2,128)} %coords_ref.1, bf16[1,1,112,128,128]{4,3,2,1,0:T(8,128)(2,1)} %tiles_ref.1), custom_call_target="tpu_custom_call" | custom-call | flops 4000000000 | bytes 7865220 | tf_op jit(solution)/shard_map/pallas_call | solution.py:244
  3.6 0.5 %collective-permute-start.3 = (bf16[32,1024]{1,0:T(8,128)(2,1)S(1)}, bf16[32,1024]{1,0:T(8,128)(2,1)S(1)}, u32[]{:S(2)}, u32[]{:S(2)}) collective-permute-start(bf16[32,1024]{1,0:T(8,128)(2,1)S(1)} %collective-permute-done.across_ref), channel_id=1, source_target_pairs={{0,1},{1,0},{2,3},{3,2},{4,5},{5,4},{6,7},{7,6},{8,9},{9,8},{10,11... | collective-permute-start | bytes 196616 | tf_op jit(solution)/shard_map/ppermute | solution.py:192
  4.1 0.1 collective-permute-start.4
  4.2 0.8 %collective-permute-done.3.across_swap_ref = bf16[32,1024]{1,0:T(8,128)(2,1)S(1)} collective-permute-done((bf16[32,1024]{1,0:T(8,128)(2,1)S(1)}, bf16[32,1024]{1,0:T(8,128)(2,1)S(1)}, u32[]{:S(2)}, u32[]{:S(2)}) %collective-permute-start.3) | collective-permute-done | bytes 65568 | tf_op jit(solution)/shard_map/ppermute | solution.py:192
  5.0 0.4 collective-permute-done.4.pair_swap_ref
  5.4 0.5 shard_map.95.own_ref
  5.9 0.2 collective-permute-start.5
  6.1 0.4 collective-permute-start.6
  6.4 0.2 collective-permute-start.7
  6.6 0.1 shard_map.96
  6.7 1.0 %collective-permute-done.7.cot_pair_ref = bf16[128,256]{1,0:T(8,128)(2,1)S(1)} collective-permute-done((bf16[128,256]{1,0:T(8,128)(2,1)S(1)}, bf16[128,256]{1,0:T(8,128)(2,1)S(1)}, u32[]{:S(2)}, u32[]{:S(2)}) %collective-permute-start.7) | collective-permute-done | bytes 65568 | tf_op jit(solution)/shard_map/ppermute | solution.py:192
  7.7 0.2 shard_map.97
  7.9 0.2 collective-permute-start.8
  8.1 0.3 shard_map.98.total_ref
  8.5 0.9 %collective-permute-done.8.other_ref = bf16[128,512]{1,0:T(8,128)(2,1)S(1)} collective-permute-done((bf16[128,512]{1,0:T(8,128)(2,1)S(1)}, bf16[128,512]{1,0:T(8,128)(2,1)S(1)}, u32[]{:S(2)}, u32[]{:S(2)}) %collective-permute-start.8) | collective-permute-done | bytes 131104 | tf_op jit(solution)/shard_map/ppermute | solution.py:192
  9.3 0.3 shard_map.99.own_ref
  9.6 0.2 collective-permute-start.9
  9.9 0.3 collective-permute-start.11
  10.2 0.8 %collective-permute-done.9.near_ref = bf16[128,512]{1,0:T(8,128)(2,1)S(1)} collective-permute-done((bf16[128,512]{1,0:T(8,128)(2,1)S(1)}, bf16[128,512]{1,0:T(8,128)(2,1)S(1)}, u32[]{:S(2)}, u32[]{:S(2)}) %collective-permute-start.9) | collective-permute-done | bytes 131104 | tf_op jit(solution)/shard_map/ppermute | solution.py:192
  11.0 0.4 shard_map.100
  11.5 0.2 collective-permute-start.10
  11.7 0.2 shard_map.101
  11.9 0.4 collective-permute-start.15
  12.3 0.2 shard_map.102.total_ref
  12.6 0.3 collective-permute-done.10.other_ref
  12.9 0.2 shard_map.103.own_ref
  13.1 0.2 collective-permute-start.12
  13.3 0.3 collective-permute-start.13
  13.7 0.2 shard_map.104.two_ref
  13.8 0.2 collective-permute-start.14
  14.1 1.1 %collective-permute-done.14.two_swap_ref = f32[128,128]{1,0:T(8,128)S(1)} collective-permute-done((f32[128,128]{1,0:T(8,128)S(1)}, f32[128,128]{1,0:T(8,128)S(1)}, u32[]{:S(2)}, u32[]{:S(2)}) %collective-permute-start.14) | collective-permute-done | bytes 65568 | tf_op jit(solution)/shard_map/ppermute | solution.py:192
  15.2 0.1 shard_map.105.dz_ref
  15.2 0.2 collective-permute-start.16
  15.5 0.4 shard_map.106
  15.9 0.7 %collective-permute-done.16.dz_swap_ref = bf16[128,512]{1,0:T(8,128)(2,1)S(1)} collective-permute-done((bf16[128,512]{1,0:T(8,128)(2,1)S(1)}, bf16[128,512]{1,0:T(8,128)(2,1)S(1)}, u32[]{:S(2)}, u32[]{:S(2)}) %collective-permute-start.16) | collective-permute-done | bytes 131104 | tf_op jit(solution)/shard_map/ppermute | solution.py:192
  16.7 0.4 shard_map.107.own_ref
  17.1 0.2 collective-permute-start.17
  17.3 0.3 collective-permute-start.18
  17.7 0.8 %collective-permute-done.17.near_ref = bf16[48,1024]{1,0:T(8,128)(2,1)S(1)} collective-permute-done((bf16[48,1024]{1,0:T(8,128)(2,1)S(1)}, bf16[48,1024]{1,0:T(8,128)(2,1)S(1)}, u32[]{:S(2)}, u32[]{:S(2)}) %collective-permute-start.17) | collective-permute-done | bytes 98336 | tf_op jit(solution)/shard_map/ppermute | solution.py:192
  18.4 0.2 collective-permute-done.18.across_ref
  18.7 1.3 %collective-permute-start.19 = (bf16[48,1024]{1,0:T(8,128)(2,1)S(1)}, bf16[48,1024]{1,0:T(8,128)(2,1)S(1)}, u32[]{:S(2)}, u32[]{:S(2)}) collective-permute-start(bf16[48,1024]{1,0:T(8,128)(2,1)S(1)} %shard_map.108.own_ref), channel_id=1, source_target_pairs={{0,8},{1,9},{2,10},{3,11},{4,12},{5,13},{6,14},{7,15},{16,24},{17,... | collective-permute-start | bytes 294920 | tf_op jit(solution)/shard_map/ppermute | solution.py:192
  20.0 27.5 %collective-permute-done.19.far_ref = bf16[48,1024]{1,0:T(8,128)(2,1)S(1)} collective-permute-done((bf16[48,1024]{1,0:T(8,128)(2,1)S(1)}, bf16[48,1024]{1,0:T(8,128)(2,1)S(1)}, u32[]{:S(2)}, u32[]{:S(2)}) %collective-permute-start.19) | collective-permute-done | bytes 98336 | tf_op jit(solution)/shard_map/ppermute | solution.py:192
  47.5 0.7 %shard_map.111 = bf16[32,1024]{1,0:T(8,128)(2,1)} custom-call(bf16[48,1024]{1,0:T(8,128)(2,1)S(1)} %shard_map.108.own_ref, bf16[48,1024]{1,0:T(8,128)(2,1)S(1)} %collective-permute-done.19.far_ref), custom_call_target="tpu_custom_call" | custom-call | bytes 327680 | tf_op jit(solution)/shard_map/pallas_call | solution.py:244
  48.1 0.5 %collective-permute-done.20.swap_ref = bf16[16,1024]{1,0:T(8,128)(2,1)S(1)} collective-permute-done((bf16[16,1024]{1,0:T(8,128)(2,1)S(1)}, bf16[16,1024]{1,0:T(8,128)(2,1)S(1)}, u32[]{:S(2)}, u32[]{:S(2)}) %collective-permute-start.20) | collective-permute-done | bytes 32800 | tf_op jit(solution)/shard_map/ppermute | solution.py:192
  48.7 0.7 %shard_map.110 = (f32[128,128]{1,0:T(8,128)}, f32[128,128]{1,0:T(8,128)}) custom-call(bf16[16,1024]{1,0:T(8,128)(2,1)S(1)} %shard_map.109.own_ref, bf16[16,1024]{1,0:T(8,128)(2,1)S(1)} %collective-permute-done.20.swap_ref), custom_call_target="tpu_custom_call" | custom-call | bytes 196608 | tf_op jit(solution)/shard_map/pallas_call | solution.py:244
  (20 shorter events, 0.1 us)
Async XLA Ops:
  0.6 3.0 %collective-permute-start = (bf16[32,1024]{1,0:T(8,128)(2,1)}, bf16[32,1024]{1,0:T(8,128)(2,1)S(1)}, u32[]{:S(2)}, u32[]{:S(2)}) collective-permute-start(bf16[32,1024]{1,0:T(8,128)(2,1)} %own_ref.1), channel_id=1, source_target_pairs={{0,1},{1,0},{2,3},{3,2},{4,20},{5,21},{6,22},{7,23},{8,9},{9,8},{1... | collective-permute-start | bytes 196616 | tf_op jit(solution)/shard_map/ppermute | solution.py:192
  0.7 2.9 %collective-permute-start.1 = (bf16[32,1024]{1,0:T(8,128)(2,1)}, bf16[32,1024]{1,0:T(8,128)(2,1)S(1)}, u32[]{:S(2)}, u32[]{:S(2)}) collective-permute-start(bf16[32,1024]{1,0:T(8,128)(2,1)} %own_ref.1), channel_id=1, source_target_pairs={{0,2},{1,3},{2,0},{3,1},{4,22},{5,23},{6,20},{7,21},{8,9},{9,8},{1... | collective-permute-start | bytes 196616 | tf_op jit(solution)/shard_map/ppermute | solution.py:192
  1.2 3.0 %collective-permute-start.2 = (bf16[32,1024]{1,0:T(8,128)(2,1)}, bf16[32,1024]{1,0:T(8,128)(2,1)S(1)}, u32[]{:S(2)}, u32[]{:S(2)}) collective-permute-start(bf16[32,1024]{1,0:T(8,128)(2,1)} %own_ref.1), channel_id=1, source_target_pairs={{0,1},{1,0},{2,3},{3,2},{4,5},{5,4},{6,7},{7,6},{8,9},{9,8},{10,11... | collective-permute-start | bytes 196616 | tf_op jit(solution)/shard_map/ppermute | solution.py:192
  1.9 3.4 %copy-start.2 = (bf16[32,1024]{1,0:T(8,128)(2,1)S(1)}, bf16[32,1024]{1,0:T(8,128)(2,1)}, u32[]{:S(2)}) copy-start(bf16[32,1024]{1,0:T(8,128)(2,1)} %own_ref.1) | copy-start | bytes 196612
  1.9 4.5 %copy-start.3 = (bf16[128,256]{1,0:T(8,128)(2,1)S(1)}, bf16[128,256]{1,0:T(8,128)(2,1)}, u32[]{:S(2)}) copy-start(bf16[128,256]{1,0:T(8,128)(2,1)} %cot_ref.1) | copy-start | bytes 196612
  2.0 4.6 %copy-start = (bf16[128,128]{1,0:T(8,128)(2,1)S(1)}, bf16[128,128]{1,0:T(8,128)(2,1)}, u32[]{:S(2)}) copy-start(bf16[128,128]{1,0:T(8,128)(2,1)} %weight_ref.5) | copy-start | bytes 98308
  2.0 4.6 %copy-start.1 = (bf16[128,128]{1,0:T(8,128)(2,1)S(1)}, bf16[128,128]{1,0:T(8,128)(2,1)}, u32[]{:S(2)}) copy-start(bf16[128,128]{1,0:T(8,128)(2,1)} %weight_ref.3) | copy-start | bytes 98308
  3.6 1.4 %collective-permute-start.3 = (bf16[32,1024]{1,0:T(8,128)(2,1)S(1)}, bf16[32,1024]{1,0:T(8,128)(2,1)S(1)}, u32[]{:S(2)}, u32[]{:S(2)}) collective-permute-start(bf16[32,1024]{1,0:T(8,128)(2,1)S(1)} %collective-permute-done.across_ref), channel_id=1, source_target_pairs={{0,1},{1,0},{2,3},{3,2},{4,5},{5,4},{6,7},{7,6},{8,9},{9,8},{10,11... | collective-permute-start | bytes 196616 | tf_op jit(solution)/shard_map/ppermute | solution.py:192
  4.1 1.3 %collective-permute-start.4 = (bf16[32,1024]{1,0:T(8,128)(2,1)S(1)}, bf16[32,1024]{1,0:T(8,128)(2,1)S(1)}, u32[]{:S(2)}, u32[]{:S(2)}) collective-permute-start(bf16[32,1024]{1,0:T(8,128)(2,1)S(1)} %collective-permute-done.1.pair_ref), channel_id=1, source_target_pairs={{0,1},{1,0},{2,3},{3,2},{4,5},{5,4},{6,7},{7,6},{8,9},{9,8},{10,11... | collective-permute-start | bytes 196616 | tf_op jit(solution)/shard_map/ppermute | solution.py:192
  5.9 1.8 %collective-permute-start.5 = (bf16[128,512]{1,0:T(8,128)(2,1)S(1)}, bf16[128,512]{1,0:T(8,128)(2,1)S(1)}, u32[]{:S(2)}, u32[]{:S(2)}) collective-permute-start(bf16[128,512]{1,0:T(8,128)(2,1)S(1)} %shard_map.95.own_ref), channel_id=1, source_target_pairs={{0,20},{1,21},{2,22},{3,23},{4,0},{5,1},{6,2},{7,3},{8,9},{9,8},{1... | collective-permute-start | bytes 393224 | tf_op jit(solution)/shard_map/ppermute | solution.py:192
  6.1 1.6 %collective-permute-start.6 = (bf16[128,512]{1,0:T(8,128)(2,1)S(1)}, bf16[128,512]{1,0:T(8,128)(2,1)S(1)}, u32[]{:S(2)}, u32[]{:S(2)}) collective-permute-start(bf16[128,512]{1,0:T(8,128)(2,1)S(1)} %shard_map.95.own_ref), channel_id=1, source_target_pairs={{0,1},{1,0},{2,3},{3,2},{4,20},{5,21},{6,22},{7,23},{8,9},{9,8},{1... | collective-permute-start | bytes 393224 | tf_op jit(solution)/shard_map/ppermute | solution.py:192
  6.4 1.3 %collective-permute-start.7 = (bf16[128,256]{1,0:T(8,128)(2,1)S(1)}, bf16[128,256]{1,0:T(8,128)(2,1)S(1)}, u32[]{:S(2)}, u32[]{:S(2)}) collective-permute-start(bf16[128,256]{1,0:T(8,128)(2,1)S(1)} %copy-done.3), channel_id=1, source_target_pairs={{0,2},{1,3},{2,0},{3,1},{4,6},{5,7},{6,4},{7,5},{8,9},{9,8},{10,11... | collective-permute-start | bytes 196616 | tf_op jit(solution)/shard_map/ppermute | solution.py:192
  7.9 1.4 %collective-permute-start.8 = (bf16[128,512]{1,0:T(8,128)(2,1)S(1)}, bf16[128,512]{1,0:T(8,128)(2,1)S(1)}, u32[]{:S(2)}, u32[]{:S(2)}) collective-permute-start(bf16[128,512]{1,0:T(8,128)(2,1)S(1)} %get-tuple-element.44.own_ref), channel_id=1, source_target_pairs={{0,1},{1,0},{2,3},{3,2},{4,5},{5,4},{6,7},{7,6},{8,9},{9,8},{10,11... | collective-permute-start | bytes 393224 | tf_op jit(solution)/shard_map/ppermute | solution.py:192
  9.6 1.4 %collective-permute-start.9 = (bf16[128,512]{1,0:T(8,128)(2,1)S(1)}, bf16[128,512]{1,0:T(8,128)(2,1)S(1)}, u32[]{:S(2)}, u32[]{:S(2)}) collective-permute-start(bf16[128,512]{1,0:T(8,128)(2,1)S(1)} %shard_map.99.own_ref), channel_id=1, source_target_pairs={{0,4},{1,5},{2,6},{3,7},{4,0},{5,1},{6,2},{7,3},{8,9},{9,8},{10,11... | collective-permute-start | bytes 393224 | tf_op jit(solution)/shard_map/ppermute | solution.py:192
  9.9 1.8 %collective-permute-start.11 = (bf16[128,512]{1,0:T(8,128)(2,1)S(1)}, bf16[128,512]{1,0:T(8,128)(2,1)S(1)}, u32[]{:S(2)}, u32[]{:S(2)}) collective-permute-start(bf16[128,512]{1,0:T(8,128)(2,1)S(1)} %get-tuple-element.49.mix_ref), channel_id=1, source_target_pairs={{0,1},{1,0},{2,3},{3,2},{4,20},{5,21},{6,22},{7,23},{8,9},{9,8},{1... | collective-permute-start | bytes 393224 | tf_op jit(solution)/shard_map/ppermute | solution.py:192
  11.5 1.4 %collective-permute-start.10 = (bf16[128,512]{1,0:T(8,128)(2,1)S(1)}, bf16[128,512]{1,0:T(8,128)(2,1)S(1)}, u32[]{:S(2)}, u32[]{:S(2)}) collective-permute-start(bf16[128,512]{1,0:T(8,128)(2,1)S(1)} %get-tuple-element.47.own_ref), channel_id=1, source_target_pairs={{0,1},{1,0},{2,3},{3,2},{4,5},{5,4},{6,7},{7,6},{8,9},{9,8},{10,11... | collective-permute-start | bytes 393224 | tf_op jit(solution)/shard_map/ppermute | solution.py:192
  11.9 2.2 %collective-permute-start.15 = (bf16[128,512]{1,0:T(8,128)(2,1)S(1)}, bf16[128,512]{1,0:T(8,128)(2,1)S(1)}, u32[]{:S(2)}, u32[]{:S(2)}) collective-permute-start(bf16[128,512]{1,0:T(8,128)(2,1)S(1)} %get-tuple-element.57.mix_ref), channel_id=1, source_target_pairs={{0,1},{1,0},{2,3},{3,2},{4,5},{5,4},{6,7},{7,6},{8,9},{9,8},{10,11... | collective-permute-start | bytes 393224 | tf_op jit(solution)/shard_map/ppermute | solution.py:192
  13.1 2.1 %collective-permute-start.12 = (bf16[128,512]{1,0:T(8,128)(2,1)S(1)}, bf16[128,512]{1,0:T(8,128)(2,1)S(1)}, u32[]{:S(2)}, u32[]{:S(2)}) collective-permute-start(bf16[128,512]{1,0:T(8,128)(2,1)S(1)} %shard_map.103.own_ref), channel_id=1, source_target_pairs={{0,4},{1,5},{2,6},{3,7},{4,16},{5,17},{6,18},{7,19},{8,9},{9,8},{1... | collective-permute-start | bytes 393224 | tf_op jit(solution)/shard_map/ppermute | solution.py:192
  13.3 1.8 %collective-permute-start.13 = (bf16[128,512]{1,0:T(8,128)(2,1)S(1)}, bf16[128,512]{1,0:T(8,128)(2,1)S(1)}, u32[]{:S(2)}, u32[]{:S(2)}) collective-permute-start(bf16[128,512]{1,0:T(8,128)(2,1)S(1)} %shard_map.103.own_ref), channel_id=1, source_target_pairs={{0,1},{1,0},{2,3},{3,2},{4,20},{5,21},{6,22},{7,23},{8,9},{9,8},{1... | collective-permute-start | bytes 393224 | tf_op jit(solution)/shard_map/ppermute | solution.py:192
  13.8 1.3 %collective-permute-start.14 = (f32[128,128]{1,0:T(8,128)S(1)}, f32[128,128]{1,0:T(8,128)S(1)}, u32[]{:S(2)}, u32[]{:S(2)}) collective-permute-start(f32[128,128]{1,0:T(8,128)S(1)} %shard_map.104.two_ref), channel_id=1, source_target_pairs={{0,1},{1,0},{2,3},{3,2},{4,5},{5,4},{6,7},{7,6},{8,9},{9,8},{10,11... | collective-permute-start | bytes 196616 | tf_op jit(solution)/shard_map/ppermute | solution.py:192
  15.2 1.4 %collective-permute-start.16 = (bf16[128,512]{1,0:T(8,128)(2,1)S(1)}, bf16[128,512]{1,0:T(8,128)(2,1)S(1)}, u32[]{:S(2)}, u32[]{:S(2)}) collective-permute-start(bf16[128,512]{1,0:T(8,128)(2,1)S(1)} %shard_map.105.dz_ref), channel_id=1, source_target_pairs={{0,1},{1,0},{2,3},{3,2},{4,5},{5,4},{6,7},{7,6},{8,9},{9,8},{10,11... | collective-permute-start | bytes 393224 | tf_op jit(solution)/shard_map/ppermute | solution.py:192
  17.1 1.3 %collective-permute-start.17 = (bf16[48,1024]{1,0:T(8,128)(2,1)S(1)}, bf16[48,1024]{1,0:T(8,128)(2,1)S(1)}, u32[]{:S(2)}, u32[]{:S(2)}) collective-permute-start(bf16[48,1024]{1,0:T(8,128)(2,1)S(1)} %shard_map.107.own_ref), channel_id=1, source_target_pairs={{0,4},{1,5},{2,6},{3,7},{4,16},{5,17},{6,18},{7,19},{8,9},{9,8},{1... | collective-permute-start | bytes 294920 | tf_op jit(solution)/shard_map/ppermute | solution.py:192
  17.3 1.3 %collective-permute-start.18 = (bf16[48,1024]{1,0:T(8,128)(2,1)S(1)}, bf16[48,1024]{1,0:T(8,128)(2,1)S(1)}, u32[]{:S(2)}, u32[]{:S(2)}) collective-permute-start(bf16[48,1024]{1,0:T(8,128)(2,1)S(1)} %shard_map.107.own_ref), channel_id=1, source_target_pairs={{0,1},{1,0},{2,3},{3,2},{4,20},{5,21},{6,22},{7,23},{8,9},{9,8},{1... | collective-permute-start | bytes 294920 | tf_op jit(solution)/shard_map/ppermute | solution.py:192
  18.7 28.8 %collective-permute-start.19 = (bf16[48,1024]{1,0:T(8,128)(2,1)S(1)}, bf16[48,1024]{1,0:T(8,128)(2,1)S(1)}, u32[]{:S(2)}, u32[]{:S(2)}) collective-permute-start(bf16[48,1024]{1,0:T(8,128)(2,1)S(1)} %shard_map.108.own_ref), channel_id=1, source_target_pairs={{0,8},{1,9},{2,10},{3,11},{4,12},{5,13},{6,14},{7,15},{16,24},{17,... | collective-permute-start | bytes 294920 | tf_op jit(solution)/shard_map/ppermute | solution.py:192
  47.5 1.2 %collective-permute-start.20 = (bf16[16,1024]{1,0:T(8,128)(2,1)S(1)}, bf16[16,1024]{1,0:T(8,128)(2,1)S(1)}, u32[]{:S(2)}, u32[]{:S(2)}) collective-permute-start(bf16[16,1024]{1,0:T(8,128)(2,1)S(1)} %shard_map.109.own_ref), channel_id=1, source_target_pairs={{0,1},{1,0},{2,3},{3,2},{4,5},{5,4},{6,7},{7,6},{8,9},{9,8},{10,11... | collective-permute-start | bytes 98312 | tf_op jit(solution)/shard_map/ppermute | solution.py:192

commit v7 on v6

--- a/solution.py
+++ b/solution.py
@@ -275,6 +275,7 @@
     coords_ref,
     tiles_ref,
     block_ref,
+    turned_ref,
     starts,
     coords,
     held,
@@ -293,6 +294,8 @@
         )
         copies[-1].start()
     block_ref[...] = jnp.zeros_like(block_ref)
+    turned_ref[...] = jnp.zeros_like(turned_ref)
+    half = turned_ref.shape[1]
     quarter = panels // 4
     core = lax.axis_index("feat") % 2
     lists.wait()
@@ -308,9 +311,14 @@
         return pl.multiple_of(starts[panel], side)
 
     def place(slot, carry):
-        rows = pl.ds(start_of(coords[0, 0, 0, slot]), side)
+        row = start_of(coords[0, 0, 0, slot])
         columns = pl.ds(start_of(coords[0, 0, 1, slot]), side)
-        block_ref[rows, columns] = held[slot]
+        block_ref[pl.ds(row, side), columns] = held[slot]
+
+        @pl.when(row < half)
+        def _():
+            turned_ref[columns, pl.ds(row, side)] = held[slot].T
+
         return carry
 
     group = 8
@@ -365,17 +373,17 @@
     keep(jnp.where(odd, across_swap_ref[...], own_swap_ref[...]), jnp.bitwise_xor(feat, 1))
     keep(pair_ref[...], jnp.bitwise_xor(feat, 2))
     keep(pair_swap_ref[...], jnp.bitwise_xor(feat, 3))
-    out_ref[...] = dot_nt(full[...], block_ref[:half, :]).astype(out_ref.dtype)
+    out_ref[...] = dot_nn(full[...], block_ref[...]).astype(out_ref.dtype)
 
 
 def forward_own_kernel(own_ref, block_ref, total_ref):
     half = own_ref.shape[1]
-    total_ref[...] = dot_nt(own_ref[...], block_ref[:half, :half])
+    total_ref[...] = dot_nn(own_ref[...], block_ref[:half, :])
 
 
 def forward_other_kernel(total_ref, other_ref, block_ref, out_ref):
     half = other_ref.shape[1]
-    total = total_ref[...] + dot_nt(other_ref[...], block_ref[:half, half:])
+    total = total_ref[...] + dot_nn(other_ref[...], block_ref[half:, :])
     out_ref[...] = total.astype(out_ref.dtype)
 
 
@@ -543,9 +551,9 @@
     across = routed(features, to_odd_across)
     pair = routed(features, to_feature_pair)
     own_swap = routed(features, to_other_core)
-    (block,) = local_call(
+    block, turned = local_call(
         functools.partial(place_kernel, panels, side),
-        [bf16_array(nodes, nodes)],
+        [bf16_array(nodes, nodes), bf16_array(nodes, half)],
         [section_counts[0, 0]]
         + [
             pltpu.with_memory_space_constraint(value, pltpu.HBM)
@@ -566,7 +574,7 @@
         [bf16_array(hidden, hidden)] * 2,
         [weight_one, lax.optimization_barrier((weight_two, block))[0]],
     )
-    across, pair, block = lax.optimization_barrier((across, pair, block))
+    across, pair, block, turned = lax.optimization_barrier((across, pair, block, turned))
     (part_one,) = local_call(
         first_kernel,
         [bf16_array(hidden, half)],
@@ -577,7 +585,7 @@
             own_swap,
             routed(across, to_other_core),
             routed(pair, to_other_core),
-            block,
+            turned,
         ],
         None,
         [pltpu.VMEM((hidden, nodes), jnp.bfloat16)],
@@ -598,12 +606,12 @@
     )
     h_swap = routed(h_one, to_other_core)
     (total_two,) = local_call(
-        forward_own_kernel, [f32_array(hidden, half)], [h_one, block], flops=product_flops // 2
+        forward_own_kernel, [f32_array(hidden, half)], [h_one, turned], flops=product_flops // 2
     )
     (part_two,) = local_call(
         forward_other_kernel,
         [bf16_array(hidden, half)],
-        [total_two, h_swap, block],
+        [total_two, h_swap, turned],
         flops=product_flops // 2,
     )
     near_two = routed(part_two, to_other_rep)

time: 49.8 us -> 49.8 us (level)
  no operation moved by 1% of the time
where the time goes in v7:
time: 49.8 us; the launch traced here: 49.3 us
  waiting for transfers between devices  35.2 us (71%)
  starting transfers between devices  6.36 us (13%)
  Pallas kernels  6.22 us (12%)
  between operations  1.48 us (3%)
    ppermute x21, waiting for transfers between devices, routed(): return lax.ppermute(value, mesh_axes, pairs)  35.2 us
    ppermute x21, starting transfers between devices, routed(): return lax.ppermute(value, mesh_axes, pairs)  6.36 us
    pallas_call x18, Pallas kernels, local_call(): pl.pallas_call(kernel, out_shape=list(outs), in_specs=[pl.BlockSpec(memor...  6.22 us
  transfers between devices with their start and end apart: 21, of which 12 were waited for; matrix products, arithmetic and copies ran while one was open for 0% of the time, Pallas kernels for 9%

profile of v7, /device:TPU:24, one launch (start us, length us, event | category | flops | bytes accessed | tf_op | source)
XLA Modules:
  0.0 49.3 jit_solution(15954809451327600108)
XLA Ops:
  0.6 0.1 collective-permute-start.1
  0.7 0.5 %collective-permute-start = (bf16[32,1024]{1,0:T(8,128)(2,1)}, bf16[32,1024]{1,0:T(8,128)(2,1)S(1)}, u32[]{:S(2)}, u32[]{:S(2)}) collective-permute-start(bf16[32,1024]{1,0:T(8,128)(2,1)} %own_ref.1), channel_id=1, source_target_pairs={{0,1},{1,0},{2,3},{3,2},{4,20},{5,21},{6,22},{7,23},{8,9},{9,8},{1... | collective-permute-start | bytes 196616 | tf_op jit(solution)/shard_map/ppermute | solution.py:192
  1.2 0.1 collective-permute-start.2
  2.0 1.6 %shard_map.94 = (bf16[1024,1024]{1,0:T(8,128)(2,1)S(1)}, bf16[1024,512]{1,0:T(8,128)(2,1)S(1)}) custom-call(s32[1]{0:T(128)} %bitcast.1.count_ref, s32[1,1,2,112]{3,2,1,0:T(2,128)} %coords_ref.1, bf16[1,1,112,128,128]{4,3,2,1,0:T(8,128)(2,1)} %tiles_ref.1), custom_call_target="tpu_custom_call" | custom-call | flops 4000000000 | bytes 9962372 | tf_op jit(solution)/shard_map/pallas_call | solution.py:244
  3.6 0.5 %collective-permute-start.3 = (bf16[32,1024]{1,0:T(8,128)(2,1)S(1)}, bf16[32,1024]{1,0:T(8,128)(2,1)S(1)}, u32[]{:S(2)}, u32[]{:S(2)}) collective-permute-start(bf16[32,1024]{1,0:T(8,128)(2,1)S(1)} %collective-permute-done.across_ref), channel_id=1, source_target_pairs={{0,1},{1,0},{2,3},{3,2},{4,5},{5,4},{6,7},{7,6},{8,9},{9,8},{10,11... | collective-permute-start | bytes 196616 | tf_op jit(solution)/shard_map/ppermute | solution.py:192
  4.1 0.1 collective-permute-start.4
  4.2 0.8 %collective-permute-done.3.across_swap_ref = bf16[32,1024]{1,0:T(8,128)(2,1)S(1)} collective-permute-done((bf16[32,1024]{1,0:T(8,128)(2,1)S(1)}, bf16[32,1024]{1,0:T(8,128)(2,1)S(1)}, u32[]{:S(2)}, u32[]{:S(2)}) %collective-permute-start.3) | collective-permute-done | bytes 65568 | tf_op jit(solution)/shard_map/ppermute | solution.py:192
  5.0 0.4 collective-permute-done.4.pair_swap_ref
  5.4 0.3 shard_map.95.own_ref
  5.7 0.2 collective-permute-start.6
  5.9 0.4 collective-permute-start.5
  6.3 0.2 collective-permute-start.7
  6.4 0.1 shard_map.96
  6.5 1.0 %collective-permute-done.7.cot_pair_ref = bf16[128,256]{1,0:T(8,128)(2,1)S(1)} collective-permute-done((bf16[128,256]{1,0:T(8,128)(2,1)S(1)}, bf16[128,256]{1,0:T(8,128)(2,1)S(1)}, u32[]{:S(2)}, u32[]{:S(2)}) %collective-permute-start.7) | collective-permute-done | bytes 65568 | tf_op jit(solution)/shard_map/ppermute | solution.py:192
  7.5 0.2 shard_map.97
  7.8 0.3 collective-permute-start.8
  8.0 0.2 shard_map.98.total_ref
  8.2 0.9 %collective-permute-done.8.other_ref = bf16[128,512]{1,0:T(8,128)(2,1)S(1)} collective-permute-done((bf16[128,512]{1,0:T(8,128)(2,1)S(1)}, bf16[128,512]{1,0:T(8,128)(2,1)S(1)}, u32[]{:S(2)}, u32[]{:S(2)}) %collective-permute-start.8) | collective-permute-done | bytes 131104 | tf_op jit(solution)/shard_map/ppermute | solution.py:192
  9.2 0.2 shard_map.99.own_ref
  9.4 0.3 collective-permute-start.9
  9.7 0.3 collective-permute-start.11
  10.0 0.8 %collective-permute-done.9.near_ref = bf16[128,512]{1,0:T(8,128)(2,1)S(1)} collective-permute-done((bf16[128,512]{1,0:T(8,128)(2,1)S(1)}, bf16[128,512]{1,0:T(8,128)(2,1)S(1)}, u32[]{:S(2)}, u32[]{:S(2)}) %collective-permute-start.9) | collective-permute-done | bytes 131104 | tf_op jit(solution)/shard_map/ppermute | solution.py:192
  10.8 0.4 shard_map.100
  11.2 0.2 collective-permute-start.10
  11.5 0.2 shard_map.101
  11.7 0.4 collective-permute-start.15
  12.1 0.2 shard_map.102.total_ref
  12.3 0.3 collective-permute-done.10.other_ref
  12.7 0.2 shard_map.103.own_ref
  12.9 0.2 collective-permute-start.13
  13.1 0.3 collective-permute-start.12
  13.5 0.2 shard_map.104.two_ref
  13.7 0.2 collective-permute-start.14
  13.9 1.1 %collective-permute-done.14.two_swap_ref = f32[128,128]{1,0:T(8,128)S(1)} collective-permute-done((f32[128,128]{1,0:T(8,128)S(1)}, f32[128,128]{1,0:T(8,128)S(1)}, u32[]{:S(2)}, u32[]{:S(2)}) %collective-permute-start.14) | collective-permute-done | bytes 65568 | tf_op jit(solution)/shard_map/ppermute | solution.py:192
  15.0 0.1 shard_map.105.dz_ref
  15.1 0.2 collective-permute-start.16
  15.3 0.4 shard_map.106
  15.7 0.7 %collective-permute-done.16.dz_swap_ref = bf16[128,512]{1,0:T(8,128)(2,1)S(1)} collective-permute-done((bf16[128,512]{1,0:T(8,128)(2,1)S(1)}, bf16[128,512]{1,0:T(8,128)(2,1)S(1)}, u32[]{:S(2)}, u32[]{:S(2)}) %collective-permute-start.16) | collective-permute-done | bytes 131104 | tf_op jit(solution)/shard_map/ppermute | solution.py:192
  16.5 0.4 shard_map.107.own_ref
  16.9 0.2 collective-permute-start.18
  17.2 0.3 collective-permute-start.17
  17.5 0.8 %collective-permute-done.18.across_ref = bf16[48,1024]{1,0:T(8,128)(2,1)S(1)} collective-permute-done((bf16[48,1024]{1,0:T(8,128)(2,1)S(1)}, bf16[48,1024]{1,0:T(8,128)(2,1)S(1)}, u32[]{:S(2)}, u32[]{:S(2)}) %collective-permute-start.18) | collective-permute-done | bytes 98336 | tf_op jit(solution)/shard_map/ppermute | solution.py:192
  18.3 0.2 collective-permute-done.17.near_ref
  18.5 1.3 %collective-permute-start.19 = (bf16[48,1024]{1,0:T(8,128)(2,1)S(1)}, bf16[48,1024]{1,0:T(8,128)(2,1)S(1)}, u32[]{:S(2)}, u32[]{:S(2)}) collective-permute-start(bf16[48,1024]{1,0:T(8,128)(2,1)S(1)} %shard_map.108.own_ref), channel_id=1, source_target_pairs={{0,8},{1,9},{2,10},{3,11},{4,12},{5,13},{6,14},{7,15},{16,24},{17,... | collective-permute-start | bytes 294920 | tf_op jit(solution)/shard_map/ppermute | solution.py:192
  19.8 27.6 %collective-permute-done.19.far_ref = bf16[48,1024]{1,0:T(8,128)(2,1)S(1)} collective-permute-done((bf16[48,1024]{1,0:T(8,128)(2,1)S(1)}, bf16[48,1024]{1,0:T(8,128)(2,1)S(1)}, u32[]{:S(2)}, u32[]{:S(2)}) %collective-permute-start.19) | collective-permute-done | bytes 98336 | tf_op jit(solution)/shard_map/ppermute | solution.py:192
  47.5 0.7 %shard_map.111 = bf16[32,1024]{1,0:T(8,128)(2,1)} custom-call(bf16[48,1024]{1,0:T(8,128)(2,1)S(1)} %shard_map.108.own_ref, bf16[48,1024]{1,0:T(8,128)(2,1)S(1)} %collective-permute-done.19.far_ref), custom_call_target="tpu_custom_call" | custom-call | bytes 327680 | tf_op jit(solution)/shard_map/pallas_call | solution.py:244
  48.1 0.5 %collective-permute-done.20.swap_ref = bf16[16,1024]{1,0:T(8,128)(2,1)S(1)} collective-permute-done((bf16[16,1024]{1,0:T(8,128)(2,1)S(1)}, bf16[16,1024]{1,0:T(8,128)(2,1)S(1)}, u32[]{:S(2)}, u32[]{:S(2)}) %collective-permute-start.20) | collective-permute-done | bytes 32800 | tf_op jit(solution)/shard_map/ppermute | solution.py:192
  48.7 0.7 %shard_map.110 = (f32[128,128]{1,0:T(8,128)}, f32[128,128]{1,0:T(8,128)}) custom-call(bf16[16,1024]{1,0:T(8,128)(2,1)S(1)} %shard_map.109.own_ref, bf16[16,1024]{1,0:T(8,128)(2,1)S(1)} %collective-permute-done.20.swap_ref), custom_call_target="tpu_custom_call" | custom-call | bytes 196608 | tf_op jit(solution)/shard_map/pallas_call | solution.py:244
  (20 shorter events, 0.1 us)
Async XLA Ops:
  0.6 3.0 %collective-permute-start.1 = (bf16[32,1024]{1,0:T(8,128)(2,1)}, bf16[32,1024]{1,0:T(8,128)(2,1)S(1)}, u32[]{:S(2)}, u32[]{:S(2)}) collective-permute-start(bf16[32,1024]{1,0:T(8,128)(2,1)} %own_ref.1), channel_id=1, source_target_pairs={{0,2},{1,3},{2,0},{3,1},{4,22},{5,23},{6,20},{7,21},{8,9},{9,8},{1... | collective-permute-start | bytes 196616 | tf_op jit(solution)/shard_map/ppermute | solution.py:192
  0.7 2.9 %collective-permute-start = (bf16[32,1024]{1,0:T(8,128)(2,1)}, bf16[32,1024]{1,0:T(8,128)(2,1)S(1)}, u32[]{:S(2)}, u32[]{:S(2)}) collective-permute-start(bf16[32,1024]{1,0:T(8,128)(2,1)} %own_ref.1), channel_id=1, source_target_pairs={{0,1},{1,0},{2,3},{3,2},{4,20},{5,21},{6,22},{7,23},{8,9},{9,8},{1... | collective-permute-start | bytes 196616 | tf_op jit(solution)/shard_map/ppermute | solution.py:192
  1.2 3.0 %collective-permute-start.2 = (bf16[32,1024]{1,0:T(8,128)(2,1)}, bf16[32,1024]{1,0:T(8,128)(2,1)S(1)}, u32[]{:S(2)}, u32[]{:S(2)}) collective-permute-start(bf16[32,1024]{1,0:T(8,128)(2,1)} %own_ref.1), channel_id=1, source_target_pairs={{0,1},{1,0},{2,3},{3,2},{4,5},{5,4},{6,7},{7,6},{8,9},{9,8},{10,11... | collective-permute-start | bytes 196616 | tf_op jit(solution)/shard_map/ppermute | solution.py:192
  1.9 3.4 %copy-start.2 = (bf16[32,1024]{1,0:T(8,128)(2,1)S(1)}, bf16[32,1024]{1,0:T(8,128)(2,1)}, u32[]{:S(2)}) copy-start(bf16[32,1024]{1,0:T(8,128)(2,1)} %own_ref.1) | copy-start | bytes 196612
  1.9 4.3 %copy-start.3 = (bf16[128,256]{1,0:T(8,128)(2,1)S(1)}, bf16[128,256]{1,0:T(8,128)(2,1)}, u32[]{:S(2)}) copy-start(bf16[128,256]{1,0:T(8,128)(2,1)} %cot_ref.1) | copy-start | bytes 196612
  2.0 4.5 %copy-start = (bf16[128,128]{1,0:T(8,128)(2,1)S(1)}, bf16[128,128]{1,0:T(8,128)(2,1)}, u32[]{:S(2)}) copy-start(bf16[128,128]{1,0:T(8,128)(2,1)} %weight_ref.5) | copy-start | bytes 98308
  2.0 4.5 %copy-start.1 = (bf16[128,128]{1,0:T(8,128)(2,1)S(1)}, bf16[128,128]{1,0:T(8,128)(2,1)}, u32[]{:S(2)}) copy-start(bf16[128,128]{1,0:T(8,128)(2,1)} %weight_ref.3) | copy-start | bytes 98308
  3.6 1.4 %collective-permute-start.3 = (bf16[32,1024]{1,0:T(8,128)(2,1)S(1)}, bf16[32,1024]{1,0:T(8,128)(2,1)S(1)}, u32[]{:S(2)}, u32[]{:S(2)}) collective-permute-start(bf16[32,1024]{1,0:T(8,128)(2,1)S(1)} %collective-permute-done.across_ref), channel_id=1, source_target_pairs={{0,1},{1,0},{2,3},{3,2},{4,5},{5,4},{6,7},{7,6},{8,9},{9,8},{10,11... | collective-permute-start | bytes 196616 | tf_op jit(solution)/shard_map/ppermute | solution.py:192
  4.1 1.3 %collective-permute-start.4 = (bf16[32,1024]{1,0:T(8,128)(2,1)S(1)}, bf16[32,1024]{1,0:T(8,128)(2,1)S(1)}, u32[]{:S(2)}, u32[]{:S(2)}) collective-permute-start(bf16[32,1024]{1,0:T(8,128)(2,1)S(1)} %collective-permute-done.1.pair_ref), channel_id=1, source_target_pairs={{0,1},{1,0},{2,3},{3,2},{4,5},{5,4},{6,7},{7,6},{8,9},{9,8},{10,11... | collective-permute-start | bytes 196616 | tf_op jit(solution)/shard_map/ppermute | solution.py:192
  5.7 1.8 %collective-permute-start.6 = (bf16[128,512]{1,0:T(8,128)(2,1)S(1)}, bf16[128,512]{1,0:T(8,128)(2,1)S(1)}, u32[]{:S(2)}, u32[]{:S(2)}) collective-permute-start(bf16[128,512]{1,0:T(8,128)(2,1)S(1)} %shard_map.95.own_ref), channel_id=1, source_target_pairs={{0,1},{1,0},{2,3},{3,2},{4,20},{5,21},{6,22},{7,23},{8,9},{9,8},{1... | collective-permute-start | bytes 393224 | tf_op jit(solution)/shard_map/ppermute | solution.py:192
  5.9 1.6 %collective-permute-start.5 = (bf16[128,512]{1,0:T(8,128)(2,1)S(1)}, bf16[128,512]{1,0:T(8,128)(2,1)S(1)}, u32[]{:S(2)}, u32[]{:S(2)}) collective-permute-start(bf16[128,512]{1,0:T(8,128)(2,1)S(1)} %shard_map.95.own_ref), channel_id=1, source_target_pairs={{0,20},{1,21},{2,22},{3,23},{4,0},{5,1},{6,2},{7,3},{8,9},{9,8},{1... | collective-permute-start | bytes 393224 | tf_op jit(solution)/shard_map/ppermute | solution.py:192
  6.3 1.3 %collective-permute-start.7 = (bf16[128,256]{1,0:T(8,128)(2,1)S(1)}, bf16[128,256]{1,0:T(8,128)(2,1)S(1)}, u32[]{:S(2)}, u32[]{:S(2)}) collective-permute-start(bf16[128,256]{1,0:T(8,128)(2,1)S(1)} %copy-done.3), channel_id=1, source_target_pairs={{0,2},{1,3},{2,0},{3,1},{4,6},{5,7},{6,4},{7,5},{8,9},{9,8},{10,11... | collective-permute-start | bytes 196616 | tf_op jit(solution)/shard_map/ppermute | solution.py:192
  7.8 1.4 %collective-permute-start.8 = (bf16[128,512]{1,0:T(8,128)(2,1)S(1)}, bf16[128,512]{1,0:T(8,128)(2,1)S(1)}, u32[]{:S(2)}, u32[]{:S(2)}) collective-permute-start(bf16[128,512]{1,0:T(8,128)(2,1)S(1)} %get-tuple-element.49.own_ref), channel_id=1, source_target_pairs={{0,1},{1,0},{2,3},{3,2},{4,5},{5,4},{6,7},{7,6},{8,9},{9,8},{10,11... | collective-permute-start | bytes 393224 | tf_op jit(solution)/shard_map/ppermute | solution.py:192
  9.4 1.4 %collective-permute-start.9 = (bf16[128,512]{1,0:T(8,128)(2,1)S(1)}, bf16[128,512]{1,0:T(8,128)(2,1)S(1)}, u32[]{:S(2)}, u32[]{:S(2)}) collective-permute-start(bf16[128,512]{1,0:T(8,128)(2,1)S(1)} %shard_map.99.own_ref), channel_id=1, source_target_pairs={{0,4},{1,5},{2,6},{3,7},{4,0},{5,1},{6,2},{7,3},{8,9},{9,8},{10,11... | collective-permute-start | bytes 393224 | tf_op jit(solution)/shard_map/ppermute | solution.py:192
  9.7 1.8 %collective-permute-start.11 = (bf16[128,512]{1,0:T(8,128)(2,1)S(1)}, bf16[128,512]{1,0:T(8,128)(2,1)S(1)}, u32[]{:S(2)}, u32[]{:S(2)}) collective-permute-start(bf16[128,512]{1,0:T(8,128)(2,1)S(1)} %get-tuple-element.54.mix_ref), channel_id=1, source_target_pairs={{0,1},{1,0},{2,3},{3,2},{4,20},{5,21},{6,22},{7,23},{8,9},{9,8},{1... | collective-permute-start | bytes 393224 | tf_op jit(solution)/shard_map/ppermute | solution.py:192
  11.2 1.4 %collective-permute-start.10 = (bf16[128,512]{1,0:T(8,128)(2,1)S(1)}, bf16[128,512]{1,0:T(8,128)(2,1)S(1)}, u32[]{:S(2)}, u32[]{:S(2)}) collective-permute-start(bf16[128,512]{1,0:T(8,128)(2,1)S(1)} %get-tuple-element.52.own_ref), channel_id=1, source_target_pairs={{0,1},{1,0},{2,3},{3,2},{4,5},{5,4},{6,7},{7,6},{8,9},{9,8},{10,11... | collective-permute-start | bytes 393224 | tf_op jit(solution)/shard_map/ppermute | solution.py:192
  11.7 2.2 %collective-permute-start.15 = (bf16[128,512]{1,0:T(8,128)(2,1)S(1)}, bf16[128,512]{1,0:T(8,128)(2,1)S(1)}, u32[]{:S(2)}, u32[]{:S(2)}) collective-permute-start(bf16[128,512]{1,0:T(8,128)(2,1)S(1)} %get-tuple-element.63.mix_ref), channel_id=1, source_target_pairs={{0,1},{1,0},{2,3},{3,2},{4,5},{5,4},{6,7},{7,6},{8,9},{9,8},{10,11... | collective-permute-start | bytes 393224 | tf_op jit(solution)/shard_map/ppermute | solution.py:192
  12.9 2.1 %collective-permute-start.13 = (bf16[128,512]{1,0:T(8,128)(2,1)S(1)}, bf16[128,512]{1,0:T(8,128)(2,1)S(1)}, u32[]{:S(2)}, u32[]{:S(2)}) collective-permute-start(bf16[128,512]{1,0:T(8,128)(2,1)S(1)} %shard_map.103.own_ref), channel_id=1, source_target_pairs={{0,1},{1,0},{2,3},{3,2},{4,20},{5,21},{6,22},{7,23},{8,9},{9,8},{1... | collective-permute-start | bytes 393224 | tf_op jit(solution)/shard_map/ppermute | solution.py:192
  13.1 1.8 %collective-permute-start.12 = (bf16[128,512]{1,0:T(8,128)(2,1)S(1)}, bf16[128,512]{1,0:T(8,128)(2,1)S(1)}, u32[]{:S(2)}, u32[]{:S(2)}) collective-permute-start(bf16[128,512]{1,0:T(8,128)(2,1)S(1)} %shard_map.103.own_ref), channel_id=1, source_target_pairs={{0,4},{1,5},{2,6},{3,7},{4,16},{5,17},{6,18},{7,19},{8,9},{9,8},{1... | collective-permute-start | bytes 393224 | tf_op jit(solution)/shard_map/ppermute | solution.py:192
  13.7 1.3 %collective-permute-start.14 = (f32[128,128]{1,0:T(8,128)S(1)}, f32[128,128]{1,0:T(8,128)S(1)}, u32[]{:S(2)}, u32[]{:S(2)}) collective-permute-start(f32[128,128]{1,0:T(8,128)S(1)} %shard_map.104.two_ref), channel_id=1, source_target_pairs={{0,1},{1,0},{2,3},{3,2},{4,5},{5,4},{6,7},{7,6},{8,9},{9,8},{10,11... | collective-permute-start | bytes 196616 | tf_op jit(solution)/shard_map/ppermute | solution.py:192
  15.1 1.4 %collective-permute-start.16 = (bf16[128,512]{1,0:T(8,128)(2,1)S(1)}, bf16[128,512]{1,0:T(8,128)(2,1)S(1)}, u32[]{:S(2)}, u32[]{:S(2)}) collective-permute-start(bf16[128,512]{1,0:T(8,128)(2,1)S(1)} %shard_map.105.dz_ref), channel_id=1, source_target_pairs={{0,1},{1,0},{2,3},{3,2},{4,5},{5,4},{6,7},{7,6},{8,9},{9,8},{10,11... | collective-permute-start | bytes 393224 | tf_op jit(solution)/shard_map/ppermute | solution.py:192
  16.9 1.4 %collective-permute-start.18 = (bf16[48,1024]{1,0:T(8,128)(2,1)S(1)}, bf16[48,1024]{1,0:T(8,128)(2,1)S(1)}, u32[]{:S(2)}, u32[]{:S(2)}) collective-permute-start(bf16[48,1024]{1,0:T(8,128)(2,1)S(1)} %shard_map.107.own_ref), channel_id=1, source_target_pairs={{0,1},{1,0},{2,3},{3,2},{4,20},{5,21},{6,22},{7,23},{8,9},{9,8},{1... | collective-permute-start | bytes 294920 | tf_op jit(solution)/shard_map/ppermute | solution.py:192
  17.2 1.3 %collective-permute-start.17 = (bf16[48,1024]{1,0:T(8,128)(2,1)S(1)}, bf16[48,1024]{1,0:T(8,128)(2,1)S(1)}, u32[]{:S(2)}, u32[]{:S(2)}) collective-permute-start(bf16[48,1024]{1,0:T(8,128)(2,1)S(1)} %shard_map.107.own_ref), channel_id=1, source_target_pairs={{0,4},{1,5},{2,6},{3,7},{4,16},{5,17},{6,18},{7,19},{8,9},{9,8},{1... | collective-permute-start | bytes 294920 | tf_op jit(solution)/shard_map/ppermute | solution.py:192
  18.5 28.9 %collective-permute-start.19 = (bf16[48,1024]{1,0:T(8,128)(2,1)S(1)}, bf16[48,1024]{1,0:T(8,128)(2,1)S(1)}, u32[]{:S(2)}, u32[]{:S(2)}) collective-permute-start(bf16[48,1024]{1,0:T(8,128)(2,1)S(1)} %shard_map.108.own_ref), channel_id=1, source_target_pairs={{0,8},{1,9},{2,10},{3,11},{4,12},{5,13},{6,14},{7,15},{16,24},{17,... | collective-permute-start | bytes 294920 | tf_op jit(solution)/shard_map/ppermute | solution.py:192
  47.5 1.2 %collective-permute-start.20 = (bf16[16,1024]{1,0:T(8,128)(2,1)S(1)}, bf16[16,1024]{1,0:T(8,128)(2,1)S(1)}, u32[]{:S(2)}, u32[]{:S(2)}) collective-permute-start(bf16[16,1024]{1,0:T(8,128)(2,1)S(1)} %shard_map.109.own_ref), channel_id=1, source_target_pairs={{0,1},{1,0},{2,3},{3,2},{4,5},{5,4},{6,7},{7,6},{8,9},{9,8},{10,11... | collective-permute-start | bytes 98312 | tf_op jit(solution)/shard_map/ppermute | solution.py:192
